TPU v7x, 32 devices: a whole 2x2x4 slice. The times are simulated.
32 devices in a mesh: wide: 16 (over z, y, x), narrow: 2 (over core).
Axes of the slice: x: 2, y: 2, z: 4, core: 2. Of those that a mesh axis runs over, the one named last changes fastest.
Arguments:
- tokens: bfloat16 [32768, 1024], P(('wide', 'narrow')), may hold values from -6 to 6
- class_table: bfloat16 [1024, 1024], P(('wide', 'narrow')), may hold values from -6 to 6
- ada_weight: bfloat16 [1024, 6144], P(('wide', 'narrow')), may hold values from -0.1875 to 0.1875
- qkv_weight: bfloat16 [1024, 3072], P(('wide', 'narrow')), may hold values from -0.1875 to 0.1875
- proj_weight: bfloat16 [1024, 1024], P(('wide', 'narrow')), may hold values from -1 to 1
- head_scale: float32 [16], replicated, may hold values from 8 to 24
- fc1_weight: bfloat16 [1024, 4096], P(('wide', 'narrow')), may hold values from -0.1875 to 0.1875
- fc2_weight: bfloat16 [4096, 1024], P(('wide', 'narrow')), may hold values from -0.125 to 0.125
- levels: int32 [32, 6], P(('wide', 'narrow')), may hold values from 0 to 10, as said below
- labels: int32 [32, 6], P(('wide', 'narrow')), may hold values from 0 to 1023, as said below
- cotangent: bfloat16 [32768, 1024], P(('wide', 'narrow')), may hold values from -6 to 6
Outputs:
- output: bfloat16 [32768, 1024], P(('wide', 'narrow'))
- tokens_grad: bfloat16 [32768, 1024], P(('wide', 'narrow'))
- table_grad: float32 [1024, 1024], P(('wide', 'narrow'))
- ada_grad: float32 [1024, 6144], P(('wide', 'narrow'))
- qkv_grad: float32 [1024, 3072], P(('wide', 'narrow'))
- proj_grad: float32 [1024, 1024], P(('wide', 'narrow'))
- scale_grad: float32 [16], replicated
- fc1_grad: float32 [1024, 4096], P(('wide', 'narrow'))
- fc2_grad: float32 [4096, 1024], P(('wide', 'narrow'))
Inputs may be any that keep to these rules, and one draw needn't show every extreme that they name: In each row the nonzero levels come first and lie in 7 to 10; their items' tokens fit in 1024; a 0 marks an empty slot. Slot 0 of the 32 rows names a class of every aligned block of 32 classes exactly once; labels of empty slots are unused.
All inputs are finite; a program needn't handle non-finite values.
Results may differ from a plain program's by a relative error of at most 0.018.
Values may be sent and summed in bfloat16 or wider, within the bound.
No kernel may reach another device: no remote copies, remote signals or barrier semaphores. Data moves between devices by JAX's collectives and lax.ppermute only.
A program may use at most 448 MiB of HBM per device.

v0:
```python
import jax
import jax.numpy as jnp
import numpy as np
from jax import lax
from jax.sharding import PartitionSpec as P

FULL_PRECISION = lax.Precision.HIGHEST
NORM_EPS = 1e-06
NEG_LARGE = -1e30
LENGTH_TABLE = np.array([0, 1, 5, 14, 30, 55, 91, 155, 255, 424, 680], np.int32)
SCALE_BOUNDS = np.array([1, 5, 14, 30, 55, 91, 155, 255, 424], np.int32)


def layout(level_row, row_count):
    level_hits = level_row[:, None] == jnp.arange(11, dtype=jnp.int32)[None, :]
    lengths = jnp.sum(jnp.where(level_hits, jnp.asarray(LENGTH_TABLE)[None, :], 0), axis=1).astype(
        jnp.int32
    )
    starts = jnp.cumsum(lengths) - lengths
    position = jnp.arange(row_count, dtype=jnp.int32)[:, None]
    inside = (position >= starts[None, :]) & (position < (starts + lengths)[None, :])
    offset = position - starts[None, :]
    reached = jnp.sum(
        (offset[:, :, None] >= jnp.asarray(SCALE_BOUNDS)[None, None, :]).astype(jnp.int32), axis=2
    )
    inside_int = inside.astype(jnp.int32)
    slots = jnp.arange(level_row.shape[0], dtype=jnp.int32)[None, :]
    covered = jnp.sum(inside_int, axis=1)
    item_of = jnp.where(covered > 0, jnp.sum(inside_int * slots, axis=1), -1)
    scale_of = jnp.sum(inside_int * reached, axis=1)
    return (inside.astype(jnp.float32), item_of, scale_of)


def block_mask(item_of, scale_of, first_row, count):
    query_item = lax.dynamic_slice_in_dim(item_of, first_row, count)
    query_scale = lax.dynamic_slice_in_dim(scale_of, first_row, count)
    query_pos = first_row + jnp.arange(count, dtype=jnp.int32)
    key_pos = jnp.arange(item_of.shape[0], dtype=jnp.int32)
    same_item = (query_item[:, None] == item_of[None, :]) & (query_item[:, None] >= 0)
    earlier = scale_of[None, :] <= query_scale[:, None]
    return same_item & earlier | (query_pos[:, None] == key_pos[None, :])


def normalize(values):
    centered = values - jnp.mean(values, axis=-1, keepdims=True)
    return centered * lax.rsqrt(jnp.mean(centered * centered, axis=-1, keepdims=True) + NORM_EPS)


def modulate(base, scale_part, shift_part):
    return normalize(base) * (1.0 + scale_part) + shift_part


def unit_rows(values):
    return values * lax.rsqrt(jnp.sum(values * values, axis=-1, keepdims=True) + NORM_EPS)


def scale_query(values, head_scale):
    return unit_rows(values) * head_scale[None, :, None]


def gelu_tanh(values):
    return jax.nn.gelu(values, approximate=True)


def per_device(
    tokens,
    class_table,
    ada_weight,
    qkv_weight,
    proj_weight,
    head_scale,
    fc1_weight,
    fc2_weight,
    levels,
    labels,
    cotangent,
):
    row_count, model_width = tokens.shape
    head_count = head_scale.shape[0]
    head_size = model_width // head_count
    table_full, ada_full, qkv_full, proj_full = (
        lax.all_gather(class_table, ("wide", "narrow"), axis=0, tiled=True),
        lax.all_gather(ada_weight, ("wide", "narrow"), axis=0, tiled=True),
        lax.all_gather(qkv_weight, ("wide", "narrow"), axis=0, tiled=True),
        lax.all_gather(proj_weight, ("wide", "narrow"), axis=0, tiled=True),
    )
    label_pick = (
        labels[0][:, None] == jnp.arange(table_full.shape[0], dtype=jnp.int32)[None, :]
    ).astype(jnp.bfloat16)
    class_vec = jnp.dot(label_pick, table_full, preferred_element_type=jnp.float32)
    lifted = jax.nn.silu(class_vec).astype(jnp.bfloat16)
    modulation = jnp.dot(lifted, ada_full, preferred_element_type=jnp.float32)
    member, item_of, scale_of = layout(levels[0], row_count)
    per_token = jnp.dot(member, modulation, precision=FULL_PRECISION)
    gamma1, gamma2, scale1, scale2, shift1, shift2 = jnp.split(per_token, 6, axis=1)
    inputs_full = tokens.astype(jnp.float32)
    hidden_one = modulate(inputs_full, scale1, shift1).astype(jnp.bfloat16)
    projected = jnp.dot(hidden_one, qkv_full, preferred_element_type=jnp.float32).reshape(
        row_count, 3, head_count, head_size
    )
    raw_query = projected[:, 0]
    raw_key = projected[:, 1]
    queries = scale_query(raw_query, head_scale).astype(jnp.bfloat16)
    keys_unit = unit_rows(raw_key).astype(jnp.bfloat16)
    values_low = projected[:, 2].astype(jnp.bfloat16)
    block_rows = min(512, row_count)
    block_count = row_count // block_rows

    def attend(block_index):
        first_row = block_index * block_rows
        query_block = lax.dynamic_slice_in_dim(queries, first_row, block_rows, 0)
        allowed = block_mask(item_of, scale_of, first_row, block_rows)
        scores = jnp.einsum(
            "qhd,khd->hqk", query_block, keys_unit, preferred_element_type=jnp.float32
        )
        scores = jnp.where(allowed[None], scores, NEG_LARGE)
        row_max = jnp.max(scores, axis=-1, keepdims=True)
        expo = jnp.exp(scores - row_max)
        row_total = jnp.sum(expo, axis=-1, keepdims=True)
        prob_low = (expo / row_total).astype(jnp.bfloat16)
        mixed_block = jnp.einsum(
            "hqk,khd->qhd", prob_low, values_low, preferred_element_type=jnp.float32
        )
        return (mixed_block, (row_max + jnp.log(row_total))[..., 0])

    mixed_blocks, log_total = lax.map(attend, jnp.arange(block_count, dtype=jnp.int32))
    mixed = mixed_blocks.reshape(row_count, model_width).astype(jnp.bfloat16)
    branch = jnp.dot(mixed, proj_full, preferred_element_type=jnp.float32)
    after_attn = inputs_full + gamma1 * branch
    hidden_two = modulate(after_attn, scale2, shift2).astype(jnp.bfloat16)
    fc1_full, fc2_full = (
        lax.all_gather(fc1_weight, ("wide", "narrow"), axis=0, tiled=True),
        lax.all_gather(fc2_weight, ("wide", "narrow"), axis=0, tiled=True),
    )
    expanded = jnp.dot(hidden_two, fc1_full, preferred_element_type=jnp.float32)
    activated = gelu_tanh(expanded).astype(jnp.bfloat16)
    mlp_out = jnp.dot(activated, fc2_full, preferred_element_type=jnp.float32)
    output = (after_attn + gamma2 * mlp_out).astype(jnp.bfloat16)
    grad_out = cotangent.astype(jnp.float32)
    fc1_back, fc2_back, qkv_back, proj_back = (
        lax.all_gather(fc1_weight, ("wide", "narrow"), axis=0, tiled=True),
        lax.all_gather(fc2_weight, ("wide", "narrow"), axis=0, tiled=True),
        lax.all_gather(qkv_weight, ("wide", "narrow"), axis=0, tiled=True),
        lax.all_gather(proj_weight, ("wide", "narrow"), axis=0, tiled=True),
    )
    mlp_down = (grad_out * gamma2).astype(jnp.bfloat16)
    d_gamma2 = grad_out * mlp_out
    fc2_sum = jnp.einsum("tf,td->fd", activated, mlp_down, preferred_element_type=jnp.float32)
    activated_grad = jnp.einsum("td,fd->tf", mlp_down, fc2_back, preferred_element_type=jnp.float32)
    _, gelu_pull = jax.vjp(gelu_tanh, expanded)
    expanded_grad = gelu_pull(activated_grad)[0].astype(jnp.bfloat16)
    fc1_sum = jnp.einsum("td,tf->df", hidden_two, expanded_grad, preferred_element_type=jnp.float32)
    hidden_two_grad = jnp.einsum(
        "tf,df->td", expanded_grad, fc1_back, preferred_element_type=jnp.float32
    )
    fc1_grad, fc2_grad = (
        lax.psum_scatter(fc1_sum, ("wide", "narrow"), scatter_dimension=0, tiled=True),
        lax.psum_scatter(fc2_sum, ("wide", "narrow"), scatter_dimension=0, tiled=True),
    )
    _, second_pull = jax.vjp(modulate, after_attn, scale2, shift2)
    after_part, d_scale2, d_shift2 = second_pull(hidden_two_grad)
    attn_grad_in = grad_out + after_part
    branch_grad = (attn_grad_in * gamma1).astype(jnp.bfloat16)
    d_gamma1 = attn_grad_in * branch
    proj_sum = jnp.einsum("td,te->de", mixed, branch_grad, preferred_element_type=jnp.float32)
    mixed_grad = jnp.einsum("te,de->td", branch_grad, proj_back, preferred_element_type=jnp.float32)
    mixed_grad = mixed_grad.astype(jnp.bfloat16).reshape(row_count, head_count, head_size)

    def back_block(partials, packed):
        key_acc, value_acc = partials
        block_index, block_total = packed
        first_row = block_index * block_rows
        query_block = lax.dynamic_slice_in_dim(queries, first_row, block_rows, 0)
        grad_block = lax.dynamic_slice_in_dim(mixed_grad, first_row, block_rows, 0)
        allowed = block_mask(item_of, scale_of, first_row, block_rows)
        scores = jnp.einsum(
            "qhd,khd->hqk", query_block, keys_unit, preferred_element_type=jnp.float32
        )
        scores = jnp.where(allowed[None], scores, NEG_LARGE)
        attn_prob = jnp.exp(scores - block_total[..., None])
        prob_grad = jnp.einsum(
            "qhd,khd->hqk", grad_block, values_low, preferred_element_type=jnp.float32
        )
        inner = jnp.sum(attn_prob * prob_grad, axis=-1, keepdims=True)
        score_grad = (attn_prob * (prob_grad - inner)).astype(jnp.bfloat16)
        query_part = jnp.einsum(
            "hqk,khd->qhd", score_grad, keys_unit, preferred_element_type=jnp.float32
        )
        key_acc = key_acc + jnp.einsum(
            "hqk,qhd->khd", score_grad, query_block, preferred_element_type=jnp.float32
        )
        value_acc = value_acc + jnp.einsum(
            "hqk,qhd->khd",
            attn_prob.astype(jnp.bfloat16),
            grad_block,
            preferred_element_type=jnp.float32,
        )
        return ((key_acc, value_acc), query_part)

    zero_heads = jnp.zeros((row_count, head_count, head_size), jnp.float32)
    (key_grad, value_grad), query_parts = lax.scan(
        back_block, (zero_heads, zero_heads), (jnp.arange(block_count, dtype=jnp.int32), log_total)
    )
    query_grad = query_parts.reshape(row_count, head_count, head_size)
    _, query_pull = jax.vjp(scale_query, raw_query, head_scale)
    raw_query_grad, scale_part = query_pull(query_grad)
    _, key_pull = jax.vjp(unit_rows, raw_key)
    raw_key_grad = key_pull(key_grad)[0]
    projected_grad = (
        jnp.stack([raw_query_grad, raw_key_grad, value_grad], axis=1)
        .reshape(row_count, 3 * model_width)
        .astype(jnp.bfloat16)
    )
    qkv_sum = jnp.einsum(
        "td,tc->dc", hidden_one, projected_grad, preferred_element_type=jnp.float32
    )
    hidden_one_grad = jnp.einsum(
        "tc,dc->td", projected_grad, qkv_back, preferred_element_type=jnp.float32
    )
    _, first_pull = jax.vjp(modulate, inputs_full, scale1, shift1)
    input_part, d_scale1, d_shift1 = first_pull(hidden_one_grad)
    tokens_grad = (attn_grad_in + input_part).astype(jnp.bfloat16)
    token_mod_grad = jnp.concatenate(
        [d_gamma1, d_gamma2, d_scale1, d_scale2, d_shift1, d_shift2], axis=1
    )
    modulation_grad = jnp.einsum(
        "ti,tc->ic", member, token_mod_grad, precision=FULL_PRECISION
    ).astype(jnp.bfloat16)
    ada_sum = jnp.einsum("id,ic->dc", lifted, modulation_grad, preferred_element_type=jnp.float32)
    lifted_grad = jnp.einsum(
        "ic,dc->id", modulation_grad, ada_full, preferred_element_type=jnp.float32
    )
    _, silu_pull = jax.vjp(jax.nn.silu, class_vec)
    class_grad = silu_pull(lifted_grad)[0]
    table_sum = jnp.einsum(
        "ic,id->cd", label_pick.astype(jnp.float32), class_grad, precision=FULL_PRECISION
    )
    table_grad, ada_grad, qkv_grad, proj_grad = (
        lax.psum_scatter(table_sum, ("wide", "narrow"), scatter_dimension=0, tiled=True),
        lax.psum_scatter(ada_sum, ("wide", "narrow"), scatter_dimension=0, tiled=True),
        lax.psum_scatter(qkv_sum, ("wide", "narrow"), scatter_dimension=0, tiled=True),
        lax.psum_scatter(proj_sum, ("wide", "narrow"), scatter_dimension=0, tiled=True),
    )
    scale_grad = lax.psum(scale_part, ("wide", "narrow"))
    return (
        output,
        tokens_grad,
        table_grad,
        ada_grad,
        qkv_grad,
        proj_grad,
        scale_grad,
        fc1_grad,
        fc2_grad,
    )


def solution(mesh):
    in_specs = (
        P(("wide", "narrow"), None),
        P(("wide", "narrow"), None),
        P(("wide", "narrow"), None),
        P(("wide", "narrow"), None),
        P(("wide", "narrow"), None),
        P(),
        P(("wide", "narrow"), None),
        P(("wide", "narrow"), None),
        P(("wide", "narrow"), None),
        P(("wide", "narrow"), None),
        P(("wide", "narrow"), None),
    )
    out_specs = (
        P(("wide", "narrow"), None),
        P(("wide", "narrow"), None),
        P(("wide", "narrow"), None),
        P(("wide", "narrow"), None),
        P(("wide", "narrow"), None),
        P(("wide", "narrow"), None),
        P(),
        P(("wide", "narrow"), None),
        P(("wide", "narrow"), None),
    )
    return jax.shard_map(
        per_device, mesh=mesh, in_specs=in_specs, out_specs=out_specs, check_vma=False
    )
```

profile of v0, /device:TPU:0, one launch (start us, length us, event | category | flops | bytes accessed | tf_op | source)
XLA Modules:
  0.0 1857.6 jit_solution(18347227528792520619)
XLA Ops:
  15.9 54.1 %all-gather.7.cloned.1.call-done = bf16[1024,1024]{1,0:T(8,128)(2,1)} async-done(((bf16[32,1024]{1,0:T(8,128)(2,1)}), bf16[1024,1024]{1,0:T(8,128)(2,1)}) %all-gather.7.cloned.1.call-update) | async-done | bytes 2097168 | tf_op jit(solution)/shard_map/all_gather | solution.py:82
  72.0 95.7 %all-gather.9.cloned.1.call-done = bf16[1024,6144]{1,0:T(8,128)(2,1)} async-done(((bf16[32,6144]{1,0:T(8,128)(2,1)}), bf16[1024,6144]{1,0:T(8,128)(2,1)}) %all-gather.9.cloned.1.call-update) | async-done | bytes 12582928 | tf_op jit(solution)/shard_map/all_gather | solution.py:83
  174.0 10.9 fusion.73
  184.9 8.3 copy-done.6
  195.5 42.8 %all-gather.11.cloned.1.call-done = bf16[1024,3072]{1,0:T(8,128)(2,1)} async-done(((bf16[32,3072]{1,0:T(8,128)(2,1)}), bf16[1024,3072]{1,0:T(8,128)(2,1)}) %all-gather.11.cloned.1.call-update) | async-done | bytes 6291472 | tf_op jit(solution)/shard_map/all_gather | solution.py:84
  238.3 9.5 fusion.88
  255.9 97.8 %while.27 = (s32[]{:T(128)}, bf16[2,512,16,64]{1,3,2,0:T(8,128)(2,1)}, f32[2,16,512]{2,1,0:T(8,128)S(1)}, s32[2]{0:T(128)S(1)}, s32[1024]{0:T(1024)S(1)}, /*inde...) while((s32[]{:T(128)}, ...), condition=%wide.region_13.14_spmd, body=%wide.region_10.13_spmd.sunk | while | flops 2226119680 | bytes 135554320 | solution.py:126
  258.6 14.8 select_reduce_fusion.5
  273.4 15.1 fusion.146
  288.5 14.3 bitcast_dynamic-update-slice_fusion.4
  306.6 14.8 select_reduce_fusion.5
  321.4 15.3 fusion.146
  336.7 15.3 bitcast_dynamic-update-slice_fusion.4
  359.3 9.1 fusion.86
  375.7 16.0 fusion.89
  391.6 62.3 %all-gather.17.cloned.1.call-done = bf16[4096,1024]{1,0:T(8,128)(2,1)} async-done(((bf16[128,1024]{1,0:T(8,128)(2,1)}), bf16[4096,1024]{1,0:T(8,128)(2,1)}) %all-gather.17.cloned.1.call-update) | async-done | bytes 8388624 | tf_op jit(solution)/shard_map/all_gather | solution.py:133
  454.0 25.4 %fusion.33 = bf16[1024,4096]{1,0:T(8,128)(2,1)} fusion(f32[1024,4096]{1,0:T(8,128)} %fusion.89, bf16[4096,1024]{1,0:T(8,128)(2,1)} %all-gather.17.cloned.1.call-done, bf16[1024,1024]{1,0:T(8,128)(2,1)} %param.27, f32[1024,6144]{1,0:T(8,128)} %copy-done.6), kind=kOutput, calls=%fused_computation.50 | convolution fusion | flops 8676966400 | bytes 39845888 | tf_op jit(solution)/shard_map/td,fd->tf/dot_general | solution.py:149
  479.3 17.3 multiply_reduce_fusion.3
  496.6 25.7 %fusion.85 = (f32[1024]{0:T(1024)S(1)}, f32[1024,1024]{1,0:T(8,128)}, bf16[1024,1024]{1,0:T(8,128)(2,1)}, f32[1024,1024]{1,0:T(8,128)}) fusion(f32[1024]{0:T(1024)S(1)} %multiply_multiply_fusion.5, f32[1024,1024]{1,0:T(8,128)} %copy-done.8, f32[1024]{0:T(1024)S(1)} %broadcast_multiply_fusion, f32[1024]{0:T(1024)S(1)} %fusion.70, ...), kind=kOutput, calls=%fused_computation.158 | convolution fusion | flops 8639216640 | bytes 52445184 | tf_op jit(solution)/shard_map/dot_general | solution.py:137
  522.4 8.4 multiply_dynamic-update-slice_fusion.1
  542.5 298.1 %while.28 = (s32[]{:T(128)}, f32[1024,16,64]{0,2,1:T(8,128)}, f32[1024,16,64]{0,2,1:T(8,128)}, f32[2,512,16,64]{1,0,3,2:T(2,128)}, s32[2]{0:T(128)S(1)}, /*index...) while((s32[]{:T(128)}, f32[1024,16,64]{0,2,1:T(8,128)}, ...), condition=%wide.region_20.21_spmd.clone, body=%wide.region_18.20_spmd.clone.sunk | while | flops 5476705280 | bytes 384034176 | solution.py:201
  545.2 14.5 fusion.156
  559.7 17.2 bitcast_add_fusion.5
  576.9 25.2 %multiply_reduce_fusion.7 = (f32[16,512]{1,0:T(8,128)S(1)}, f32[16,512,1024]{2,1,0:T(8,128)}) fusion(f32[16,512,1024]{2,1,0:T(8,128)} %fusion.156, f32[16,512]{1,0:T(8,128)S(1)} %dynamic-slice_bitcast_fusion.2, pred[512,1024]{1,0:T(8,128)(4,1)S(1)} %fusion.157, bf16[1024,16,64]{0,2,1:T(8,128)(2,1)} %get-tuple-element.470, ...), kind=kOutput, calls=%fused_computation.16.clone.1 | convolution fusion | flops 1107288064 | bytes 70844416 | tf_op jit(solution)/shard_map/while/body/eval_jaxpr/qhd,khd->hqk/dot_general | solution.py:181
  602.2 28.0 %multiply_convert_fusion.10 = bf16[16,512,1024]{2,1,0:T(8,128)(2,1)} fusion(f32[16,512,1024]{2,1,0:T(8,128)} %get-tuple-element.386, f32[16,512,1024]{2,1,0:T(8,128)} %fusion.156, f32[16,512]{1,0:T(8,128)S(1)} %get-tuple-element.387, f32[16,512]{1,0:T(8,128)S(1)} %dynamic-slice_bitcast_fusion.2, pred[512,1024]{1,0:T(8,128)(4,1)S(1)} %fusion.157), kind=kLoop, calls=%fused_computation.15.clone.1 | loop fusion | flops 41943040 | bytes 84475904 | tf_op jit(solution)/shard_map/while/body/eval_jaxpr/convert_element_type | solution.py:185
  630.2 10.6 convolution_bitcast_fusion.2
  652.4 38.1 %dynamic_update_slice.19 = f32[2,512,16,64]{1,0,3,2:T(2,128)} dynamic-update-slice(f32[2,512,16,64]{1,0,3,2:T(2,128)} %get-tuple-element.446, f32[1,512,16,64]{1,0,3,2:T(1,128)} %copy.87, s32[]{:T(128)S(6)} %copy.105, s32[]{:T(128)} %constant.51.clone.1..sunk.1, s32[]{:T(128)} %constant.51.clone.1..sunk.1, s32[]{:T(128)} %constant.51.clone.1..sunk.1) | dynamic-update-slice | bytes 4194308 | tf_op jit(solution)/shard_map/while/body/jit(dynamic_update_index_in_dim)/dynamic_update_slice | solution.py:126
  693.1 14.4 fusion.156
  707.6 18.3 bitcast_add_fusion.5
  725.8 25.2 %multiply_reduce_fusion.7 = (f32[16,512]{1,0:T(8,128)S(1)}, f32[16,512,1024]{2,1,0:T(8,128)}) fusion(f32[16,512,1024]{2,1,0:T(8,128)} %fusion.156, f32[16,512]{1,0:T(8,128)S(1)} %dynamic-slice_bitcast_fusion.2, pred[512,1024]{1,0:T(8,128)(4,1)S(1)} %fusion.157, bf16[1024,16,64]{0,2,1:T(8,128)(2,1)} %get-tuple-element.470, ...), kind=kOutput, calls=%fused_computation.16.clone.1 | convolution fusion | flops 1107288064 | bytes 70844416 | tf_op jit(solution)/shard_map/while/body/eval_jaxpr/qhd,khd->hqk/dot_general | solution.py:181
  751.1 27.8 %multiply_convert_fusion.10 = bf16[16,512,1024]{2,1,0:T(8,128)(2,1)} fusion(f32[16,512,1024]{2,1,0:T(8,128)} %get-tuple-element.386, f32[16,512,1024]{2,1,0:T(8,128)} %fusion.156, f32[16,512]{1,0:T(8,128)S(1)} %get-tuple-element.387, f32[16,512]{1,0:T(8,128)S(1)} %dynamic-slice_bitcast_fusion.2, pred[512,1024]{1,0:T(8,128)(4,1)S(1)} %fusion.157), kind=kLoop, calls=%fused_computation.15.clone.1 | loop fusion | flops 41943040 | bytes 84475904 | tf_op jit(solution)/shard_map/while/body/eval_jaxpr/convert_element_type | solution.py:185
  778.9 10.6 convolution_bitcast_fusion.2
  790.8 7.9 bitcast_add_fusion.4
  802.2 38.1 %dynamic_update_slice.19 = f32[2,512,16,64]{1,0,3,2:T(2,128)} dynamic-update-slice(f32[2,512,16,64]{1,0,3,2:T(2,128)} %get-tuple-element.446, f32[1,512,16,64]{1,0,3,2:T(1,128)} %copy.87, s32[]{:T(128)S(6)} %copy.105, s32[]{:T(128)} %constant.51.clone.1..sunk.1, s32[]{:T(128)} %constant.51.clone.1..sunk.1, s32[]{:T(128)} %constant.51.clone.1..sunk.1) | dynamic-update-slice | bytes 4194308 | tf_op jit(solution)/shard_map/while/body/jit(dynamic_update_index_in_dim)/dynamic_update_slice | solution.py:126
  847.2 6.7 reshape.399
  853.9 8.3 fusion.53
  881.7 14.8 fusion.42
  904.7 13.1 convolution_convert_fusion
  925.2 12.2 fusion.91
  937.4 21.0 %fusion.77 = f32[4096,1024]{1,0:T(8,128)} fusion(bf16[1024,1024]{1,0:T(8,128)(2,1)} %param.27, f32[1024,6144]{1,0:T(8,128)} %copy-done.6, f32[1024,4096]{1,0:T(8,128)} %fusion.89), kind=kOutput, calls=%fused_computation.154 | convolution fusion | flops 8630829056 | bytes 39845888 | tf_op jit(solution)/shard_map/tf,td->fd/dot_general | solution.py:148
  958.4 16.2 fusion.93
  974.7 10.5 fusion.75
  997.8 40.2 %psum.7 = f32[16]{0:T(128)} all-reduce(f32[16]{0:T(128)S(1)} %multiply_reduce_fusion.1), channel_id=1, replica_groups=mesh['wide'=16,'narrow'=2] {'wide','narrow'}, use_global_device_ids=true, to_apply=%region_30.31 | all-reduce | flops 16 | bytes 128 | tf_op jit(solution)/shard_map/psum | solution.py:244
  1045.5 19.7 %reduce-scatter.7.cloned.1.call-done = f32[32,1024]{1,0:T(8,128)} async-done(((f32[1024,1024]{1,0:T(8,128)}), f32[32,1024]{1,0:T(8,128)}) %reduce-scatter.7.cloned.1.call-update) | async-done | bytes 131088 | tf_op jit(solution)/shard_map/reduce_scatter | solution.py:239
  1065.2 157.9 %reduce-scatter.11.cloned.1.call-done = f32[32,3072]{1,0:T(8,128)} async-done(((f32[1024,3072]{1,0:T(8,128)}), f32[32,3072]{1,0:T(8,128)}) %reduce-scatter.11.cloned.1.call-update) | async-done | bytes 393232 | tf_op jit(solution)/shard_map/reduce_scatter | solution.py:241
  1223.1 184.9 %reduce-scatter.17.cloned.1.call-done = f32[128,1024]{1,0:T(8,128)} async-done(((f32[4096,1024]{1,0:T(8,128)}), f32[128,1024]{1,0:T(8,128)}) %reduce-scatter.17.cloned.1.call-update) | async-done | bytes 524304 | tf_op jit(solution)/shard_map/reduce_scatter | solution.py:158
  1407.9 187.5 %reduce-scatter.15.cloned.1.call-done = f32[32,4096]{1,0:T(8,128)} async-done(((f32[1024,4096]{1,0:T(8,128)}), f32[32,4096]{1,0:T(8,128)}) %reduce-scatter.15.cloned.1.call-update) | async-done | bytes 524304 | tf_op jit(solution)/shard_map/reduce_scatter | solution.py:157
  1595.4 255.0 %reduce-scatter.9.cloned.1.call-done = f32[32,6144]{1,0:T(8,128)} async-done(((f32[1024,6144]{1,0:T(8,128)}), f32[32,6144]{1,0:T(8,128)}) %reduce-scatter.9.cloned.1.call-update) | async-done | bytes 786448 | tf_op jit(solution)/shard_map/reduce_scatter | solution.py:240
  (239 shorter events, 139.7 us)
Async XLA Ops:
  7.2 8.5 copy-start.54
  7.2 7.1 copy-start.10
  7.2 62.8 %copy-start.52 = (s32[1,6]{1,0:T(1,128)S(1)}, s32[1,6]{1,0:T(1,128)}, u32[]{:S(2)}) copy-start(s32[1,6]{1,0:T(1,128)} %param.26) | copy-start | bytes 76
  7.2 62.8 %all-gather.7.cloned.1.call-start = ((), (), s32[]{:S(2)}) async-start(), calls=%async_computation.6 | async-start | bytes 2162688 | tf_op jit(solution)/shard_map/all_gather | solution.py:82
  7.9 159.7 %all-gather.9.cloned.1.call-start = ((), (), s32[]{:S(2)}) async-start(), calls=%async_computation.7 | async-start | bytes 12976128 | tf_op jit(solution)/shard_map/all_gather | solution.py:83
  8.7 229.6 %all-gather.11.cloned.1.call-start = ((), (), s32[]{:S(2)}) async-start(), calls=%async_computation.8 | async-start | bytes 6488064 | tf_op jit(solution)/shard_map/all_gather | solution.py:84
  9.4 349.9 %all-gather.13.cloned.1.call-start = ((), (), s32[]{:S(2)}) async-start(), calls=%async_computation.9 | async-start | bytes 2162688 | tf_op jit(solution)/shard_map/all_gather | solution.py:85
  10.0 365.7 %all-gather.15.cloned.1.call-start = ((), (), s32[]{:S(2)}) async-start(), calls=%async_computation.10 | async-start | bytes 8650752 | tf_op jit(solution)/shard_map/all_gather | solution.py:132
  10.6 443.4 %all-gather.17.cloned.1.call-start = ((), (), s32[]{:S(2)}) async-start(), calls=%async_computation.11 | async-start | bytes 8650752 | tf_op jit(solution)/shard_map/all_gather | solution.py:133
  11.2 1034.3 %reduce-scatter.13.cloned.1.call-start = ((), (), s32[]{:S(2)}) async-start(), calls=%async_computation.15 | async-start | bytes 4325376 | tf_op jit(solution)/shard_map/reduce_scatter | solution.py:242
  12.3 161.7 %copy-start.48 = (s32[6,1]{0,1:T(1,128)}, s32[6,1]{0,1:T(1,128)S(1)}, u32[]{:S(2)}) copy-start(s32[6,1]{0,1:T(1,128)S(1)} %reduce-window.7) | copy-start | bytes 76
  12.3 161.7 %copy-start.46 = (s32[6]{0:T(128)}, s32[6]{0:T(128)S(1)}, u32[]{:S(2)}) copy-start(s32[6]{0:T(128)S(1)} %bitcast_subtract_fusion) | copy-start | bytes 76
  14.3 170.6 %copy-start.34 = (f32[1024]{0:T(1024)}, f32[1024]{0:T(1024)S(1)}, u32[]{:S(2)}) copy-start(f32[1024]{0:T(1024)S(1)} %broadcast_multiply_fusion.1) | copy-start | bytes 12292
  15.6 169.3 %copy-start.38 = (f32[1024]{0:T(1024)}, f32[1024]{0:T(1024)S(1)}, u32[]{:S(2)}) copy-start(f32[1024]{0:T(1024)S(1)} %fusion.69) | copy-start | bytes 12292
  72.0 102.0 %copy-start.26 = (f32[6,1024]{1,0:T(8,128)}, f32[6,1024]{1,0:T(8,128)S(1)}, u32[]{:S(2)}) copy-start(f32[6,1024]{1,0:T(8,128)S(1)} %fusion.64) | copy-start | bytes 73732
  184.9 8.3 copy-start.6
  249.2 6.7 copy-start.28
  273.3 15.2 copy-start.4
  273.3 15.2 copy-start.21
  321.4 15.3 copy-start.4
  321.4 15.3 copy-start.21
  368.4 128.2 %copy-start.36 = (f32[1024]{0:T(1024)}, f32[1024]{0:T(1024)S(1)}, u32[]{:S(2)}) copy-start(f32[1024]{0:T(1024)S(1)} %broadcast_multiply_fusion) | copy-start | bytes 12292
  370.4 126.2 %copy-start.40 = (f32[1024]{0:T(1024)}, f32[1024]{0:T(1024)S(1)}, u32[]{:S(2)}) copy-start(f32[1024]{0:T(1024)S(1)} %fusion.70) | copy-start | bytes 12292
  522.4 8.4 copy-start.44
  522.4 9.7 copy-start.19
  536.5 528.7 %reduce-scatter.7.cloned.1.call-start = ((), (), s32[]{:S(2)}) async-start(), calls=%async_computation.12 | async-start | bytes 4325376 | tf_op jit(solution)/shard_map/reduce_scatter | solution.py:239
  542.6 17.1 copy-start.1
  630.2 12.0 copy-start
  648.9 41.7 %copy-start.2 = (bf16[1024,16,64]{0,2,1:T(8,128)(2,1)S(1)}, bf16[1024,16,64]{0,2,1:T(8,128)(2,1)}, u32[]{:S(2)}) copy-start(bf16[1024,16,64]{0,2,1:T(8,128)(2,1)} %copy-done.1) | copy-start | bytes 6291460 | tf_op jit(solution)/shard_map/while
  690.6 17.0 copy-start.1
  778.9 11.9 copy-start
  790.8 7.9 copy-start.12
  798.7 41.7 %copy-start.2 = (bf16[1024,16,64]{0,2,1:T(8,128)(2,1)S(1)}, bf16[1024,16,64]{0,2,1:T(8,128)(2,1)}, u32[]{:S(2)}) copy-start(bf16[1024,16,64]{0,2,1:T(8,128)(2,1)} %copy-done.1) | copy-start | bytes 6291460 | tf_op jit(solution)/shard_map/while
  853.9 8.4 copy-start.29
  853.9 8.4 copy-start.31
  853.9 8.5 copy-start.5
  881.6 14.9 copy-start.9
  881.6 14.9 copy-start.16
  881.7 14.9 copy-start.37
  881.7 14.9 copy-start.41
  902.2 15.6 slice-start
  904.7 13.1 slice-start.1
  904.7 13.1 slice-start.2
  925.1 298.0 %reduce-scatter.11.cloned.1.call-start = ((), (), s32[]{:S(2)}) async-start(), calls=%async_computation.14 | async-start | bytes 12976128 | tf_op jit(solution)/shard_map/reduce_scatter | solution.py:241
  937.3 470.6 %reduce-scatter.17.cloned.1.call-start = ((), (), s32[]{:S(2)}) async-start(), calls=%async_computation.17 | async-start | bytes 17301504 | tf_op jit(solution)/shard_map/reduce_scatter | solution.py:158
  958.4 637.1 %reduce-scatter.15.cloned.1.call-start = ((), (), s32[]{:S(2)}) async-start(), calls=%async_computation.16 | async-start | bytes 17301504 | tf_op jit(solution)/shard_map/reduce_scatter | solution.py:157
  974.6 875.8 %reduce-scatter.9.cloned.1.call-start = ((), (), s32[]{:S(2)}) async-start(), calls=%async_computation.13 | async-start | bytes 25952256 | tf_op jit(solution)/shard_map/reduce_scatter | solution.py:240
  992.0 46.0 %copy-start.43 = (f32[1024]{0:T(1024)S(1)}, f32[1024]{0:T(1024)}, u32[]{:S(2)}) copy-start(f32[1024]{0:T(1024)} %copy-done.42) | copy-start | bytes 12292
  (29 other events, 102.3 us)
Sparse Core Ops, SparseCore 0:
  10.9 59.0 all-gather.6
  72.9 94.7 all-gather.8
  170.5 67.7 all-gather.10
  241.0 54.9 all-gather.12
  298.7 76.4 all-gather.14
  377.9 76.0 all-gather.16
  536.6 139.4 reduce-scatter.12
  925.2 139.9 reduce-scatter.6
  1071.8 151.2 reduce-scatter.10
  1225.9 182.0 reduce-scatter.16
  1410.9 184.4 reduce-scatter.14
  1603.4 246.9 reduce-scatter.8
where the time goes:
time: 1870 us; the launch traced here: 1860 us
  waiting for transfers between devices  1060 us (57%)
  matrix products  437 us (23%)
  other arithmetic  156 us (8%)
  local copies, waits for them, and re-layouts  142 us (8%)
  blocking collectives  40.2 us (2%)
    reduce_scatter x1, waiting for transfers between devices, per_device(): lax.psum_scatter(ada_sum, ('wide', 'narrow'), scatter_dimension=0, tiled=...  255 us
    reduce_scatter x1, waiting for transfers between devices, per_device(): lax.psum_scatter(fc1_sum, ('wide', 'narrow'), scatter_dimension=0, tiled=...  187 us
    reduce_scatter x1, waiting for transfers between devices, per_device(): lax.psum_scatter(fc2_sum, ('wide', 'narrow'), scatter_dimension=0, tiled=...  185 us
    reduce_scatter x1, waiting for transfers between devices, per_device(): lax.psum_scatter(qkv_sum, ('wide', 'narrow'), scatter_dimension=0, tiled=...  158 us
    all_gather x1, waiting for transfers between devices, per_device(): lax.all_gather(ada_weight, ('wide', 'narrow'), axis=0, tiled=True)  95.7 us
    dynamic_update_slice x4, local copies, waits for them, and re-layouts, per_device(): lax.map(attend, jnp.arange(block_count, dtype=jnp.int32))  83.3 us
    all_gather x1, waiting for transfers between devices, per_device(): lax.all_gather(fc2_weight, ('wide', 'narrow'), axis=0, tiled=True)  62.3 us
    convert_element_type x2, other arithmetic, back_block(): score_grad = (attn_prob * (prob_grad - inner)).astype(jnp.bfloat16)  55.9 us
  transfers between devices with their start and end apart: 12, of which 9 were waited for; matrix products, arithmetic and copies ran while one was open for 34% of the time, Pallas kernels for 0%

commit v1 on v0

--- a/solution.py
+++ b/solution.py
@@ -9,6 +9,48 @@
 NEG_LARGE = -1e30
 LENGTH_TABLE = np.array([0, 1, 5, 14, 30, 55, 91, 155, 255, 424, 680], np.int32)
 SCALE_BOUNDS = np.array([1, 5, 14, 30, 55, 91, 155, 255, 424], np.int32)
+
+
+BOTH = ("wide", "narrow")
+
+
+def bit_count(size):
+    return size.bit_length() - 1
+
+
+def flip(values, axis, size, bit):
+    return lax.ppermute(values, axis, [(i, i ^ (1 << bit)) for i in range(size)])
+
+
+def halving_order(wide, narrow, turn):
+    inner = list(range(bit_count(narrow)))
+    outer = list(range(bit_count(wide)))
+    turning, last = outer[:-1], outer[-1:]
+    turn = turn % max(1, len(turning))
+    return [("narrow", b) for b in inner] + [
+        ("wide", b) for b in turning[turn:] + turning[:turn] + last
+    ]
+
+
+def scatter_sum(partial, wide, narrow, turn):
+    sizes = {"wide": wide, "narrow": narrow}
+    dims = [("wide", b) for b in reversed(range(bit_count(wide)))] + [
+        ("narrow", b) for b in reversed(range(bit_count(narrow)))
+    ]
+    rows, columns = partial.shape
+    block = partial.reshape((2,) * len(dims) + (rows // (wide * narrow), columns))
+    order = halving_order(wide, narrow, turn)
+    for step, (axis, bit) in enumerate(order):
+        at = dims.index((axis, bit))
+        dims.pop(at)
+        mine = (lax.axis_index(axis) >> bit) & 1
+        sent = lax.dynamic_index_in_dim(block, 1 - mine, at, keepdims=False)
+        kept = lax.dynamic_index_in_dim(block, mine, at, keepdims=False)
+        got = flip(sent, axis, sizes[axis], bit)
+        block = kept.astype(jnp.float32) + got.astype(jnp.float32)
+        if step < len(order) - 1:
+            block = block.astype(jnp.bfloat16)
+    return block
 
 
 def layout(level_row, row_count):
@@ -78,18 +120,32 @@
     row_count, model_width = tokens.shape
     head_count = head_scale.shape[0]
     head_size = model_width // head_count
-    table_full, ada_full, qkv_full, proj_full = (
-        lax.all_gather(class_table, ("wide", "narrow"), axis=0, tiled=True),
-        lax.all_gather(ada_weight, ("wide", "narrow"), axis=0, tiled=True),
-        lax.all_gather(qkv_weight, ("wide", "narrow"), axis=0, tiled=True),
-        lax.all_gather(proj_weight, ("wide", "narrow"), axis=0, tiled=True),
-    )
+    wide, narrow = lax.axis_size("wide"), lax.axis_size("narrow")
+    devices = wide * narrow
+    me = lax.axis_index("wide") * narrow + lax.axis_index("narrow")
+    slots = labels.shape[1]
+    own_classes = class_table.shape[0]
+    label_rows = jnp.zeros((16, model_width), jnp.bfloat16)
+    label_rows = label_rows.at[0, :slots].set((labels[0] // 256).astype(jnp.bfloat16))
+    label_rows = label_rows.at[1, :slots].set((labels[0] % 256).astype(jnp.bfloat16))
+    packed = lax.all_gather(
+        jnp.concatenate([class_table, label_rows], axis=0), BOTH, axis=0, tiled=False
+    )
+    table_full = packed[:, :own_classes].reshape(-1, model_width)
+    qkv_full, proj_full = (
+        lax.all_gather(qkv_weight, BOTH, axis=0, tiled=True),
+        lax.all_gather(proj_weight, BOTH, axis=0, tiled=True),
+    )
+    label_parts = packed[:, own_classes : own_classes + 2, :slots].astype(jnp.int32)
+    labels_all = (label_parts[:, 0] * 256 + label_parts[:, 1]).reshape(-1)
     label_pick = (
-        labels[0][:, None] == jnp.arange(table_full.shape[0], dtype=jnp.int32)[None, :]
+        labels_all[:, None] == jnp.arange(table_full.shape[0], dtype=jnp.int32)[None, :]
     ).astype(jnp.bfloat16)
     class_vec = jnp.dot(label_pick, table_full, preferred_element_type=jnp.float32)
     lifted = jax.nn.silu(class_vec).astype(jnp.bfloat16)
-    modulation = jnp.dot(lifted, ada_full, preferred_element_type=jnp.float32)
+    ada_columns = lax.all_to_all(ada_weight, BOTH, 1, 0, tiled=True)
+    modulation_columns = jnp.dot(lifted, ada_columns, preferred_element_type=jnp.float32)
+    modulation = lax.all_to_all(modulation_columns, BOTH, 0, 1, tiled=True)
     member, item_of, scale_of = layout(levels[0], row_count)
     per_token = jnp.dot(member, modulation, precision=FULL_PRECISION)
     gamma1, gamma2, scale1, scale2, shift1, shift2 = jnp.split(per_token, 6, axis=1)
@@ -137,15 +193,11 @@
     mlp_out = jnp.dot(activated, fc2_full, preferred_element_type=jnp.float32)
     output = (after_attn + gamma2 * mlp_out).astype(jnp.bfloat16)
     grad_out = cotangent.astype(jnp.float32)
-    fc1_back, fc2_back, qkv_back, proj_back = (
-        lax.all_gather(fc1_weight, ("wide", "narrow"), axis=0, tiled=True),
-        lax.all_gather(fc2_weight, ("wide", "narrow"), axis=0, tiled=True),
-        lax.all_gather(qkv_weight, ("wide", "narrow"), axis=0, tiled=True),
-        lax.all_gather(proj_weight, ("wide", "narrow"), axis=0, tiled=True),
-    )
+    fc1_back, fc2_back, qkv_back, proj_back = fc1_full, fc2_full, qkv_full, proj_full
     mlp_down = (grad_out * gamma2).astype(jnp.bfloat16)
     d_gamma2 = grad_out * mlp_out
     fc2_sum = jnp.einsum("tf,td->fd", activated, mlp_down, preferred_element_type=jnp.float32)
+    fc2_grad = scatter_sum(fc2_sum.astype(jnp.bfloat16), wide, narrow, 0)
     activated_grad = jnp.einsum("td,fd->tf", mlp_down, fc2_back, preferred_element_type=jnp.float32)
     _, gelu_pull = jax.vjp(gelu_tanh, expanded)
     expanded_grad = gelu_pull(activated_grad)[0].astype(jnp.bfloat16)
@@ -153,16 +205,14 @@
     hidden_two_grad = jnp.einsum(
         "tf,df->td", expanded_grad, fc1_back, preferred_element_type=jnp.float32
     )
-    fc1_grad, fc2_grad = (
-        lax.psum_scatter(fc1_sum, ("wide", "narrow"), scatter_dimension=0, tiled=True),
-        lax.psum_scatter(fc2_sum, ("wide", "narrow"), scatter_dimension=0, tiled=True),
-    )
+    fc1_grad = scatter_sum(fc1_sum.astype(jnp.bfloat16), wide, narrow, 1)
     _, second_pull = jax.vjp(modulate, after_attn, scale2, shift2)
     after_part, d_scale2, d_shift2 = second_pull(hidden_two_grad)
     attn_grad_in = grad_out + after_part
     branch_grad = (attn_grad_in * gamma1).astype(jnp.bfloat16)
     d_gamma1 = attn_grad_in * branch
     proj_sum = jnp.einsum("td,te->de", mixed, branch_grad, preferred_element_type=jnp.float32)
+    proj_grad = scatter_sum(proj_sum.astype(jnp.bfloat16), wide, narrow, 2)
     mixed_grad = jnp.einsum("te,de->td", branch_grad, proj_back, preferred_element_type=jnp.float32)
     mixed_grad = mixed_grad.astype(jnp.bfloat16).reshape(row_count, head_count, head_size)
 
@@ -226,22 +276,35 @@
     modulation_grad = jnp.einsum(
         "ti,tc->ic", member, token_mod_grad, precision=FULL_PRECISION
     ).astype(jnp.bfloat16)
-    ada_sum = jnp.einsum("id,ic->dc", lifted, modulation_grad, preferred_element_type=jnp.float32)
-    lifted_grad = jnp.einsum(
-        "ic,dc->id", modulation_grad, ada_full, preferred_element_type=jnp.float32
-    )
-    _, silu_pull = jax.vjp(jax.nn.silu, class_vec)
+    gathered = lax.all_gather(modulation_grad, BOTH, axis=0, tiled=True)
+    own_width = model_width // devices
+    own_lifted = lax.dynamic_slice_in_dim(lifted, me * own_width, own_width, 1)
+    own_vec = lax.dynamic_slice_in_dim(class_vec, me * own_width, own_width, 1)
+    ada_grad = jnp.einsum("id,ic->dc", own_lifted, gathered, preferred_element_type=jnp.float32)
+    lifted_grad = jnp.einsum("ic,dc->id", gathered, ada_weight, preferred_element_type=jnp.float32)
+    _, silu_pull = jax.vjp(jax.nn.silu, own_vec)
     class_grad = silu_pull(lifted_grad)[0]
-    table_sum = jnp.einsum(
+    table_columns = jnp.einsum(
         "ic,id->cd", label_pick.astype(jnp.float32), class_grad, precision=FULL_PRECISION
     )
-    table_grad, ada_grad, qkv_grad, proj_grad = (
-        lax.psum_scatter(table_sum, ("wide", "narrow"), scatter_dimension=0, tiled=True),
-        lax.psum_scatter(ada_sum, ("wide", "narrow"), scatter_dimension=0, tiled=True),
-        lax.psum_scatter(qkv_sum, ("wide", "narrow"), scatter_dimension=0, tiled=True),
-        lax.psum_scatter(proj_sum, ("wide", "narrow"), scatter_dimension=0, tiled=True),
-    )
-    scale_grad = lax.psum(scale_part, ("wide", "narrow"))
+    head_rows = -(-head_count // own_width)
+    head_rows += -head_rows % 8
+    scale_rows = jnp.pad(scale_part, (0, head_rows * own_width - head_count)).reshape(
+        1, head_rows, own_width
+    )
+    outgoing = jnp.concatenate(
+        [
+            table_columns.reshape(devices, own_classes, own_width),
+            jnp.broadcast_to(scale_rows, (devices, head_rows, own_width)),
+        ],
+        axis=1,
+    ).reshape(devices * (own_classes + head_rows), own_width)
+    incoming = lax.all_to_all(outgoing, BOTH, 0, 1, tiled=True)
+    table_grad = incoming[:own_classes]
+    scale_grad = jnp.sum(
+        incoming[own_classes:].reshape(head_rows, devices, own_width), axis=1
+    ).reshape(-1)[:head_count]
+    qkv_grad = scatter_sum(qkv_sum.astype(jnp.bfloat16), wide, narrow, 0)
     return (
         output,
         tokens_grad,

time: 1870 us -> 1080 us (0.58)
  waiting for transfers between devices: 1060 us -> 223 us
  local copies, waits for them, and re-layouts: 142 us -> 195 us
  blocking collectives: 40.2 us -> 0 us
  starting transfers between devices: 0.47 us -> 40 us
  matrix products: 437 us -> 405 us
  other arithmetic: 156 us -> 183 us
    reduce_scatter x6 -> x0, waiting for transfers between devices: 805 us -> none  [the longest x1 255 us: per_device(): lax.psum_scatter(ada_sum, ('wide', 'narrow'), scatter_dimension=0, tiled=...]
    all_gather x4, waiting for transfers between devices: 193 us -> 75.7 us  [the longest x1 50.9 us: per_device(): lax.all_gather(jnp.concatenate([class_table, label_rows], axis=0), BOTH,...]
    ppermute x0 -> x20, waiting for transfers between devices: none -> 82.8 us  [flip(): return lax.ppermute(values, axis, [(i, i ^ 1 << bit) for i in range(size)])]
    psum x1 -> x0, blocking collectives: 40.2 us -> none  [per_device(): scale_grad = lax.psum(scale_part, ('wide', 'narrow'))]
    dynamic_slice x0 -> x9, local copies, waits for them, and re-layouts: none -> 29.1 us  [the longest x4 20.1 us: scatter_sum(): kept = lax.dynamic_index_in_dim(block, mine, at, keepdims=False)]
    convert_element_type x0 -> x18, other arithmetic: none -> 27.2 us  [the longest x16 26.4 us: scatter_sum(): block = block.astype(jnp.bfloat16)]
    all_to_all x0 -> x3, waiting for transfers between devices: none -> 25.8 us  [the longest x1 14.3 us: per_device(): incoming = lax.all_to_all(outgoing, BOTH, 0, 1, tiled=True)]
    all_gather x1, waiting for transfers between devices: 62.3 us -> 36.6 us  [per_device(): lax.all_gather(fc2_weight, ('wide', 'narrow'), axis=0, tiled=True)]
  transfers between devices with their start and end apart: 12 -> 29, of which waited for: 9 -> 17; matrix products, arithmetic and copies ran while one was open for 34% -> 31% of each run, Pallas kernels for 0% -> 0%
where the time goes in v1:
time: 1080 us; the launch traced here: 1070 us
  matrix products  405 us (38%)
  waiting for transfers between devices  223 us (21%)
  local copies, waits for them, and re-layouts  195 us (18%)
  other arithmetic  183 us (17%)
  starting transfers between devices  40 us (4%)
  between operations  15.8 us (1%)
    dynamic_update_slice x4, local copies, waits for them, and re-layouts, per_device(): lax.map(attend, jnp.arange(block_count, dtype=jnp.int32))  83.3 us
    ppermute x20, waiting for transfers between devices, flip(): return lax.ppermute(values, axis, [(i, i ^ 1 << bit) for i in range(size)])  82.8 us
    convert_element_type x2, other arithmetic, back_block(): score_grad = (attn_prob * (prob_grad - inner)).astype(jnp.bfloat16)  55.6 us
    all_gather x1, waiting for transfers between devices, per_device(): lax.all_gather(jnp.concatenate([class_table, label_rows], axis=0), BOTH,...  50.9 us
    dot_general x2, matrix products, back_block(): jnp.einsum('qhd,khd->hqk', grad_block, values_low, preferred_element_type...  49.8 us
    all_gather x1, waiting for transfers between devices, per_device(): lax.all_gather(fc2_weight, ('wide', 'narrow'), axis=0, tiled=True)  36.6 us
    dot_general x2, matrix products, back_block(): jnp.einsum('hqk,qhd->khd', attn_prob.astype(jnp.bfloat16), grad_block, pr...  35.5 us
    reduce_sum x2, other arithmetic, attend(): row_total = jnp.sum(expo, axis=-1, keepdims=True)  30.4 us
  transfers between devices with their start and end apart: 29, of which 17 were waited for; matrix products, arithmetic and copies ran while one was open for 31% of the time, Pallas kernels for 0%

profile of v1, /device:TPU:0, one launch (start us, length us, event | category | flops | bytes accessed | tf_op | source)
XLA Modules:
  0.0 1065.5 jit_solution(18019633383824797888)
XLA Ops:
  24.3 50.9 %all-gather.17.cloned.1.call-done = bf16[1536,1024]{1,0:T(8,128)(2,1)} async-done(((bf16[48,1024]{1,0:T(8,128)(2,1)}), bf16[1536,1024]{1,0:T(8,128)(2,1)}) %all-gather.17.cloned.1.call-update) | async-done | bytes 3145744 | tf_op jit(solution)/shard_map/all_gather | solution.py:131
  89.3 11.6 %all-to-all-done.1 = f32[32,6,192]{2,1,0:T(8,128)S(1)} async-done(((f32[32,6,192]{2,1,0:T(8,128)}), f32[32,6,192]{2,1,0:T(8,128)S(1)}, u32[]{:S(2)}, u32[]{:S(2)}) %all-to-all-start.1) | async-done | bytes 147488 | tf_op jit(solution)/shard_map/all_to_all | solution.py:148
  101.0 11.4 %fusion.101 = f32[1024,6144]{1,0:T(8,128)S(1)} fusion(f32[6,6144]{1,0:T(8,128)S(1)} %all_to_all.42, s32[6]{0:T(128)} %bitcast.297, s32[6]{0:T(128)} %copy-done.70), kind=kOutput, calls=%fused_computation.246 | convolution fusion | flops 453003264 | bytes 25313328 | tf_op jit(solution)/shard_map/dot_general | solution.py:150
  112.4 8.4 copy-done.8
  123.0 24.8 %all-gather.9.cloned.1.call-done = bf16[1024,3072]{1,0:T(8,128)(2,1)} async-done(((bf16[32,3072]{1,0:T(8,128)(2,1)}), bf16[1024,3072]{1,0:T(8,128)(2,1)}) %all-gather.9.cloned.1.call-update) | async-done | bytes 6291472 | tf_op jit(solution)/shard_map/all_gather | solution.py:136
  147.9 9.5 fusion.114
  170.7 97.9 %while.29 = (s32[]{:T(128)}, bf16[2,512,16,64]{1,3,2,0:T(8,128)(2,1)}, f32[2,16,512]{2,1,0:T(8,128)}, s32[2]{0:T(128)S(1)}, s32[1024]{0:T(1024)S(1)}, /*index=5*...) while((s32[]{:T(128)}, ...), condition=%wide.region_13.14_spmd, body=%wide.region_10.13_spmd.sunk | while | flops 2226119680 | bytes 135554320 | solution.py:182
  173.4 14.8 %select_reduce_fusion.5 = (f32[16,512]{1,0:T(8,128)S(1)}, f32[16,512,1024]{2,1,0:T(8,128)}) fusion(pred[512,1024]{1,0:T(8,128)(4,1)S(1)} %fusion.168, bf16[1024,16,64]{0,2,1:T(8,128)(2,1)S(1)} %get-tuple-element.493, bf16[1024,16,64]{0,2,1:T(8,128)(2,1)} %get-tuple-element.492, s32[]{:T(128)S(6)} %select_n.179), kind=kOutput, calls=%fused_computation.2.clone.1 | convolution fusion | flops 1090510848 | bytes 37257220 | tf_op jit(solution)/shard_map/while/body/eval_jaxpr/qhd,khd->hqk/dot_general | solution.py:169
  188.2 15.3 %fusion.169 = f32[16,512]{1,0:T(8,128)S(1)} fusion(f32[16,512,1024]{2,1,0:T(8,128)} %get-tuple-element.442, f32[16,512]{1,0:T(8,128)S(1)} %get-tuple-element.443, pred[512,1024]{1,0:T(8,128)(4,1)S(1)} %fusion.168), kind=kLoop, calls=%fused_computation.3.clone.1 | loop fusion | flops 25157632 | bytes 34144256 | tf_op jit(solution)/shard_map/while/body/eval_jaxpr/reduce_sum | solution.py:175
  203.6 14.2 %bitcast_dynamic-update-slice_fusion.4 = bf16[2,512,16,64]{1,3,2,0:T(8,128)(2,1)S(1)} fusion(bf16[2,512,16,64]{1,3,2,0:T(8,128)(2,1)S(1)} %copy-done.41, s32[]{:T(128)S(6)} %copy.284, bf16[1024,16,64]{0,2,1:T(8,128)(2,1)S(1)} %copy-done.5, f32[16,512,1024]{2,1,0:T(8,128)} %get-tuple-element.442, f32[16,512]{1,0:T(8,128)S(1)} %fusion.169, ...), kind=kOutput, calls=%fused_computation.5.clone.1 | convolution fusion | flops 1107296256 | bytes 38338564 | tf_op jit(solution)/shard_map/while/body/eval_jaxpr/hqk,khd->qhd/dot_general | solution.py:177
  221.6 15.0 %select_reduce_fusion.5 = (f32[16,512]{1,0:T(8,128)S(1)}, f32[16,512,1024]{2,1,0:T(8,128)}) fusion(pred[512,1024]{1,0:T(8,128)(4,1)S(1)} %fusion.168, bf16[1024,16,64]{0,2,1:T(8,128)(2,1)S(1)} %get-tuple-element.493, bf16[1024,16,64]{0,2,1:T(8,128)(2,1)} %get-tuple-element.492, s32[]{:T(128)S(6)} %select_n.179), kind=kOutput, calls=%fused_computation.2.clone.1 | convolution fusion | flops 1090510848 | bytes 37257220 | tf_op jit(solution)/shard_map/while/body/eval_jaxpr/qhd,khd->hqk/dot_general | solution.py:169
  236.6 15.1 %fusion.169 = f32[16,512]{1,0:T(8,128)S(1)} fusion(f32[16,512,1024]{2,1,0:T(8,128)} %get-tuple-element.442, f32[16,512]{1,0:T(8,128)S(1)} %get-tuple-element.443, pred[512,1024]{1,0:T(8,128)(4,1)S(1)} %fusion.168), kind=kLoop, calls=%fused_computation.3.clone.1 | loop fusion | flops 25157632 | bytes 34144256 | tf_op jit(solution)/shard_map/while/body/eval_jaxpr/reduce_sum | solution.py:175
  251.7 15.2 %bitcast_dynamic-update-slice_fusion.4 = bf16[2,512,16,64]{1,3,2,0:T(8,128)(2,1)S(1)} fusion(bf16[2,512,16,64]{1,3,2,0:T(8,128)(2,1)S(1)} %copy-done.41, s32[]{:T(128)S(6)} %copy.284, bf16[1024,16,64]{0,2,1:T(8,128)(2,1)S(1)} %copy-done.5, f32[16,512,1024]{2,1,0:T(8,128)} %get-tuple-element.442, f32[16,512]{1,0:T(8,128)S(1)} %fusion.169, ...), kind=kOutput, calls=%fused_computation.5.clone.1 | convolution fusion | flops 1107296256 | bytes 38338564 | tf_op jit(solution)/shard_map/while/body/eval_jaxpr/hqk,khd->qhd/dot_general | solution.py:177
  275.1 9.1 fusion.111
  291.2 16.4 %fusion.115 = f32[1024,4096]{1,0:T(8,128)} fusion(bf16[1024,1024]{1,0:T(8,128)(2,1)} %fusion.53, bf16[1024,4096]{1,0:T(8,128)(2,1)} %all-gather.13.cloned.1.call-done), kind=kOutput, calls=%fused_computation.256 | convolution fusion | flops 8589934592 | bytes 27262976 | tf_op jit(solution)/shard_map/dot_general | solution.py:191
  307.6 19.1 %convolution_convert_fusion = bf16[4096,1024]{1,0:T(8,128)(2,1)} fusion(bf16[1024,1024]{1,0:T(8,128)(2,1)S(1)} %copy-done.17, f32[1024,6144]{1,0:T(8,128)} %copy-done.8, f32[1024,4096]{1,0:T(8,128)} %fusion.115), kind=kOutput, calls=%fused_computation.56 | convolution fusion | flops 8635023360 | bytes 31457280 | tf_op jit(solution)/shard_map/tf,td->fd/dot_general | solution.py:199
  326.6 36.6 %all-gather.15.cloned.1.call-done = bf16[4096,1024]{1,0:T(8,128)(2,1)} async-done(((bf16[128,1024]{1,0:T(8,128)(2,1)}), bf16[4096,1024]{1,0:T(8,128)(2,1)}) %all-gather.15.cloned.1.call-update) | async-done | bytes 8388624 | tf_op jit(solution)/shard_map/all_gather | solution.py:189
  363.2 25.1 %fusion.33 = bf16[1024,4096]{1,0:T(8,128)(2,1)} fusion(f32[1024,4096]{1,0:T(8,128)} %fusion.115, bf16[4096,1024]{1,0:T(8,128)(2,1)} %all-gather.15.cloned.1.call-done, bf16[1024,1024]{1,0:T(8,128)(2,1)S(1)} %copy-done.17, f32[1024,6144]{1,0:T(8,128)} %copy-done.8), kind=kOutput, calls=%fused_computation.50 | convolution fusion | flops 8676966400 | bytes 39845888 | tf_op jit(solution)/shard_map/td,fd->tf/dot_general | solution.py:201
  388.3 15.6 %convolution_convert_fusion.1 = bf16[1024,4096]{1,0:T(8,128)(2,1)} fusion(bf16[1024,1024]{1,0:T(8,128)(2,1)} %fusion.53, bf16[1024,4096]{1,0:T(8,128)(2,1)} %fusion.33), kind=kOutput, calls=%fused_computation.57 | convolution fusion | flops 8594128896 | bytes 18874368 | tf_op jit(solution)/shard_map/td,tf->df/dot_general | solution.py:204
  403.9 13.9 %multiply_reduce_fusion.3 = (f32[1024]{0:T(1024)S(1)}, f32[1024,1024]{1,0:T(8,128)}) fusion(f32[1024,1024]{1,0:T(8,128)S(1)} %copy-done.11, f32[1024]{0:T(1024)S(1)} %broadcast_multiply_fusion, f32[1024,6144]{1,0:T(8,128)} %copy-done.8, bf16[1024,4096]{1,0:T(8,128)(2,1)S(1)} %copy-done.81, bf16[1024,4096]{1,0:T(8,128)(2,1)} %all-gather.13.cloned.1.call-done), kind=kOutput, calls=%fused_computation.116 | convolution fusion | flops 8595176448 | bytes 29368320 | tf_op jit(solution)/shard_map/tf,df->td/dot_general | solution.py:205
  417.8 25.4 %fusion.110 = (f32[1024]{0:T(1024)S(1)}, f32[1024,1024]{1,0:T(8,128)}, bf16[1024,1024]{1,0:T(8,128)(2,1)}, f32[1024,1024]{1,0:T(8,128)}) fusion(f32[1024]{0:T(1024)S(1)} %multiply_multiply_fusion.5, f32[1024,1024]{1,0:T(8,128)} %copy-done.10, f32[1024]{0:T(1024)S(1)} %broadcast_multiply_fusion, f32[1024]{0:T(1024)S(1)} %fusion.96, ...), kind=kOutput, calls=%fused_computation.250 | convolution fusion | flops 8639216640 | bytes 52445184 | tf_op jit(solution)/shard_map/dot_general | solution.py:193
  443.2 7.7 multiply_dynamic-update-slice_fusion.1
  458.4 296.6 %while.30 = (s32[]{:T(128)}, f32[1024,16,64]{0,2,1:T(8,128)}, f32[1024,16,64]{0,2,1:T(8,128)}, f32[2,512,16,64]{1,0,3,2:T(2,128)}, s32[2]{0:T(128)S(1)}, /*index...) while((s32[]{:T(128)}, f32[1024,16,64]{0,2,1:T(8,128)}, ...), condition=%wide.region_20.21_spmd.clone, body=%wide.region_18.20_spmd.clone.sunk | while | flops 5476705280 | bytes 384034176 | solution.py:251
  461.0 14.4 %fusion.179 = f32[16,512,1024]{2,1,0:T(8,128)} fusion(bf16[1024,16,64]{0,2,1:T(8,128)(2,1)S(1)} %get-tuple-element.539, bf16[1024,16,64]{0,2,1:T(8,128)(2,1)} %get-tuple-element.536, s32[]{:T(128)S(6)} %select_n.183), kind=kOutput, calls=%fused_computation.32.clone.1 | convolution fusion | flops 1073741824 | bytes 36700164 | tf_op jit(solution)/shard_map/while/body/eval_jaxpr/qhd,khd->hqk/dot_general | solution.py:226
  475.4 17.2 %bitcast_add_fusion.5 = f32[1024,16,64]{0,2,1:T(8,128)} fusion(f32[1024,16,64]{0,2,1:T(8,128)} %get-tuple-element.517, f32[16,512,1024]{2,1,0:T(8,128)} %fusion.179, f32[16,512]{1,0:T(8,128)S(1)} %dynamic-slice_bitcast_fusion.18, pred[512,1024]{1,0:T(8,128)(4,1)S(1)} %fusion.180, pred[]{:T(512)S(6)} %compare.20, ...), kind=kOutput, calls=%fused_computation.23.clone.1 | convolution fusion | flops 1101004800 | bytes 43548676 | tf_op jit(solution)/shard_map/while/body/eval_jaxpr/hqk,qhd->khd/dot_general | solution.py:242
  492.6 24.9 %multiply_reduce_fusion.7 = (f32[16,512]{1,0:T(8,128)S(1)}, f32[16,512,1024]{2,1,0:T(8,128)}) fusion(f32[16,512,1024]{2,1,0:T(8,128)} %fusion.179, f32[16,512]{1,0:T(8,128)S(1)} %dynamic-slice_bitcast_fusion.18, pred[512,1024]{1,0:T(8,128)(4,1)S(1)} %fusion.180, bf16[1024,16,64]{0,2,1:T(8,128)(2,1)S(1)} %copy-done.6, ...), kind=kOutput, calls=%fused_computation.16.clone.1 | convolution fusion | flops 1107288064 | bytes 70844416 | tf_op jit(solution)/shard_map/while/body/eval_jaxpr/qhd,khd->hqk/dot_general | solution.py:231
  517.5 27.8 %multiply_convert_fusion.8 = bf16[16,512,1024]{2,1,0:T(8,128)(2,1)} fusion(f32[16,512,1024]{2,1,0:T(8,128)} %get-tuple-element.458, f32[16,512,1024]{2,1,0:T(8,128)} %fusion.179, f32[16,512]{1,0:T(8,128)S(1)} %get-tuple-element.459, f32[16,512]{1,0:T(8,128)S(1)} %dynamic-slice_bitcast_fusion.18, pred[512,1024]{1,0:T(8,128)(4,1)S(1)} %fusion.180), kind=kLoop, calls=%fused_computation.15.clone.1 | loop fusion | flops 41943040 | bytes 84475904 | tf_op jit(solution)/shard_map/while/body/eval_jaxpr/convert_element_type | solution.py:235
  545.3 10.5 convolution_bitcast_fusion.2
  567.2 38.1 %dynamic_update_slice.19 = f32[2,512,16,64]{1,0,3,2:T(2,128)} dynamic-update-slice(f32[2,512,16,64]{1,0,3,2:T(2,128)} %get-tuple-element.518, f32[1,512,16,64]{1,0,3,2:T(1,128)} %copy.276, s32[]{:T(128)S(6)} %copy.295, s32[]{:T(128)} %constant.294.clone.1..sunk.1, s32[]{:T(128)} %constant.294.clone.1..sunk.1, s32[]{:T(128)} %constant.294.clone.1..sunk.1) | dynamic-update-slice | bytes 4194308 | tf_op jit(solution)/shard_map/while/body/jit(dynamic_update_index_in_dim)/dynamic_update_slice | solution.py:182
  607.8 14.4 %fusion.179 = f32[16,512,1024]{2,1,0:T(8,128)} fusion(bf16[1024,16,64]{0,2,1:T(8,128)(2,1)S(1)} %get-tuple-element.539, bf16[1024,16,64]{0,2,1:T(8,128)(2,1)} %get-tuple-element.536, s32[]{:T(128)S(6)} %select_n.183), kind=kOutput, calls=%fused_computation.32.clone.1 | convolution fusion | flops 1073741824 | bytes 36700164 | tf_op jit(solution)/shard_map/while/body/eval_jaxpr/qhd,khd->hqk/dot_general | solution.py:226
  622.2 18.3 %bitcast_add_fusion.5 = f32[1024,16,64]{0,2,1:T(8,128)} fusion(f32[1024,16,64]{0,2,1:T(8,128)} %get-tuple-element.517, f32[16,512,1024]{2,1,0:T(8,128)} %fusion.179, f32[16,512]{1,0:T(8,128)S(1)} %dynamic-slice_bitcast_fusion.18, pred[512,1024]{1,0:T(8,128)(4,1)S(1)} %fusion.180, pred[]{:T(512)S(6)} %compare.20, ...), kind=kOutput, calls=%fused_computation.23.clone.1 | convolution fusion | flops 1101004800 | bytes 43548676 | tf_op jit(solution)/shard_map/while/body/eval_jaxpr/hqk,qhd->khd/dot_general | solution.py:242
  640.6 24.9 %multiply_reduce_fusion.7 = (f32[16,512]{1,0:T(8,128)S(1)}, f32[16,512,1024]{2,1,0:T(8,128)}) fusion(f32[16,512,1024]{2,1,0:T(8,128)} %fusion.179, f32[16,512]{1,0:T(8,128)S(1)} %dynamic-slice_bitcast_fusion.18, pred[512,1024]{1,0:T(8,128)(4,1)S(1)} %fusion.180, bf16[1024,16,64]{0,2,1:T(8,128)(2,1)S(1)} %copy-done.6, ...), kind=kOutput, calls=%fused_computation.16.clone.1 | convolution fusion | flops 1107288064 | bytes 70844416 | tf_op jit(solution)/shard_map/while/body/eval_jaxpr/qhd,khd->hqk/dot_general | solution.py:231
  665.4 27.8 %multiply_convert_fusion.8 = bf16[16,512,1024]{2,1,0:T(8,128)(2,1)} fusion(f32[16,512,1024]{2,1,0:T(8,128)} %get-tuple-element.458, f32[16,512,1024]{2,1,0:T(8,128)} %fusion.179, f32[16,512]{1,0:T(8,128)S(1)} %get-tuple-element.459, f32[16,512]{1,0:T(8,128)S(1)} %dynamic-slice_bitcast_fusion.18, pred[512,1024]{1,0:T(8,128)(4,1)S(1)} %fusion.180), kind=kLoop, calls=%fused_computation.15.clone.1 | loop fusion | flops 41943040 | bytes 84475904 | tf_op jit(solution)/shard_map/while/body/eval_jaxpr/convert_element_type | solution.py:235
  693.3 10.5 convolution_bitcast_fusion.2
  705.2 7.8 bitcast_add_fusion.4
  716.5 38.1 %dynamic_update_slice.19 = f32[2,512,16,64]{1,0,3,2:T(2,128)} dynamic-update-slice(f32[2,512,16,64]{1,0,3,2:T(2,128)} %get-tuple-element.518, f32[1,512,16,64]{1,0,3,2:T(1,128)} %copy.276, s32[]{:T(128)S(6)} %copy.295, s32[]{:T(128)} %constant.294.clone.1..sunk.1, s32[]{:T(128)} %constant.294.clone.1..sunk.1, s32[]{:T(128)} %constant.294.clone.1..sunk.1) | dynamic-update-slice | bytes 4194308 | tf_op jit(solution)/shard_map/while/body/jit(dynamic_update_index_in_dim)/dynamic_update_slice | solution.py:182
  768.3 7.9 constant_dynamic-slice_fusion.3
  819.1 8.8 convolution_convert_fusion.3
  830.8 14.4 %fusion.46 = (f32[1024,6144]{1,0:T(8,128)}, f32[1024]{0:T(1024)S(1)}, f32[1024,1024]{1,0:T(8,128)S(1)}) fusion(f32[1024,6144]{1,0:T(8,128)} %fusion.50, bf16[1024,1024]{1,0:T(8,128)(2,1)S(1)} %copy-done.14, f32[1024]{0:T(1024)S(1)} %copy-done.62, f32[1024]{0:T(1024)S(1)} %copy-done.58, f32[1024,6144]{1,0:T(8,128)} %copy-done.8, ...), kind=kOutput, calls=%fused_computation.82 | convolution fusion | flops 6450838528 | bytes 27275264 | tf_op jit(solution)/shard_map/tc,dc->td/dot_general | solution.py:267
  853.2 12.9 %fusion.36 = bf16[1,6,6144]{2,1,0:T(8,128)(2,1)} fusion(f32[1024,6144]{1,0:T(8,128)} %constant_dynamic-update-slice_fusion, s32[6]{0:T(128)S(1)} %bitcast.298, s32[6]{0:T(128)S(1)} %copy-done.71), kind=kOutput, calls=%fused_computation.59 | convolution fusion | flops 453040128 | bytes 25239600 | tf_op jit(solution)/shard_map/ti,tc->ic/dot_general | solution.py:276
  880.2 11.3 %collective-permute-done.6 = bf16[2,2,2,32,1024]{4,3,0,1,2:T(8,128)(2,1)S(1)} collective-permute-done((bf16[2,2,2,32,1024]{4,3,0,1,2:T(8,128)(2,1)S(1)}, bf16[2,2,2,32,1024]{4,3,0,1,2:T(8,128)(2,1)S(1)}, u32[]{:S(2)}, u32[]{:S(2)}) %collective-permute-start.6) | collective-permute-done | bytes 524320 | tf_op jit(solution)/shard_map/ppermute | solution.py:22
  939.0 8.8 all-to-all-start.2
  961.1 14.3 %all-to-all-done.2 = f32[32,1,1280]{2,1,0:T(1,128)S(1)} async-done(((f32[32,1,1280]{2,1,0:T(1,128)}), f32[32,1,1280]{2,1,0:T(1,128)S(1)}, u32[]{:S(2)}, u32[]{:S(2)}) %all-to-all-start.2) | async-done | bytes 163872 | tf_op jit(solution)/shard_map/all_to_all | solution.py:302
  979.1 10.2 collective-permute-done.2
  996.1 8.7 collective-permute-done.3
  1010.8 14.8 %collective-permute-done.12 = bf16[2,2,32,4096]{3,2,0,1:T(8,128)(2,1)S(1)} collective-permute-done((bf16[2,2,32,4096]{3,2,0,1:T(8,128)(2,1)S(1)}, bf16[2,2,32,4096]{3,2,0,1:T(8,128)(2,1)S(1)}, u32[]{:S(2)}, u32[]{:S(2)}) %collective-permute-start.12) | collective-permute-done | bytes 1048608 | tf_op jit(solution)/shard_map/ppermute | solution.py:22
  1028.0 8.2 collective-permute-done.13
  1041.9 12.6 %collective-permute-done.14 = bf16[32,4096]{1,0:T(8,128)(2,1)S(1)} collective-permute-done((bf16[32,4096]{1,0:T(8,128)(2,1)S(1)}, bf16[32,4096]{1,0:T(8,128)(2,1)S(1)}, u32[]{:S(2)}, u32[]{:S(2)}) %collective-permute-start.14) | collective-permute-done | bytes 262176 | tf_op jit(solution)/shard_map/ppermute | solution.py:22
  (399 shorter events, 263.2 us)
Async XLA Ops:
  7.2 68.0 %all-gather.17.cloned.1.call-start = ((), (), s32[]{:S(2)}) async-start(), calls=%async_computation.7 | async-start | bytes 3244032 | tf_op jit(solution)/shard_map/all_gather | solution.py:131
  8.3 15.8 %copy-start.78 = (s32[9]{0:T(128)S(1)}, s32[9]{0:T(128)}, u32[]{:S(2)}) copy-start(s32[9]{0:T(128)} %constant.318.clone) | copy-start | bytes 112
  9.8 138.1 %all-gather.9.cloned.1.call-start = ((), (), s32[]{:S(2)}) async-start(), calls=%async_computation.3 | async-start | bytes 6488064 | tf_op jit(solution)/shard_map/all_gather | solution.py:136
  10.5 264.6 %all-gather.11.cloned.1.call-start = ((), (), s32[]{:S(2)}) async-start(), calls=%async_computation.4 | async-start | bytes 2162688 | tf_op jit(solution)/shard_map/all_gather | solution.py:137
  11.3 279.9 %all-gather.13.cloned.1.call-start = ((), (), s32[]{:S(2)}) async-start(), calls=%async_computation.5 | async-start | bytes 8650752 | tf_op jit(solution)/shard_map/all_gather | solution.py:188
  14.6 68.1 %all-to-all-start = ((bf16[32,32,192]{2,0,1:T(8,128)(2,1)}), bf16[32,32,192]{2,0,1:T(8,128)(2,1)S(1)}, u32[]{:S(2)}, u32[]{:S(2)}) async-start(bf16[32,32,192]{2,0,1:T(8,128)(2,1)} %copy.186), calls=%async_computation | async-start | bytes 1048576 | tf_op jit(solution)/shard_map/all_to_all | solution.py:146
  21.9 341.3 %all-gather.15.cloned.1.call-start = ((), (), s32[]{:S(2)}) async-start(), calls=%async_computation.6 | async-start | bytes 8650752 | tf_op jit(solution)/shard_map/all_gather | solution.py:189
  22.9 52.3 %copy-start.72 = (s32[6,1]{0,1:T(1,128)}, s32[6,1]{0,1:T(1,128)S(1)}, u32[]{:S(2)}) copy-start(s32[6,1]{0,1:T(1,128)S(1)} %reduce-window.7) | copy-start | bytes 76
  23.3 89.1 %copy-start.57 = (f32[1024]{0:T(1024)}, f32[1024]{0:T(1024)S(1)}, u32[]{:S(2)}) copy-start(f32[1024]{0:T(1024)S(1)} %broadcast_multiply_fusion.1) | copy-start | bytes 12292
  24.0 63.6 %copy-start.65 = (f32[1024]{0:T(1024)}, f32[1024]{0:T(1024)S(1)}, u32[]{:S(2)}) copy-start(f32[1024]{0:T(1024)S(1)} %fusion.47) | copy-start | bytes 12292
  82.5 29.9 %copy-start.54 = (bf16[192,1024]{1,0:T(8,128)(2,1)}, bf16[192,1024]{1,0:T(8,128)(2,1)S(1)}, u32[]{:S(2)}) copy-start(bf16[192,1024]{1,0:T(8,128)(2,1)S(1)} %get-tuple-element.307) | copy-start | bytes 1179652
  83.9 17.0 %all-to-all-start.1 = ((f32[32,6,192]{2,1,0:T(8,128)}), f32[32,6,192]{2,1,0:T(8,128)S(1)}, u32[]{:S(2)}, u32[]{:S(2)}) async-start(f32[32,6,192]{2,1,0:T(8,128)} %copy.189), calls=%async_computation.1 | async-start | bytes 524288 | tf_op jit(solution)/shard_map/all_to_all | solution.py:148
  87.3 845.4 %all-gather.19.cloned.1.call-start = ((), (), s32[]{:S(2)}) async-start(), calls=%async_computation.8 | async-start | bytes 3244032 | tf_op jit(solution)/shard_map/all_gather | solution.py:279
  87.6 24.8 %copy-start.61 = (f32[1024]{0:T(1024)}, f32[1024]{0:T(1024)S(1)}, u32[]{:S(2)}) copy-start(f32[1024]{0:T(1024)S(1)} %fusion.95) | copy-start | bytes 12292
  284.2 133.6 %copy-start.59 = (f32[1024]{0:T(1024)}, f32[1024]{0:T(1024)S(1)}, u32[]{:S(2)}) copy-start(f32[1024]{0:T(1024)S(1)} %broadcast_multiply_fusion) | copy-start | bytes 12292
  286.2 131.6 %copy-start.63 = (f32[1024]{0:T(1024)}, f32[1024]{0:T(1024)S(1)}, u32[]{:S(2)}) copy-start(f32[1024]{0:T(1024)S(1)} %fusion.96) | copy-start | bytes 12292
  291.2 16.4 %copy-start.17 = (bf16[1024,1024]{1,0:T(8,128)(2,1)S(1)}, bf16[1024,1024]{1,0:T(8,128)(2,1)}, u32[]{:S(2)}) copy-start(bf16[1024,1024]{1,0:T(8,128)(2,1)} %param.31) | copy-start | bytes 6291460
  475.4 17.2 %copy-start.6 = (bf16[1024,16,64]{0,2,1:T(8,128)(2,1)S(1)}, bf16[1024,16,64]{0,2,1:T(8,128)(2,1)}, u32[]{:S(2)}) copy-start(bf16[1024,16,64]{0,2,1:T(8,128)(2,1)} %get-tuple-element.542) | copy-start | bytes 6291460 | tf_op jit(solution)/shard_map/while
  563.7 41.6 %copy-start.3 = (bf16[1024,16,64]{0,2,1:T(8,128)(2,1)S(1)}, bf16[1024,16,64]{0,2,1:T(8,128)(2,1)}, u32[]{:S(2)}) copy-start(bf16[1024,16,64]{0,2,1:T(8,128)(2,1)} %get-tuple-element.570) | copy-start | bytes 6291460 | tf_op jit(solution)/shard_map/while
  622.2 18.4 %copy-start.6 = (bf16[1024,16,64]{0,2,1:T(8,128)(2,1)S(1)}, bf16[1024,16,64]{0,2,1:T(8,128)(2,1)}, u32[]{:S(2)}) copy-start(bf16[1024,16,64]{0,2,1:T(8,128)(2,1)} %get-tuple-element.542) | copy-start | bytes 6291460 | tf_op jit(solution)/shard_map/while
  713.0 41.6 %copy-start.3 = (bf16[1024,16,64]{0,2,1:T(8,128)(2,1)S(1)}, bf16[1024,16,64]{0,2,1:T(8,128)(2,1)}, u32[]{:S(2)}) copy-start(bf16[1024,16,64]{0,2,1:T(8,128)(2,1)} %get-tuple-element.570) | copy-start | bytes 6291460 | tf_op jit(solution)/shard_map/while
  776.1 18.9 %slice-start = ((s8[12582912]{0:T(1024)(128)(4,1)}), s8[4194304]{0:T(1024)(128)(4,1)S(1)}, s32[]{:S(2)}) async-start(s8[12582912]{0:T(1024)(128)(4,1)} %bitcast.275), calls=%async_computation.9 | async-start | bytes 8388608
  776.1 18.9 %slice-start.1 = ((s8[12582912]{0:T(1024)(128)(4,1)}), s8[4194304]{0:T(1024)(128)(4,1)S(1)}, s32[]{:S(2)}) async-start(s8[12582912]{0:T(1024)(128)(4,1)} %bitcast.275), calls=%async_computation.10 | async-start | bytes 8388608
  789.0 128.0 %collective-permute-start.10 = (bf16[2,2,2,2,32,4096]{5,4,0,3,1,2:T(8,128)(2,1)}, bf16[2,2,2,2,32,4096]{5,4,0,3,1,2:T(8,128)(2,1)}, u32[]{:S(2)}, u32[]{:S(2)}) collective-permute-start(bf16[2,2,2,2,32,4096]{5,4,0,3,1,2:T(8,128)(2,1)} %bitcast.238), channel_id=1, source_target_pairs={{0,1},{1,0},{2,3},{3,2},{4,5},{5,4},{6,7},{7,6},{8,9},{9,8},{10,11... | collective-permute-start | bytes 12582920 | tf_op jit(solution)/shard_map/ppermute | solution.py:22
  789.3 137.0 %collective-permute-start.15 = (bf16[2,2,2,2,128,1024]{5,4,0,1,2,3:T(8,128)(2,1)}, bf16[2,2,2,2,128,1024]{5,4,0,1,2,3:T(8,128)(2,1)}, u32[]{:S(2)}, u32[]{:S(2)}) collective-permute-start(bf16[2,2,2,2,128,1024]{5,4,0,1,2,3:T(8,128)(2,1)} %bitcast.237), channel_id=1, source_target_pairs={{0,1},{1,0},{2,3},{3,2},{4,5},{5,4},{6,7},{7,6},{8,9},{9,8},{10,11... | collective-permute-start | bytes 12582920 | tf_op jit(solution)/shard_map/ppermute | solution.py:22
  794.7 78.8 %collective-permute-start.5 = (bf16[2,2,2,2,32,1024]{5,4,0,2,3,1:T(8,128)(2,1)}, bf16[2,2,2,2,32,1024]{5,4,0,2,3,1:T(8,128)(2,1)}, u32[]{:S(2)}, u32[]{:S(2)}) collective-permute-start(bf16[2,2,2,2,32,1024]{5,4,0,2,3,1:T(8,128)(2,1)} %bitcast.240), channel_id=1, source_target_pairs={{0,1},{1,0},{2,3},{3,2},{4,5},{5,4},{6,7},{7,6},{8,9},{9,8},{10,11... | collective-permute-start | bytes 3145736 | tf_op jit(solution)/shard_map/ppermute | solution.py:22
  873.3 38.9 %collective-permute-start = (bf16[2,2,2,2,32,3072]{5,4,0,1,2,3:T(8,128)(2,1)}, bf16[2,2,2,2,32,3072]{5,4,0,1,2,3:T(8,128)(2,1)}, u32[]{:S(2)}, u32[]{:S(2)}) collective-permute-start(bf16[2,2,2,2,32,3072]{5,4,0,1,2,3:T(8,128)(2,1)} %bitcast.239), channel_id=1, source_target_pairs={{0,1},{1,0},{2,3},{3,2},{4,5},{5,4},{6,7},{7,6},{8,9},{9,8},{10,11... | collective-permute-start | bytes 9437192 | tf_op jit(solution)/shard_map/ppermute | solution.py:22
  876.0 17.3 %copy-start.29 = (f32[1024,1024]{1,0:T(8,128)S(1)}, f32[1024,1024]{1,0:T(8,128)}, u32[]{:S(2)}) copy-start(f32[1024,1024]{1,0:T(8,128)} %copy-done.28) | copy-start | bytes 12582916
  876.0 15.6 %collective-permute-start.6 = (bf16[2,2,2,32,1024]{4,3,0,1,2:T(8,128)(2,1)S(1)}, bf16[2,2,2,32,1024]{4,3,0,1,2:T(8,128)(2,1)S(1)}, u32[]{:S(2)}, u32[]{:S(2)}) collective-permute-start(bf16[2,2,2,32,1024]{4,3,0,1,2:T(8,128)(2,1)S(1)} %dynamic-slice_bitcast_fusion.9), channel_id=1, source_target_pairs={{0,8},{2,10},{4,12},{6,14},{8,0},{10,2},{12,4},{14,6},{16,24},{18,... | collective-permute-start | bytes 1572872 | tf_op jit(solution)/shard_map/ppermute | solution.py:22
  891.8 16.8 %copy-start.19 = (bf16[1024,1024]{1,0:T(8,128)(2,1)S(1)}, bf16[1024,1024]{1,0:T(8,128)(2,1)}, u32[]{:S(2)}) copy-start(bf16[1024,1024]{1,0:T(8,128)(2,1)} %param.31) | copy-start | bytes 6291460
  891.8 16.8 %copy-start.68 = (f32[1024]{0:T(1024)S(1)}, f32[1024]{0:T(1024)}, u32[]{:S(2)}) copy-start(f32[1024]{0:T(1024)} %copy-done.67) | copy-start | bytes 12292
  891.9 9.0 collective-permute-start.7
  901.0 5.1 collective-permute-start.8
  906.2 5.3 collective-permute-start.9
  916.8 34.9 %collective-permute-start.1 = (bf16[2,2,2,32,3072]{4,3,0,1,2:T(8,128)(2,1)}, bf16[2,2,2,32,3072]{4,3,0,1,2:T(8,128)(2,1)}, u32[]{:S(2)}, u32[]{:S(2)}) collective-permute-start(bf16[2,2,2,32,3072]{4,3,0,1,2:T(8,128)(2,1)} %dynamic-slice_bitcast_fusion.3), channel_id=1, source_target_pairs={{0,2},{2,0},{4,6},{6,4},{8,10},{10,8},{12,14},{14,12},{16,18},{18,... | collective-permute-start | bytes 4718600 | tf_op jit(solution)/shard_map/ppermute | solution.py:22
  924.9 67.5 %collective-permute-start.11 = (bf16[2,2,2,32,4096]{4,3,0,2,1:T(8,128)(2,1)}, bf16[2,2,2,32,4096]{4,3,0,2,1:T(8,128)(2,1)}, u32[]{:S(2)}, u32[]{:S(2)}) collective-permute-start(bf16[2,2,2,32,4096]{4,3,0,2,1:T(8,128)(2,1)} %dynamic-slice_bitcast_fusion.2), channel_id=1, source_target_pairs={{0,4},{2,6},{4,0},{6,2},{8,12},{10,14},{12,8},{14,10},{16,20},{18,... | collective-permute-start | bytes 6291464 | tf_op jit(solution)/shard_map/ppermute | solution.py:22
  939.0 36.4 %all-to-all-start.2 = ((f32[32,1,1280]{2,1,0:T(1,128)}), f32[32,1,1280]{2,1,0:T(1,128)S(1)}, u32[]{:S(2)}, u32[]{:S(2)}) async-start(f32[32,1,1280]{2,1,0:T(1,128)} %reshape.577), calls=%async_computation.2 | async-start | bytes 327680 | tf_op jit(solution)/shard_map/all_to_all | solution.py:302
  955.2 34.1 %collective-permute-start.2 = (bf16[2,2,32,3072]{3,2,0,1:T(8,128)(2,1)}, bf16[2,2,32,3072]{3,2,0,1:T(8,128)(2,1)S(1)}, u32[]{:S(2)}, u32[]{:S(2)}) collective-permute-start(bf16[2,2,32,3072]{3,2,0,1:T(8,128)(2,1)} %dynamic-slice_bitcast_fusion.6), channel_id=1, source_target_pairs={{0,4},{2,6},{4,0},{6,2},{8,12},{10,14},{12,8},{14,10},{16,20},{18,... | collective-permute-start | bytes 2359304 | tf_op jit(solution)/shard_map/ppermute | solution.py:22
  958.2 48.4 %collective-permute-start.16 = (bf16[2,2,2,128,1024]{4,3,0,1,2:T(8,128)(2,1)}, bf16[2,2,2,128,1024]{4,3,0,1,2:T(8,128)(2,1)}, u32[]{:S(2)}, u32[]{:S(2)}) collective-permute-start(bf16[2,2,2,128,1024]{4,3,0,1,2:T(8,128)(2,1)} %dynamic-slice_bitcast_fusion.1), channel_id=1, source_target_pairs={{0,2},{2,0},{4,6},{6,4},{8,10},{10,8},{12,14},{14,12},{16,18},{18,... | collective-permute-start | bytes 6291464 | tf_op jit(solution)/shard_map/ppermute | solution.py:22
  990.6 16.0 %copy-start.21 = (bf16[2,2,2,2,128,1024]{5,4,0,1,2,3:T(8,128)(2,1)S(1)}, bf16[2,2,2,2,128,1024]{5,4,0,1,2,3:T(8,128)(2,1)}, u32[]{:S(2)}) copy-start(bf16[2,2,2,2,128,1024]{5,4,0,1,2,3:T(8,128)(2,1)} %fusion.34) | copy-start | bytes 12582916
  990.6 14.2 %collective-permute-start.3 = (bf16[2,32,3072]{2,1,0:T(8,128)(2,1)S(1)}, bf16[2,32,3072]{2,1,0:T(8,128)(2,1)S(1)}, u32[]{:S(2)}, u32[]{:S(2)}) collective-permute-start(bf16[2,32,3072]{2,1,0:T(8,128)(2,1)S(1)} %dynamic-slice_bitcast_fusion.10), channel_id=1, source_target_pairs={{0,8},{2,10},{4,12},{6,14},{8,0},{10,2},{12,4},{14,6},{16,24},{18,... | collective-permute-start | bytes 1179656 | tf_op jit(solution)/shard_map/ppermute | solution.py:22
  995.5 30.2 %collective-permute-start.12 = (bf16[2,2,32,4096]{3,2,0,1:T(8,128)(2,1)S(1)}, bf16[2,2,32,4096]{3,2,0,1:T(8,128)(2,1)S(1)}, u32[]{:S(2)}, u32[]{:S(2)}) collective-permute-start(bf16[2,2,32,4096]{3,2,0,1:T(8,128)(2,1)S(1)} %dynamic-slice_bitcast_fusion.5), channel_id=1, source_target_pairs={{0,8},{2,10},{4,12},{6,14},{8,0},{10,2},{12,4},{14,6},{16,24},{18,... | collective-permute-start | bytes 3145736 | tf_op jit(solution)/shard_map/ppermute | solution.py:22
  1005.0 21.7 %collective-permute-start.4 = (bf16[32,3072]{1,0:T(8,128)(2,1)S(1)}, bf16[32,3072]{1,0:T(8,128)(2,1)S(1)}, u32[]{:S(2)}, u32[]{:S(2)}) collective-permute-start(bf16[32,3072]{1,0:T(8,128)(2,1)S(1)} %dynamic-slice_bitcast_fusion.14), channel_id=1, source_target_pairs={{0,16},{2,18},{4,20},{6,22},{8,24},{10,26},{12,28},{14,30},{16,0},... | collective-permute-start | bytes 589832 | tf_op jit(solution)/shard_map/ppermute | solution.py:22
  1009.3 18.2 %collective-permute-start.17 = (bf16[2,2,128,1024]{3,2,0,1:T(8,128)(2,1)S(1)}, bf16[2,2,128,1024]{3,2,0,1:T(8,128)(2,1)S(1)}, u32[]{:S(2)}, u32[]{:S(2)}) collective-permute-start(bf16[2,2,128,1024]{3,2,0,1:T(8,128)(2,1)S(1)} %dynamic-slice_bitcast_fusion.4), channel_id=1, source_target_pairs={{0,4},{2,6},{4,0},{6,2},{8,12},{10,14},{12,8},{14,10},{16,20},{18,... | collective-permute-start | bytes 3145736 | tf_op jit(solution)/shard_map/ppermute | solution.py:22
  1026.0 10.2 collective-permute-start.13
  1027.9 11.9 %collective-permute-start.18 = (bf16[2,128,1024]{2,1,0:T(8,128)(2,1)S(1)}, bf16[2,128,1024]{2,1,0:T(8,128)(2,1)S(1)}, u32[]{:S(2)}, u32[]{:S(2)}) collective-permute-start(bf16[2,128,1024]{2,1,0:T(8,128)(2,1)S(1)} %dynamic-slice_bitcast_fusion.7), channel_id=1, source_target_pairs={{0,8},{2,10},{4,12},{6,14},{8,0},{10,2},{12,4},{14,6},{16,24},{18,... | collective-permute-start | bytes 1572872 | tf_op jit(solution)/shard_map/ppermute | solution.py:22
  1036.3 18.1 %collective-permute-start.14 = (bf16[32,4096]{1,0:T(8,128)(2,1)S(1)}, bf16[32,4096]{1,0:T(8,128)(2,1)S(1)}, u32[]{:S(2)}, u32[]{:S(2)}) collective-permute-start(bf16[32,4096]{1,0:T(8,128)(2,1)S(1)} %dynamic-slice_bitcast_fusion.12), channel_id=1, source_target_pairs={{0,16},{2,18},{4,20},{6,22},{8,24},{10,26},{12,28},{14,30},{16,0},... | collective-permute-start | bytes 786440 | tf_op jit(solution)/shard_map/ppermute | solution.py:22
  1040.1 17.2 %collective-permute-start.19 = (bf16[128,1024]{1,0:T(8,128)(2,1)S(1)}, bf16[128,1024]{1,0:T(8,128)(2,1)S(1)}, u32[]{:S(2)}, u32[]{:S(2)}) collective-permute-start(bf16[128,1024]{1,0:T(8,128)(2,1)S(1)} %dynamic-slice_bitcast_fusion.11), channel_id=1, source_target_pairs={{0,16},{2,18},{4,20},{6,22},{8,24},{10,26},{12,28},{14,30},{16,0},... | collective-permute-start | bytes 786440 | tf_op jit(solution)/shard_map/ppermute | solution.py:22
  (73 other events, 507.1 us)
Sparse Core Ops, SparseCore 0:
  11.5 63.6 all-gather.16
  78.1 69.7 all-gather.8
  150.7 54.8 all-gather.10
  208.3 76.0 all-gather.12
  287.1 76.0 all-gather.14
  866.2 59.4 all-gather.18

commit v2 on v1

v2 whole, which is shorter than its diff:
```python
import functools
import jax
import jax.numpy as jnp
import numpy as np
from jax import lax
from jax.experimental import pallas as pl
from jax.experimental.pallas import tpu as pltpu
from jax.sharding import PartitionSpec as P

NORM_EPS = 1e-06
BF, F32 = jnp.bfloat16, jnp.float32
VMEM_BYTES = 56 * 2**20
HEAD = 64
PAIR = 2 * HEAD
GROUP = 4
GELU_A, GELU_B = 0.7978845608028654, 0.044715


def nn(a, b):
    return lax.dot_general(a, b, (((1,), (0,)), ((), ())), preferred_element_type=F32)


def nt(a, b):
    return lax.dot_general(a, b, (((1,), (1,)), ((), ())), preferred_element_type=F32)


def tn(a, b):
    return lax.dot_general(a, b, (((0,), (0,)), ((), ())), preferred_element_type=F32)


def halves(x):
    high = x.astype(BF)
    return high, (x - high.astype(F32)).astype(BF)


def params(steps=1):
    return pltpu.CompilerParams(
        vmem_limit_bytes=VMEM_BYTES, dimension_semantics=("arbitrary",) * steps
    )


def cost(flops, size, exps=0):
    return pl.CostEstimate(flops=int(flops), bytes_accessed=int(size), transcendentals=int(exps))


def head_ones(dtype=BF):
    row = lax.broadcasted_iota(jnp.int32, (PAIR, PAIR), 0) // HEAD
    column = lax.broadcasted_iota(jnp.int32, (PAIR, PAIR), 1) // HEAD
    return (row == column).astype(F32).astype(dtype)


def head_sums(x):
    ones = head_ones()
    parts = []
    for at in range(0, x.shape[1], PAIR):
        high, low = halves(x[:, at : at + PAIR])
        parts.append(nn(high, ones) + nn(low, ones))
    return parts[0] if len(parts) == 1 else jnp.concatenate(parts, axis=1)


def centre(x):
    mean = jnp.mean(x, axis=-1, keepdims=True)
    centred = x - mean
    rstd = lax.rsqrt(jnp.mean(centred * centred, axis=-1, keepdims=True) + NORM_EPS)
    return centred * rstd, rstd


def qkv_kernel(places, tokens, member, modulation, *refs, pieces):
    weights, (scale, hidden, q, k, v, rq, rk, ordered) = refs[: 3 * pieces], refs[3 * pieces :]
    step = pl.program_id(0)
    width = tokens.shape[1]
    block = ordered.shape[1]
    per = width // block
    rows = 256

    @pl.when(step == 0)
    def _():
        for at in range(0, tokens.shape[0], rows):
            here = pl.ds(at, rows)
            unit, _ = centre(tokens[here, :].astype(F32))
            sc = nn(member[here, :], modulation[:, 2 * width : 3 * width])
            sh = nn(member[here, :], modulation[:, 4 * width : 5 * width])
            hidden[here, :] = (unit * (1.0 + sc) + sh).astype(BF)

    for which in range(3):

        @pl.when((step >= which * per) & (step < (which + 1) * per))
        def _():
            if pieces == 1:
                ordered[...] = weights[which][...]
            else:
                own, other = weights[2 * which : 2 * which + 2]
                owners = places.shape[1]
                size = width // owners
                for owner in range(owners):
                    place = places[which, owner]
                    at = pl.multiple_of((place // 2) * size, size)
                    put = slice(owner * size, (owner + 1) * size)

                    @pl.when(place % 2 == 0)
                    def _():
                        ordered[put, :] = own[pl.ds(at, size), :]

                    @pl.when(place % 2 == 1)
                    def _():
                        ordered[put, :] = other[pl.ds(at, size), :]

            for at in range(0, tokens.shape[0], rows):
                here = pl.ds(at, rows)
                out = nn(hidden[here, :], ordered[...])
                if which == 0:
                    r = lax.rsqrt(head_sums(out * out) + NORM_EPS)
                    rq[here, :] = r.astype(BF)
                    q[here, :] = (out * r * scale[0:1, :]).astype(BF)
                if which == 1:
                    r = lax.rsqrt(head_sums(out * out) + NORM_EPS)
                    rk[here, :] = r.astype(BF)
                    k[here, :] = (out * r).astype(BF)
                if which == 2:
                    v[here, :] = out.astype(BF)


def qkv_call(places, tokens, member, modulation, weights, scale_lanes, block=512):
    count, width = tokens.shape
    per = width // block
    pieces = len(weights[0])
    part = lambda rows, which: pl.BlockSpec(
        (rows, block), lambda s, p: (0, jnp.clip(s - which * per, 0, per - 1))
    )
    whole = lambda x: pl.BlockSpec(x.shape, lambda s, p: (0, 0))
    columns = [part(count, i) for i in range(3)]
    return pl.pallas_call(
        functools.partial(qkv_kernel, pieces=pieces),
        grid_spec=pltpu.PrefetchScalarGridSpec(
            num_scalar_prefetch=1,
            grid=(3 * per,),
            in_specs=[whole(tokens), whole(member), whole(modulation)]
            + [part(w.shape[0], i) for i in range(3) for w in weights[i]]
            + [part(8, 0)],
            out_specs=[pl.BlockSpec((count, width), lambda s, p: (0, 0))]
            + columns
            + columns[:2]
            + [pl.BlockSpec((width, block), lambda s, p: (0, s))],
        ),
        out_shape=[jax.ShapeDtypeStruct((count, width), BF)] * 6
        + [jax.ShapeDtypeStruct((width, 3 * width), BF)],
        compiler_params=params(),
        cost_estimate=cost(6 * count * width * width, 2 * (13 * count * width)),
        name="qkv_forward",
    )(places, tokens, member, modulation, *[w for ws in weights for w in ws], scale_lanes)


def lane_masked(x, which):
    lane = lax.broadcasted_iota(jnp.int32, x.shape, 1) // HEAD
    return jnp.where(lane == which, x, jnp.zeros_like(x))


def attn_fwd_kernel(span, q, k, v, start, end, mixed, rest, inverse, v_ext, qm, *, qb, kb):
    count = q.shape[0]
    pairs = q.shape[1] // PAIR
    for pair in range(pairs):
        lanes = slice(pair * PAIR, (pair + 1) * PAIR)
        for h in range(2):
            vv = v[:, lanes]
            lane = lax.broadcasted_iota(jnp.int32, vv.shape, 1) // HEAD
            v_ext[2 * pair + h] = jnp.where(lane == h, vv, jnp.ones_like(vv))
            qm[2 * pair + h] = lane_masked(q[:, lanes], h)

    def one_block(i, _):
        first = pl.multiple_of(i * qb, qb)
        here = pl.ds(first, qb)
        low, high = start[here, :], end[here, :]

        def step(j, totals):
            at = pl.multiple_of(j * kb, kb)
            there = pl.ds(at, kb)
            place = at + lax.broadcasted_iota(jnp.int32, (qb, kb), 1)
            seen = (place >= low) & (place < high)
            out = []
            for h in range(2 * pairs):
                pair = h // 2
                s = nt(qm[h, here, :], k[there, pair * PAIR : (pair + 1) * PAIR])
                p = jnp.where(seen, jnp.exp(s), 0.0).astype(BF)
                out.append(totals[h] + nn(p, v_ext[h, there, :]))
            return tuple(out)

        totals = lax.fori_loop(
            span[0, i], span[1, i], step, tuple(jnp.zeros((qb, PAIR), F32) for _ in range(2 * pairs))
        )
        for pair in range(pairs):
            t0, t1 = totals[2 * pair], totals[2 * pair + 1]
            lane = lax.broadcasted_iota(jnp.int32, t0.shape, 1) // HEAD
            top = jnp.where(lane == 0, t0, t1)
            sums = pltpu.roll(jnp.where(lane == 0, t1, t0), HEAD, 1)
            inv = 1.0 / sums
            high_part, low_part = halves(top * inv)
            mixed[here, pair * PAIR : (pair + 1) * PAIR] = high_part
            rest[here, pair * PAIR : (pair + 1) * PAIR] = low_part
            turned = jnp.transpose(inv)
            inverse[0, 2 * pair : 2 * pair + 1, here] = turned[0:1, :]
            inverse[0, 2 * pair + 1 : 2 * pair + 2, here] = turned[HEAD : HEAD + 1, :]
        return 0

    lax.fori_loop(0, count // qb, one_block, 0)


def attn_fwd_call(span, q, k, v, start, end, qb=256, kb=256):
    count, width = q.shape
    lanes = GROUP * HEAD
    column = pl.BlockSpec((count, lanes), lambda g, s: (0, g))
    edge = pl.BlockSpec((count, 1), lambda g, s: (0, 0))
    heads = width // HEAD
    return pl.pallas_call(
        functools.partial(attn_fwd_kernel, qb=qb, kb=kb),
        grid_spec=pltpu.PrefetchScalarGridSpec(
            num_scalar_prefetch=1,
            grid=(heads // GROUP,),
            in_specs=[column, column, column, edge, edge],
            out_specs=[column, column, pl.BlockSpec((1, 8, count), lambda g, s: (g, 0, 0))],
            scratch_shapes=[
                pltpu.VMEM((GROUP, count, PAIR), BF),
                pltpu.VMEM((GROUP, count, PAIR), BF),
            ],
        ),
        out_shape=[
            jax.ShapeDtypeStruct((count, width), BF),
            jax.ShapeDtypeStruct((count, width), BF),
            jax.ShapeDtypeStruct((heads // GROUP, 8, count), F32),
        ],
        compiler_params=params(),
        cost_estimate=cost(16 * count * count * heads * HEAD, 8 * count * width, heads * count * count),
        name="attention_forward",
    )(span, q, k, v, start, end)


def attn_bwd_kernel(
    span, q, k, v, do, start, end, inverse, delta, rq, rk, scale,
    dq, dk, dv, scale_grad, qm, km, dom, dq_acc, dk_acc, dv_acc, *, qb, kb,
):
    count = q.shape[0]
    pairs = q.shape[1] // PAIR
    for pair in range(pairs):
        lanes = slice(pair * PAIR, (pair + 1) * PAIR)
        for h in range(2):
            qm[2 * pair + h] = lane_masked(q[:, lanes], h)
            km[2 * pair + h] = lane_masked(k[:, lanes], h)
            dom[2 * pair + h] = lane_masked(do[:, lanes], h)
    dk_acc[...] = jnp.zeros_like(dk_acc)
    dv_acc[...] = jnp.zeros_like(dv_acc)

    def one_block(i, _):
        first = pl.multiple_of(i * qb, qb)
        here = pl.ds(first, qb)
        low, high = start[0:1, here], end[0:1, here]
        dq_acc[...] = jnp.zeros_like(dq_acc)

        def step(j, _):
            at = pl.multiple_of(j * kb, kb)
            there = pl.ds(at, kb)
            place = at + lax.broadcasted_iota(jnp.int32, (kb, qb), 0)
            seen = (place >= low) & (place < high)
            for pair in range(pairs):
                lanes = slice(pair * PAIR, (pair + 1) * PAIR)
                ps, dss = [], []
                for h in (2 * pair, 2 * pair + 1):
                    s = nt(k[there, lanes], qm[h, here, :])
                    p = jnp.where(seen, jnp.exp(s) * inverse[0, h : h + 1, here], 0.0)
                    dp = nt(v[there, lanes], dom[h, here, :])
                    ps.append(p.astype(BF))
                    dss.append((p * (dp - delta[0, h : h + 1, here])).astype(BF))
                dv_acc[there, lanes] += nn(ps[0], dom[2 * pair, here, :]) + nn(ps[1], dom[2 * pair + 1, here, :])
                dk_acc[there, lanes] += nn(dss[0], qm[2 * pair, here, :]) + nn(dss[1], qm[2 * pair + 1, here, :])
                dq_acc[:, lanes] += tn(dss[0], km[2 * pair, there, :]) + tn(dss[1], km[2 * pair + 1, there, :])
            return 0

        lax.fori_loop(span[0, i], span[1, i], step, 0)
        g = dq_acc[...]
        sc = scale[0:1, :]
        unit = q[here, :].astype(F32) / sc
        inner = head_sums(unit * g)
        dq[here, :] = (sc * rq[here, :].astype(F32) * (g - unit * inner)).astype(BF)
        return jnp.sum(inner, axis=0, keepdims=True)

    def looped(i, total):
        return total + one_block(i, 0)

    total = lax.fori_loop(0, count // qb, looped, jnp.zeros((1, q.shape[1]), F32))
    scale_grad[...] = jnp.broadcast_to(total, scale_grad.shape)
    for at in range(0, count, qb):
        here = pl.ds(at, qb)
        g = dk_acc[here, :]
        unit = k[here, :].astype(F32)
        dk[here, :] = (rk[here, :].astype(F32) * (g - unit * head_sums(unit * g))).astype(BF)
    dv[...] = dv_acc[...].astype(BF)


def attn_bwd_call(span, q, k, v, do, start, end, inverse, delta, rq, rk, scale_lanes, qb=256, kb=256):
    count, width = q.shape
    lanes = GROUP * HEAD
    column = pl.BlockSpec((count, lanes), lambda g, s: (0, g))
    edge = pl.BlockSpec((8, count), lambda g, s: (0, 0))
    row = pl.BlockSpec((1, 8, count), lambda g, s: (g, 0, 0))
    small = pl.BlockSpec((8, lanes), lambda g, s: (0, g))
    heads = width // HEAD
    return pl.pallas_call(
        functools.partial(attn_bwd_kernel, qb=qb, kb=kb),
        grid_spec=pltpu.PrefetchScalarGridSpec(
            num_scalar_prefetch=1,
            grid=(heads // GROUP,),
            in_specs=[column] * 4 + [edge] * 2 + [row] * 2 + [column] * 2 + [small],
            out_specs=[column] * 3 + [small],
            scratch_shapes=[pltpu.VMEM((GROUP, count, PAIR), BF)] * 3
            + [pltpu.VMEM((qb, lanes), F32)]
            + [pltpu.VMEM((count, lanes), F32)] * 2,
        ),
        out_shape=[jax.ShapeDtypeStruct((count, width), BF)] * 3
        + [jax.ShapeDtypeStruct((8, width), F32)],
        compiler_params=params(),
        cost_estimate=cost(40 * count * count * heads * HEAD, 18 * count * width, heads * count * count),
        name="attention_backward",
    )(span, q, k, v, do, start, end, inverse, delta, rq, rk, scale_lanes)


def proj_kernel(tokens, mixed, cotangent, member, modulation, weight, after, branch, hidden, down):
    width = tokens.shape[1]
    part = lambda i: nn(member[...], modulation[:, i * width : (i + 1) * width])
    out = nn(mixed[...], weight[...])
    total = tokens[...].astype(F32) + part(0) * out
    after[...] = total
    branch[...] = out.astype(BF)
    unit, _ = centre(total)
    hidden[...] = (unit * (1.0 + part(3)) + part(5)).astype(BF)
    down[...] = (cotangent[...].astype(F32) * part(1)).astype(BF)


def proj_call(tokens, mixed, cotangent, member, modulation, weight, rows=256):
    count, width = tokens.shape
    some = pl.BlockSpec((rows, width), lambda s: (s, 0))
    whole = lambda x: pl.BlockSpec(x.shape, lambda s: (0, 0))
    return pl.pallas_call(
        proj_kernel,
        grid=(count // rows,),
        in_specs=[
            some,
            some,
            some,
            pl.BlockSpec((rows, member.shape[1]), lambda s: (s, 0)),
            whole(modulation),
            pl.BlockSpec((width, width), lambda s: (0, 0)),
        ],
        out_specs=[some] * 4,
        out_shape=[
            jax.ShapeDtypeStruct((count, width), d) for d in (F32, BF, BF, BF)
        ],
        compiler_params=params(),
        cost_estimate=cost(2 * count * width * width, 16 * count * width),
        name="projection",
    )(tokens, mixed, cotangent, member, modulation, weight)


def split_blocks(odd, result, rows, kept, sent):
    result = result.astype(BF)
    for at in range(0, result.shape[0], 2 * rows):
        even_part = result[at : at + rows]
        odd_part = result[at + rows : at + 2 * rows]
        put = slice(at // 2, at // 2 + rows)
        kept[put, :] = jnp.where(odd, odd_part, even_part)
        sent[put, :] = jnp.where(odd, even_part, odd_part)


def mlp_kernel(core, hidden, down, up_w, down_w, *refs, rows, own):
    split = len(refs) == 9
    mlp, back = refs[:2]
    grads = refs[2:-3]
    active, grad, turned = refs[-3:]
    step = pl.program_id(0)
    odd = core[0] == 1

    @pl.when(step == 0)
    def _():
        mlp[...] = jnp.zeros_like(mlp)
        back[...] = jnp.zeros_like(back)
        turned[...] = jnp.transpose(hidden[...])

    for at in range(0, hidden.shape[0], rows):
        here = pl.ds(at, rows)
        e = nn(hidden[here, :], up_w[...])
        da = nt(down[here, :], down_w[...])
        square = e * e
        t = jnp.tanh(e * (GELU_A + GELU_A * GELU_B * square))
        half = 0.5 + 0.5 * t
        act = (e * half).astype(BF)
        slope = half + e * (0.5 - 0.5 * t * t) * (GELU_A + 3.0 * GELU_A * GELU_B * square)
        de = (da * slope).astype(BF)
        active[here, :] = act
        grad[here, :] = de
        mlp[here, :] += nn(act, down_w[...])
        back[here, :] += nt(de, up_w[...])
    if split:
        split_blocks(odd, tn(active[...], down[...]), own, grads[2], grads[3])
        split_blocks(odd, nn(turned[...], grad[...]), own, grads[0], grads[1])
    else:
        grads[1][...] = tn(active[...], down[...]).astype(BF)
        grads[0][...] = nn(turned[...], grad[...]).astype(BF)


def mlp_call(core, hidden, down, packed, own, split, block=512, rows=256):
    count, width = hidden.shape
    units = (packed.shape[1] - width) // 2
    per = width // block
    whole = pl.BlockSpec((count, width), lambda s, c: (0, 0))
    first_up, first_down = width // block, (width + units) // width
    wide = lambda n, first: pl.BlockSpec((n, block), lambda s, c: (0, first + s))
    tall = lambda n, first: pl.BlockSpec((n, width), lambda s, c: (s % per, first + s // per))
    kept = 2 if split else 1
    copies = 2 if split else 1
    return pl.pallas_call(
        functools.partial(mlp_kernel, rows=rows, own=own),
        grid_spec=pltpu.PrefetchScalarGridSpec(
            num_scalar_prefetch=1,
            grid=(units // block,),
            in_specs=[whole, whole, wide(width, first_up), tall(block, first_down)],
            out_specs=[whole, whole]
            + [wide(width // kept, 0)] * copies
            + [tall(block // kept, 0)] * copies,
            scratch_shapes=[
                pltpu.VMEM((count, block), BF),
                pltpu.VMEM((count, block), BF),
                pltpu.VMEM((width, count), BF),
            ],
        ),
        out_shape=[jax.ShapeDtypeStruct((count, width), F32)] * 2
        + [jax.ShapeDtypeStruct((width // kept, units), BF)] * (2 * copies),
        compiler_params=params(),
        cost_estimate=cost(12 * count * width * units, 8 * width * units + 12 * count * width),
        name="feed_forward",
    )(core, hidden, down, packed, packed)


def item_sums(turned, x):
    high, low = halves(x)
    return nn(turned, high) + nn(turned, low)


def norm_back(unit, rstd, w):
    inner = jnp.mean(w * unit, axis=-1, keepdims=True)
    return (w - jnp.mean(w, axis=-1, keepdims=True) - unit * inner) * rstd


def middle_kernel(
    mlp, back, after, cotangent, branch, mixed, rest, member, turned, modulation, weight,
    output, grad_in, branch_grad, mixed_grad, delta, sums,
):
    width = after.shape[1]
    part = lambda i: nn(member[...], modulation[:, i * width : (i + 1) * width])
    upstream = cotangent[...].astype(F32)
    v = after[...]
    output[...] = (v + part(1) * mlp[...]).astype(BF)
    g = back[...]
    unit, rstd = centre(v)
    total = upstream + norm_back(unit, rstd, g * (1.0 + part(3)))
    grad_in[...] = total
    down = (total * part(0)).astype(BF)
    branch_grad[...] = down
    mg = nt(down, weight[...]).astype(BF)
    mixed_grad[...] = mg
    product = mg.astype(F32) * (mixed[...].astype(F32) + rest[...].astype(F32))
    head = lax.broadcasted_iota(jnp.int32, (32, width), 0)
    lane = lax.broadcasted_iota(jnp.int32, (32, width), 1) // HEAD
    wanted = GROUP * (head // 8) + head % 8
    pick = jnp.where((wanted == lane) & (head % 8 < GROUP), 1.0, 0.0).astype(BF)
    high, low = halves(product)
    delta[...] = nt(pick, high) + nt(pick, low)

    @pl.when(pl.program_id(0) == 0)
    def _():
        sums[...] = jnp.zeros_like(sums)

    for i, x in enumerate((total * branch[...].astype(F32), upstream * mlp[...], g * unit, g)):
        sums[:, i * width : (i + 1) * width] += item_sums(turned[...], x)


def middle_call(mlp, back, after, cotangent, branch, mixed, rest, member, turned, modulation, weight, rows=256):
    count, width = after.shape
    some = pl.BlockSpec((rows, width), lambda s: (s, 0))
    whole = lambda x: pl.BlockSpec(x.shape, lambda s: (0, 0))
    items = turned.shape[0]
    heads = 8 * (width // HEAD // GROUP)
    return pl.pallas_call(
        middle_kernel,
        grid=(count // rows,),
        in_specs=[some] * 7
        + [
            pl.BlockSpec((rows, member.shape[1]), lambda s: (s, 0)),
            pl.BlockSpec((items, rows), lambda s: (0, s)),
            whole(modulation),
            pl.BlockSpec((width, width), lambda s: (0, 0)),
        ],
        out_specs=[some] * 4
        + [
            pl.BlockSpec((heads, rows), lambda s: (0, s)),
            pl.BlockSpec((items, 4 * width), lambda s: (0, 0)),
        ],
        out_shape=[jax.ShapeDtypeStruct((count, width), d) for d in (BF, F32, BF, BF)]
        + [
            jax.ShapeDtypeStruct((heads, count), F32),
            jax.ShapeDtypeStruct((items, 4 * width), F32),
        ],
        compiler_params=params(),
        cost_estimate=cost(4 * count * width * width, 30 * count * width),
        name="middle",
    )(mlp, back, after, cotangent, branch, mixed, rest, member, turned, modulation, weight)


def first_kernel(dq, dk, dv, weight, tokens, grad_in, member, turned, modulation, tokens_grad, sums):
    width = tokens.shape[1]
    g = (
        nt(dq[...], weight[:, :width])
        + nt(dk[...], weight[:, width : 2 * width])
        + nt(dv[...], weight[:, 2 * width :])
    )
    unit, rstd = centre(tokens[...].astype(F32))
    sc = nn(member[...], modulation[:, 2 * width : 3 * width])
    tokens_grad[...] = (grad_in[...] + norm_back(unit, rstd, g * (1.0 + sc))).astype(BF)

    @pl.when(pl.program_id(0) == 0)
    def _():
        sums[...] = jnp.zeros_like(sums)

    for i, x in enumerate((g * unit, g)):
        sums[:, i * width : (i + 1) * width] += item_sums(turned[...], x)


def first_call(dq, dk, dv, weight, tokens, grad_in, member, turned, modulation, rows=256):
    count, width = tokens.shape
    some = pl.BlockSpec((rows, width), lambda s: (s, 0))
    whole = lambda x: pl.BlockSpec(x.shape, lambda s: (0, 0))
    items = turned.shape[0]
    return pl.pallas_call(
        first_kernel,
        grid=(count // rows,),
        in_specs=[some] * 3
        + [
            whole(weight),
            some,
            some,
            pl.BlockSpec((rows, member.shape[1]), lambda s: (s, 0)),
            pl.BlockSpec((items, rows), lambda s: (0, s)),
            whole(modulation),
        ],
        out_specs=[some, pl.BlockSpec((items, 2 * width), lambda s: (0, 0))],
        out_shape=[
            jax.ShapeDtypeStruct((count, width), BF),
            jax.ShapeDtypeStruct((items, 2 * width), F32),
        ],
        compiler_params=params(),
        cost_estimate=cost(6 * count * width * width, 18 * count * width),
        name="first_norm_backward",
    )(dq, dk, dv, weight, tokens, grad_in, member, turned, modulation)


def weight_grad_kernel(core, *refs, rows, count):
    split = (len(refs) - 2 - count) == 2
    x = refs[0]
    ys = refs[1 : 1 + count]
    outs = refs[1 + count : -1]
    turned = refs[-1]
    step = pl.program_id(0)
    per = pl.num_programs(0) // count

    @pl.when(step == 0)
    def _():
        turned[...] = jnp.transpose(x[...])

    for which in range(count):

        @pl.when((step >= which * per) & (step < (which + 1) * per))
        def _():
            result = nn(turned[...], ys[which][...])
            if split:
                split_blocks(core[0] == 1, result, rows, outs[0], outs[1])
            else:
                outs[0][...] = result.astype(BF)


def weight_grad_call(core, x, ys, rows, split, block=512):
    count, width = x.shape
    columns = ys[0].shape[1]
    per = columns // block
    steps = per * len(ys)
    wide = lambda n: pl.BlockSpec((n, block), lambda s, c: (0, s))
    shapes = [(width // 2, columns * len(ys))] * 2 if split else [(width, columns * len(ys))]
    part = lambda which: pl.BlockSpec(
        (count, block), lambda s, c: (0, jnp.clip(s - which * per, 0, per - 1))
    )
    return pl.pallas_call(
        functools.partial(weight_grad_kernel, rows=rows, count=len(ys)),
        grid_spec=pltpu.PrefetchScalarGridSpec(
            num_scalar_prefetch=1,
            grid=(steps,),
            in_specs=[pl.BlockSpec((count, width), lambda s, c: (0, 0))]
            + [part(i) for i in range(len(ys))],
            out_specs=[wide(shape[0]) for shape in shapes],
            scratch_shapes=[pltpu.VMEM((width, count), BF)],
        ),
        out_shape=[jax.ShapeDtypeStruct(s, BF) for s in shapes],
        compiler_params=params(),
        cost_estimate=cost(2 * count * width * columns * len(ys), 4 * count * columns * len(ys)),
        name="weight_grad",
    )(core, x, *ys)


BOTH = ("wide", "narrow")
LENGTH_TABLE = np.array([0, 1, 5, 14, 30, 55, 91, 155, 255, 424, 680], np.int32)
SCALE_BOUNDS = np.array([1, 5, 14, 30, 55, 91, 155, 255, 424], np.int32)


def bit_count(size):
    return size.bit_length() - 1


def flip(values, axis, size, bit):
    return lax.ppermute(values, axis, [(i, i ^ (1 << bit)) for i in range(size)])


def chip_order(wide, turn):
    outer = list(range(bit_count(wide)))
    turning, last = outer[:-1], outer[-1:]
    turn = turn % max(1, len(turning))
    return turning[turn:] + turning[:turn] + last


def sum_to_owners(block, dims, order, sizes):
    dims = list(dims)
    for step, (axis, bit) in enumerate(order):
        at = dims.index((axis, bit))
        dims.pop(at)
        mine = (lax.axis_index(axis) >> bit) & 1
        sent = lax.dynamic_index_in_dim(block, 1 - mine, at, keepdims=False)
        kept = lax.dynamic_index_in_dim(block, mine, at, keepdims=False)
        got = flip(sent, axis, sizes[axis], bit)
        block = kept.astype(F32) + got.astype(F32)
        if step < len(order) - 1:
            block = block.astype(BF)
    return block


def scatter_sum(parts, sizes, turn):
    wide, narrow = sizes["wide"], sizes["narrow"]
    dims = [("wide", b) for b in reversed(range(bit_count(wide)))]
    dims += [("narrow", b) for b in reversed(range(bit_count(narrow)))]
    order = [("narrow", b) for b in range(bit_count(narrow))]
    order += [("wide", b) for b in chip_order(wide, turn)]
    if len(parts) == 2:
        kept, sent = parts
        got = flip(sent, "narrow", narrow, 0)
        block = (kept.astype(F32) + got.astype(F32)).astype(BF)
        dims.remove(("narrow", 0))
        order = order[1:]
    else:
        (block,) = parts
    own = block.shape[0] // 2 ** len(dims)
    return sum_to_owners(block.reshape((2,) * len(dims) + (own, block.shape[1])), dims, order, sizes)


def gather_halves(shard, sizes, order):
    block = shard[None]
    for bit in order:
        got = flip(block, "wide", sizes["wide"], bit)
        block = jnp.concatenate([block, got], axis=0)
    block = block.reshape(-1, shard.shape[1])
    return block, flip(block, "narrow", sizes["narrow"], 0)


def relative_place(owner, me, order):
    apart = owner ^ me
    place = jnp.zeros_like(apart)
    for at, bit in enumerate(order):
        place = place | (((apart >> (bit + 1)) & 1) << at)
    return 2 * place + (apart & 1)


def layout(level_row, count):
    lengths = jnp.sum(
        jnp.where(
            level_row[:, None] == jnp.arange(11, dtype=jnp.int32)[None, :],
            jnp.asarray(LENGTH_TABLE)[None, :],
            0,
        ),
        axis=1,
    ).astype(jnp.int32)
    starts = jnp.cumsum(lengths) - lengths
    position = jnp.arange(count, dtype=jnp.int32)[None, :]
    inside = (position >= starts[:, None]) & (position < (starts + lengths)[:, None])
    inside_int = inside.astype(jnp.int32)
    covered = jnp.sum(inside_int, axis=0, keepdims=True) > 0
    first = jnp.where(covered, jnp.sum(inside_int * starts[:, None], axis=0, keepdims=True), position)
    offset = position - first
    length = jnp.full_like(position, int(LENGTH_TABLE[1]))
    for low, high in zip(LENGTH_TABLE[1:-1], LENGTH_TABLE[2:]):
        length = jnp.where(offset >= int(low), int(high), length)
    return inside, first, first + jnp.where(covered, length, 1)


def per_device(
    tokens,
    class_table,
    ada_weight,
    qkv_weight,
    proj_weight,
    head_scale,
    fc1_weight,
    fc2_weight,
    levels,
    labels,
    cotangent,
):
    count, width = tokens.shape
    head_count = head_scale.shape[0]
    sizes = {"wide": lax.axis_size("wide"), "narrow": lax.axis_size("narrow")}
    devices = sizes["wide"] * sizes["narrow"]
    me = lax.axis_index("wide") * sizes["narrow"] + lax.axis_index("narrow")
    core = (lax.axis_index("narrow") & 1).reshape(1).astype(jnp.int32)
    owners = jnp.arange(devices, dtype=jnp.int32)
    slots = labels.shape[1]
    own = proj_weight.shape[0]
    blocks = fc2_weight.shape[0] // own
    paired = own % 16 == 0 and sizes["narrow"] == 2

    label_block = jnp.zeros((own, PAIR), BF)
    label_block = label_block.at[0, :slots].set((labels[0] // 256).astype(BF))
    label_block = label_block.at[1, :slots].set((labels[0] % 256).astype(BF))
    table_shard = jnp.concatenate([class_table, label_block], axis=1)
    if paired:
        orders = [chip_order(sizes["wide"], turn)[::-1] for turn in range(3)]
        table_halves = gather_halves(table_shard, sizes, orders[0])
        table_all = jnp.stack([h.reshape(-1, own, width + PAIR) for h in table_halves], axis=1)
        table_all = table_all.reshape(devices, own, width + PAIR)
        weights = [
            gather_halves(qkv_weight[:, i * width : (i + 1) * width], sizes, orders[i])
            for i in range(3)
        ]
        table_places = relative_place(owners, me, orders[0])
        places = jnp.stack([relative_place(owners, me, o) for o in orders]).astype(jnp.int32)
    else:
        table_all = lax.all_gather(table_shard, BOTH, axis=0, tiled=False)
        qkv_all = lax.all_gather(qkv_weight, BOTH, axis=0, tiled=True)
        weights = [(qkv_all[:, i * width : (i + 1) * width],) for i in range(3)]
        table_places = owners
        places = jnp.stack([owners] * 3)
    up_shard = fc1_weight.reshape(own, devices, blocks, own).transpose(0, 2, 1, 3)
    packed = lax.all_gather(
        jnp.concatenate(
            [proj_weight, up_shard.reshape(own, -1)]
            + [fc2_weight[i * own : (i + 1) * own] for i in range(blocks)],
            axis=1,
        ),
        BOTH,
        axis=0,
        tiled=True,
    )

    picked = (table_places[:, None] == owners[None, :]).astype(F32)
    label_parts = jnp.dot(
        picked, table_all[:, :2, width : width + 2 * slots].reshape(devices, -1).astype(F32)
    ).reshape(devices, 2, 2 * slots)
    labels_all = (256.0 * label_parts[:, 0, :slots] + label_parts[:, 1, :slots]).astype(jnp.int32)
    labels_all = labels_all.reshape(-1)
    label_owner = labels_all // own
    if paired:
        label_place = relative_place(label_owner, me, orders[0]) * own + labels_all % own
    else:
        label_place = labels_all
    label_pick = (
        label_place[:, None] == jnp.arange(devices * own, dtype=jnp.int32)[None, :]
    ).astype(BF)
    class_vec = jnp.dot(
        label_pick, table_all[:, :, :width].reshape(-1, width), preferred_element_type=F32
    )
    lifted = jax.nn.silu(class_vec).astype(BF)
    ada_columns = lax.all_to_all(ada_weight, BOTH, 1, 0, tiled=True)
    modulation = lax.all_to_all(
        jnp.dot(lifted, ada_columns, preferred_element_type=F32), BOTH, 0, 1, tiled=True
    )
    high = lax.reduce_precision(modulation, 8, 7)
    middle = lax.reduce_precision(modulation - high, 8, 7)
    low = modulation - high - middle
    terms = jnp.pad(jnp.concatenate([high, middle, low]), ((0, 32 - 3 * slots), (0, 0))).astype(BF)

    inside, first, last = layout(levels[0], count)
    turned = jnp.pad(inside.astype(BF), ((0, 16 - slots), (0, 0)))
    member = jnp.pad(jnp.concatenate([inside] * 3).astype(BF), ((0, 32 - 3 * slots), (0, 0))).T
    starts = jnp.broadcast_to(first, (8, count))
    ends = jnp.broadcast_to(last, (8, count))
    tile = 256
    span = jnp.concatenate(
        [first[:, ::tile] // tile, (last[:, tile - 1 :: tile] + tile - 1) // tile]
    ).astype(jnp.int32)
    scale_lanes = jnp.broadcast_to(jnp.repeat(head_scale, width // head_count)[None], (8, width))

    hidden_one, q, k, v, rq, rk, qkv_full = qkv_call(
        places, tokens, member, terms, weights, scale_lanes
    )
    mixed, rest, inverse = attn_fwd_call(
        span, q, k, v, first.reshape(count, 1), last.reshape(count, 1), tile, tile
    )
    after, branch, hidden_two, down = proj_call(tokens, mixed, cotangent, member, terms, packed)
    mlp, back, *grads = mlp_call(core, hidden_two, down, packed, own, paired)
    split = 2 if paired else 1
    fc1_grad = scatter_sum(grads[:split], sizes, 0)
    fc2_grad = scatter_sum(grads[split:], sizes, 1)
    fc1_grad = fc1_grad.reshape(own, blocks, devices, own).transpose(0, 2, 1, 3).reshape(own, -1)
    fc2_grad = fc2_grad.reshape(own, blocks, width).transpose(1, 0, 2).reshape(-1, width)
    output, grad_in, branch_grad, mixed_grad, delta, sums = middle_call(
        mlp, back, after, cotangent, branch, mixed, rest, member, turned, terms, packed
    )
    proj_grad = scatter_sum(
        weight_grad_call(core, mixed, [branch_grad], own, paired), sizes, 2
    )
    dq, dk, dv, scale_part = attn_bwd_call(
        span, q, k, v, mixed_grad, starts, ends, inverse,
        delta.reshape(-1, 8, count), rq, rk, scale_lanes, tile, tile,
    )
    qkv_grad = scatter_sum(weight_grad_call(core, hidden_one, [dq, dk, dv], own, paired), sizes, 0)
    tokens_grad, first_sums = first_call(
        dq, dk, dv, qkv_full, tokens, grad_in, member, turned, terms
    )

    early, late = sums[:slots].astype(BF), first_sums[:slots].astype(BF)
    early_all = lax.all_gather(early, BOTH, axis=0, tiled=True)
    late_all = lax.all_gather(late, BOTH, axis=0, tiled=True)
    cut = lambda x, i: x[:, i * width : (i + 1) * width]
    pieces = [cut(early_all, 0), cut(early_all, 1), cut(late_all, 0), cut(early_all, 2), cut(late_all, 1), cut(early_all, 3)]
    modulation_grad = jnp.concatenate(pieces, axis=1)
    own_width = width // devices
    own_lifted = lax.dynamic_slice_in_dim(lifted, me * own_width, own_width, 1)
    own_vec = lax.dynamic_slice_in_dim(class_vec, me * own_width, own_width, 1)
    ada_grad = tn(own_lifted, modulation_grad)
    lifted_grad = nt(modulation_grad, ada_weight)
    _, silu_pull = jax.vjp(jax.nn.silu, own_vec)
    class_grad = silu_pull(lifted_grad)[0]
    label_true = (labels_all[:, None] == jnp.arange(devices * own, dtype=jnp.int32)[None, :]).astype(F32)
    table_columns = jnp.einsum("ic,id->cd", label_true, class_grad, precision=lax.Precision.HIGHEST)
    scale_sums = scale_part[0].reshape(head_count, HEAD)[:, 0]
    head_rows = -(-head_count // own_width)
    head_rows += -head_rows % 8
    scale_rows = jnp.pad(scale_sums, (0, head_rows * own_width - head_count)).reshape(
        1, head_rows, own_width
    )
    outgoing = jnp.concatenate(
        [
            table_columns.reshape(devices, own, own_width),
            jnp.broadcast_to(scale_rows, (devices, head_rows, own_width)),
        ],
        axis=1,
    ).reshape(-1, own_width)
    incoming = lax.all_to_all(outgoing, BOTH, 0, 1, tiled=True)
    table_grad = incoming[:own]
    scale_grad = jnp.sum(incoming[own:].reshape(head_rows, devices, own_width), axis=1).reshape(-1)[
        :head_count
    ]
    return (
        output,
        tokens_grad,
        table_grad,
        ada_grad,
        qkv_grad,
        proj_grad,
        scale_grad,
        fc1_grad,
        fc2_grad,
    )


def solution(mesh):
    rows = P(BOTH, None)
    in_specs = (rows,) * 5 + (P(),) + (rows,) * 5
    out_specs = (rows,) * 6 + (P(),) + (rows,) * 2
    return jax.shard_map(
        per_device, mesh=mesh, in_specs=in_specs, out_specs=out_specs, check_vma=False
    )
```

time: 1080 us -> 680 us (0.63)
  matrix products: 405 us -> 5.85 us
  Pallas kernels: 0 us -> 237 us
  other arithmetic: 183 us -> 26.3 us
  local copies, waits for them, and re-layouts: 195 us -> 46.8 us
  starting transfers between devices: 40 us -> 82.1 us
  blocking collectives: 0 us -> 40.9 us
    dot_general x33 -> x6, matrix products: 405 us -> 5.85 us  [the longest x1 2.34 us: tn(): lax.dot_general(a, b, (((0,), (0,)), ((), ())), preferred_element_type=F32)]
    pallas_call x0 -> x9, Pallas kernels: none -> 237 us  [the longest x1 63.7 us: mlp_call(): pl.pallas_call(functools.partial(mlp_kernel, rows=rows, own=own), grid_sp...]
    all_gather x6 -> x2, waiting for transfers between devices: 112 us -> 0.03 us  [the longest x1 0.02 us: per_device(): early_all = lax.all_gather(early, BOTH, axis=0, tiled=True)]
    ppermute x20 -> x40, waiting for transfers between devices: 82.8 us -> 188 us  [flip(): return lax.ppermute(values, axis, [(i, i ^ 1 << bit) for i in range(size)])]
    dynamic_update_slice x4 -> x0, local copies, waits for them, and re-layouts: 83.3 us -> none  [per_device(): lax.map(attend, jnp.arange(block_count, dtype=jnp.int32))]
    convert_element_type x24 -> x18, other arithmetic: 98.6 us -> 17 us  [the longest x4 11.8 us: scatter_sum(): block = (kept.astype(F32) + got.astype(F32)).astype(BF)]
    ppermute x20 -> x40, starting transfers between devices: 20 us -> 71.2 us  [flip(): return lax.ppermute(values, axis, [(i, i ^ 1 << bit) for i in range(size)])]
    reduce_sum x13 -> x3, other arithmetic: 45.6 us -> 0.47 us  [the longest x1 0.2 us: per_device(): jnp.sum(incoming[own:].reshape(head_rows, devices, own_width), axis=1)]
  transfers between devices with their start and end apart: 29 -> 45, of which waited for: 17 -> 22; matrix products, arithmetic and copies ran while one was open for 31% -> 10% of each run, Pallas kernels for 0% -> 24%
where the time goes in v2:
time: 680 us; the launch traced here: 672 us
  Pallas kernels  237 us (35%)
  waiting for transfers between devices  217 us (32%)
  starting transfers between devices  82.1 us (12%)
  local copies, waits for them, and re-layouts  46.8 us (7%)
  blocking collectives  40.9 us (6%)
  other arithmetic  26.3 us (4%)
  between operations  15.6 us (2%)
    ppermute x40, waiting for transfers between devices, flip(): return lax.ppermute(values, axis, [(i, i ^ 1 << bit) for i in range(size)])  188 us
    ppermute x40, starting transfers between devices, flip(): return lax.ppermute(values, axis, [(i, i ^ 1 << bit) for i in range(size)])  71.2 us
    pallas_call x1, Pallas kernels, mlp_call(): pl.pallas_call(functools.partial(mlp_kernel, rows=rows, own=own), grid_sp...  63.7 us
    pallas_call x1, Pallas kernels, attn_bwd_call(): pl.pallas_call(functools.partial(attn_bwd_kernel, qb=qb, kb=kb), grid_spe...  50.6 us
    all_gather x1, blocking collectives, per_device(): late_all = lax.all_gather(late, BOTH, axis=0, tiled=True)  40.9 us
    pallas_call x1, Pallas kernels, attn_fwd_call(): pl.pallas_call(functools.partial(attn_fwd_kernel, qb=qb, kb=kb), grid_spe...  35.8 us
    all_to_all x1, waiting for transfers between devices, per_device(): incoming = lax.all_to_all(outgoing, BOTH, 0, 1, tiled=True)  27 us
    pallas_call x1, Pallas kernels, qkv_call(): pl.pallas_call(functools.partial(qkv_kernel, pieces=pieces), grid_spec=pl...  25.1 us
  transfers between devices with their start and end apart: 45, of which 22 were waited for; matrix products, arithmetic and copies ran while one was open for 10% of the time, Pallas kernels for 24%

profile of v2, /device:TPU:0, one launch (start us, length us, event | category | flops | bytes accessed | tf_op | source)
XLA Modules:
  0.0 671.9 jit_solution(12011510836690841039)
XLA Ops:
  11.6 4.1 collective-permute-start
  17.4 3.8 all-to-all-start
  21.3 2.7 collective-permute-start.10
  24.2 2.7 collective-permute-start.5
  33.0 21.6 %collective-permute-done.10 = bf16[1,32,1024]{2,1,0:T(8,128)(2,1)S(1)} collective-permute-done((bf16[1,32,1024]{2,1,0:T(8,128)(2,1)S(1)}, bf16[1,32,1024]{2,1,0:T(8,128)(2,1)S(1)}, u32[]{:S(2)}, u32[]{:S(2)}) %collective-permute-start.10) | collective-permute-done | bytes 65568 | tf_op jit(solution)/shard_map/ppermute | solution.py:623
  58.7 2.1 collective-permute-start.1
  60.8 19.9 %collective-permute-done.1 = bf16[2,32,1152]{2,1,0:T(8,128)(2,1)S(1)} collective-permute-done((bf16[2,32,1152]{2,1,0:T(8,128)(2,1)S(1)}, bf16[2,32,1152]{2,1,0:T(8,128)(2,1)S(1)}, u32[]{:S(2)}, u32[]{:S(2)}) %collective-permute-start.1) | collective-permute-done | bytes 147488 | tf_op jit(solution)/shard_map/ppermute | solution.py:623
  82.1 6.9 %collective-permute-done.2 = bf16[4,32,1152]{2,1,0:T(8,128)(2,1)S(1)} collective-permute-done((bf16[4,32,1152]{2,1,0:T(8,128)(2,1)S(1)}, bf16[4,32,1152]{2,1,0:T(8,128)(2,1)S(1)}, u32[]{:S(2)}, u32[]{:S(2)}) %collective-permute-start.2) | collective-permute-done | bytes 294944 | tf_op jit(solution)/shard_map/ppermute | solution.py:623
  93.1 5.9 collective-permute-done.3
  105.1 20.2 %collective-permute-done.13 = bf16[8,32,1024]{2,1,0:T(8,128)(2,1)S(1)} collective-permute-done((bf16[8,32,1024]{2,1,0:T(8,128)(2,1)S(1)}, bf16[8,32,1024]{2,1,0:T(8,128)(2,1)S(1)}, u32[]{:S(2)}, u32[]{:S(2)}) %collective-permute-start.13) | collective-permute-done | bytes 524320 | tf_op jit(solution)/shard_map/ppermute | solution.py:623
  131.4 3.3 all-to-all-start.1
  135.0 7.6 %collective-permute-done.18 = bf16[8,32,1024]{2,1,0:T(8,128)(2,1)} collective-permute-done((bf16[8,32,1024]{2,1,0:T(8,128)(2,1)S(1)}, bf16[8,32,1024]{2,1,0:T(8,128)(2,1)}, u32[]{:S(2)}, u32[]{:S(2)}) %collective-permute-start.18) | collective-permute-done | bytes 524320 | tf_op jit(solution)/shard_map/ppermute | solution.py:623
  147.8 2.5 all-to-all-done.1
  152.4 25.1 %qkv_forward.1 = (bf16[1024,1024]{1,0:T(8,128)(2,1)}, bf16[1024,1024]{1,0:T(8,128)(2,1)}, bf16[1024,1024]{1,0:T(8,128)(2,1)}, bf16[1024,1024]{1,0:T(8,128)(2,1)}...) custom-call(s32[3,32]{1,0:T(4,128)} %pad_add_fusion.1.places, ...), custom_call_target="tpu_custom_call" | custom-call | flops 6442450944 | bytes 27262976 | tf_op jit(solution)/shard_map/qkv_forward/pallas_call | solution.py:132
  177.5 35.8 %attention_forward.1 = (bf16[1024,1024]{1,0:T(8,128)(2,1)}, bf16[1024,1024]{1,0:T(8,128)(2,1)}, f32[4,8,1024]{2,1,0:T(8,128)}) custom-call(s32[2,4]{1,0:T(2,128)} %pad_add_fusion.2.span, bf16[1024,1024]{1,0:T(8,128)(2,1)} %get-tuple-element.69.q, bf16[1024,1024]{1,0:T(8,128)(2,1)} %get-tuple-element.70.k, bf16[1024,1024]{1,0:T(8,128)(2,1)} %get-tuple-element.71.v, ...), custom_call_target="tpu_custom_call" | custom-call | flops 17179869184 | bytes 8388608 | tf_op jit(solution)/shard_map/attention_forward/pallas_call | solution.py:213
  213.3 9.5 %projection.1 = (f32[1024,1024]{1,0:T(8,128)}, bf16[1024,1024]{1,0:T(8,128)(2,1)}, bf16[1024,1024]{1,0:T(8,128)(2,1)}, bf16[1024,1024]{1,0:T(8,128)(2,1)}) custom-call(bf16[1024,1024]{1,0:T(8,128)(2,1)} %tokens.5, bf16[1024,1024]{1,0:T(8,128)(2,1)} %get-tuple-element.72.mixed.refs_0_, bf16[1024,1024]{1,0:T(8,128)(2,1)} %cotangent.3, ...), custom_call_target="tpu_custom_call" | custom-call | flops 2147483648 | bytes 16777216 | tf_op jit(solution)/shard_map/projection/pallas_call | solution.py:340
  222.8 63.7 %feed_forward.1 = (f32[1024,1024]{1,0:T(8,128)}, f32[1024,1024]{1,0:T(8,128)}, bf16[512,4096]{1,0:T(8,128)(2,1)}, bf16[512,4096]{1,0:T(8,128)(2,1)}, bf16[512,40...) custom-call(s32[1]{0:T(128)} %bitcast.core, bf16[1024,1024]{1,0:T(8,128)(2,1)} %get-tuple-element.73.hidden, ...), custom_call_target="tpu_custom_call" | custom-call | flops 51539607552 | bytes 46137344 | tf_op jit(solution)/shard_map/feed_forward/pallas_call | solution.py:417
  287.0 17.5 %middle.1 = (bf16[1024,1024]{1,0:T(8,128)(2,1)}, f32[1024,1024]{1,0:T(8,128)}, bf16[1024,1024]{1,0:T(8,128)(2,1)}, bf16[1024,1024]{1,0:T(8,128)(2,1)}, f32[32,1024]{1,0:T(8,128)}, /*index=5*/f32[16,4096]{1,0:T(8,128)}) custom-call(f32[1024,1024]{1,0:T(8,128)} %get-tuple-element.75.mlp, f32[1024,1024]{1,0:T(8,128)} %get-tuple-element.76.back, ...), custom_call_target="tpu_custom_call" | custom-call | flops 4294967296 | bytes 31457280 | tf_op jit(solution)/shard_map/middle/pallas_call | solution.py:489
  304.5 6.2 weight_grad.3
  312.0 50.6 %attention_backward.1 = (bf16[1024,1024]{1,0:T(8,128)(2,1)}, bf16[1024,1024]{1,0:T(8,128)(2,1)}, bf16[1024,1024]{1,0:T(8,128)(2,1)}, f32[8,1024]{1,0:T(8,128)}) custom-call(s32[2,4]{1,0:T(2,128)} %pad_add_fusion.2.span, bf16[1024,1024]{1,0:T(8,128)(2,1)} %get-tuple-element.69.q, bf16[1024,1024]{1,0:T(8,128)(2,1)} %get-tuple-element.70.k, ...), custom_call_target="tpu_custom_call" | custom-call | flops 42949672960 | bytes 18874368 | tf_op jit(solution)/shard_map/attention_backward/pallas_call | solution.py:305
  362.6 12.7 %weight_grad.2 = (bf16[512,3072]{1,0:T(8,128)(2,1)}, bf16[512,3072]{1,0:T(8,128)(2,1)}) custom-call(s32[1]{0:T(128)} %bitcast.core, bf16[1024,1024]{1,0:T(8,128)(2,1)} %get-tuple-element.95.refs_0_, bf16[1024,1024]{1,0:T(8,128)(2,1)} %get-tuple-element.86.dq.refs_1_, bf16[1024,1024]{1,0:T(8,128)(2,1)} %get-tuple-element.87.dk.refs_2_, ...), custom_call_target="tpu_custom_call" | custom-call | flops 6442450944 | bytes 12582912 | tf_op jit(solution)/shard_map/weight_grad/pallas_call | solution.py:596
  377.4 27.4 %collective-permute-start.26 = (bf16[2,2,2,32,1024]{4,3,0,1,2:T(8,128)(2,1)S(1)}, bf16[2,2,2,32,1024]{4,3,0,1,2:T(8,128)(2,1)S(1)}, u32[]{:S(2)}, u32[]{:S(2)}) collective-permute-start(bf16[2,2,2,32,1024]{4,3,0,1,2:T(8,128)(2,1)S(1)} %bitcast.192), channel_id=1, source_target_pairs={{0,8},{2,10},{4,12},{6,14},{8,0},{10,2},{12,4},{14,6},{16,24},{18,... | collective-permute-start | bytes 1572872 | tf_op jit(solution)/shard_map/ppermute | solution.py:623
  404.8 16.2 %first_norm_backward.1 = (bf16[1024,1024]{1,0:T(8,128)(2,1)}, f32[16,2048]{1,0:T(8,128)}) custom-call(bf16[1024,1024]{1,0:T(8,128)(2,1)} %get-tuple-element.86.dq.refs_1_, bf16[1024,1024]{1,0:T(8,128)(2,1)} %get-tuple-element.87.dk.refs_2_, bf16[1024,1024]{1,0:T(8,128)(2,1)} %get-tuple-element.88.dv.refs_3_, bf16[1024,3072]{1,0:T(8,128)(2,1)} %get-tuple-element.89.weight, ...), custom_call_target="tpu_custom_call" | custom-call | flops 6442450944 | bytes 18874368 | tf_op jit(solution)/shard_map/first_norm_backward/pallas_call | solution.py:539
  422.3 8.8 %collective-permute-done.27 = bf16[2,2,32,1024]{3,2,0,1:T(8,128)(2,1)S(1)} collective-permute-done((bf16[2,2,32,1024]{3,2,0,1:T(8,128)(2,1)S(1)}, bf16[2,2,32,1024]{3,2,0,1:T(8,128)(2,1)S(1)}, u32[]{:S(2)}, u32[]{:S(2)}) %collective-permute-start.27) | collective-permute-done | bytes 262176 | tf_op jit(solution)/shard_map/ppermute | solution.py:623
  431.3 40.9 %all-gather.1 = bf16[32,6,2048]{2,1,0:T(8,128)(2,1)S(1)} all-gather(bf16[1,6,2048]{2,1,0:T(8,128)(2,1)S(1)} %fusion.39), channel_id=1, replica_groups=mesh['wide'=16,'narrow'=2] {'wide','narrow'}, dimensions={0}, use_global_device_ids=true | all-gather | bytes 811008 | tf_op jit(solution)/shard_map/all_gather | solution.py:831
  473.7 3.7 reshape.674
  479.1 4.0 add_convert_fusion.2
  490.8 3.5 all-to-all-start.2
  495.0 2.3 fusion.34
  497.3 27.0 %all-to-all-done.2 = f32[32,1,1280]{2,1,0:T(1,128)S(1)} async-done(((f32[32,1,1280]{2,1,0:T(1,128)}), f32[32,1,1280]{2,1,0:T(1,128)S(1)}, u32[]{:S(2)}, u32[]{:S(2)}) %all-to-all-start.2) | async-done | bytes 163872 | tf_op jit(solution)/shard_map/all_to_all | solution.py:857
  528.1 2.1 fusion.2
  531.8 3.7 add_convert_fusion
  536.4 14.3 %collective-permute-done.22 = bf16[2,2,32,3072]{3,2,0,1:T(8,128)(2,1)S(1)} collective-permute-done((bf16[2,2,32,3072]{3,2,0,1:T(8,128)(2,1)S(1)}, bf16[2,2,32,3072]{3,2,0,1:T(8,128)(2,1)S(1)}, u32[]{:S(2)}, u32[]{:S(2)}) %collective-permute-start.22) | collective-permute-done | bytes 786464 | tf_op jit(solution)/shard_map/ppermute | solution.py:623
  552.0 3.7 add_convert_fusion.1
  555.8 4.7 collective-permute-done.23
  560.6 3.4 collective-permute-start.24
  566.0 4.1 collective-permute-done.24
  570.9 23.9 %collective-permute-done.36 = bf16[2,2,2,32,4096]{4,3,2,1,0:T(8,128)(2,1)S(1)} collective-permute-done((bf16[2,2,2,32,4096]{4,3,2,1,0:T(8,128)(2,1)S(1)}, bf16[2,2,2,32,4096]{4,3,2,1,0:T(8,128)(2,1)S(1)}, u32[]{:S(2)}, u32[]{:S(2)}) %collective-permute-start.36) | collective-permute-done | bytes 2097184 | tf_op jit(solution)/shard_map/ppermute | solution.py:623
  596.3 12.2 %collective-permute-done.31 = bf16[2,2,2,32,4096]{4,3,2,1,0:T(8,128)(2,1)S(1)} collective-permute-done((bf16[2,2,2,32,4096]{4,3,2,1,0:T(8,128)(2,1)S(1)}, bf16[2,2,2,32,4096]{4,3,2,1,0:T(8,128)(2,1)S(1)}, u32[]{:S(2)}, u32[]{:S(2)}) %collective-permute-start.31) | collective-permute-done | bytes 2097184 | tf_op jit(solution)/shard_map/ppermute | solution.py:623
  610.8 9.3 %collective-permute-done.37 = bf16[2,2,32,4096]{3,2,1,0:T(8,128)(2,1)S(1)} collective-permute-done((bf16[2,2,32,4096]{3,2,1,0:T(8,128)(2,1)S(1)}, bf16[2,2,32,4096]{3,2,1,0:T(8,128)(2,1)S(1)}, u32[]{:S(2)}, u32[]{:S(2)}) %collective-permute-start.37) | collective-permute-done | bytes 1048608 | tf_op jit(solution)/shard_map/ppermute | solution.py:623
  620.5 1.9 collective-permute-start.38
  622.3 7.7 %collective-permute-done.32 = bf16[2,2,32,4096]{3,2,1,0:T(8,128)(2,1)S(1)} collective-permute-done((bf16[2,2,32,4096]{3,2,1,0:T(8,128)(2,1)S(1)}, bf16[2,2,32,4096]{3,2,1,0:T(8,128)(2,1)S(1)}, u32[]{:S(2)}, u32[]{:S(2)}) %collective-permute-start.32) | collective-permute-done | bytes 1048608 | tf_op jit(solution)/shard_map/ppermute | solution.py:623
  633.0 2.7 collective-permute-start.39
  635.6 10.0 %collective-permute-done.33 = bf16[2,32,4096]{2,1,0:T(8,128)(2,1)S(1)} collective-permute-done((bf16[2,32,4096]{2,1,0:T(8,128)(2,1)S(1)}, bf16[2,32,4096]{2,1,0:T(8,128)(2,1)S(1)}, u32[]{:S(2)}, u32[]{:S(2)}) %collective-permute-start.33) | collective-permute-done | bytes 524320 | tf_op jit(solution)/shard_map/ppermute | solution.py:623
  645.9 4.1 collective-permute-done.39
  650.9 5.6 collective-permute-done.34
  657.2 3.1 copy.198
  660.3 4.4 reshape.653
  (270 shorter events, 77.4 us)
Async XLA Ops:
  7.2 206.1 %all-gather.5.cloned.1.call-start = ((), (), s32[]{:S(2)}) async-start(), calls=%async_computation.3 | async-start | bytes 19464192 | tf_op jit(solution)/shard_map/all_gather | solution.py:752
  11.6 47.1 %collective-permute-start = (bf16[1,32,1152]{2,1,0:T(8,128)(2,1)S(1)}, bf16[1,32,1152]{2,1,0:T(8,128)(2,1)S(1)}, u32[]{:S(2)}, u32[]{:S(2)}) collective-permute-start(bf16[1,32,1152]{2,1,0:T(8,128)(2,1)S(1)} %maximum_bitcast_fusion), channel_id=1, source_target_pairs={{0,16},{2,18},{4,20},{6,22},{8,24},{10,26},{12,28},{14,30},{16,0},... | collective-permute-start | bytes 221192 | tf_op jit(solution)/shard_map/ppermute | solution.py:623
  17.4 112.8 %all-to-all-start = ((bf16[32,32,192]{2,0,1:T(8,128)(2,1)}), bf16[32,32,192]{2,0,1:T(8,128)(2,1)S(1)}, u32[]{:S(2)}, u32[]{:S(2)}) async-start(bf16[32,32,192]{2,0,1:T(8,128)(2,1)} %copy.150), calls=%async_computation | async-start | bytes 1048576 | tf_op jit(solution)/shard_map/all_to_all | solution.py:781
  21.3 33.3 %collective-permute-start.10 = (bf16[1,32,1024]{2,1,0:T(8,128)(2,1)S(1)}, bf16[1,32,1024]{2,1,0:T(8,128)(2,1)S(1)}, u32[]{:S(2)}, u32[]{:S(2)}) collective-permute-start(bf16[1,32,1024]{2,1,0:T(8,128)(2,1)S(1)} %get-tuple-element.153), channel_id=1, source_target_pairs={{0,16},{2,18},{4,20},{6,22},{8,24},{10,26},{12,28},{14,30},{16,0},... | collective-permute-start | bytes 196616 | tf_op jit(solution)/shard_map/ppermute | solution.py:623
  24.0 32.4 %collective-permute-start.15 = (bf16[1,32,1024]{2,1,0:T(8,128)(2,1)S(1)}, bf16[1,32,1024]{2,1,0:T(8,128)(2,1)S(1)}, u32[]{:S(2)}, u32[]{:S(2)}) collective-permute-start(bf16[1,32,1024]{2,1,0:T(8,128)(2,1)S(1)} %get-tuple-element.151), channel_id=1, source_target_pairs={{0,16},{2,18},{4,20},{6,22},{8,24},{10,26},{12,28},{14,30},{16,0},... | collective-permute-start | bytes 196616 | tf_op jit(solution)/shard_map/ppermute | solution.py:623
  24.2 33.7 %collective-permute-start.5 = (bf16[1,32,1024]{2,1,0:T(8,128)(2,1)S(1)}, bf16[1,32,1024]{2,1,0:T(8,128)(2,1)S(1)}, u32[]{:S(2)}, u32[]{:S(2)}) collective-permute-start(bf16[1,32,1024]{2,1,0:T(8,128)(2,1)S(1)} %get-tuple-element.152), channel_id=1, source_target_pairs={{0,16},{2,18},{4,20},{6,22},{8,24},{10,26},{12,28},{14,30},{16,0},... | collective-permute-start | bytes 196616 | tf_op jit(solution)/shard_map/ppermute | solution.py:623
  54.6 27.4 %collective-permute-start.11 = (bf16[2,32,1024]{2,1,0:T(8,128)(2,1)S(1)}, bf16[2,32,1024]{2,1,0:T(8,128)(2,1)S(1)}, u32[]{:S(2)}, u32[]{:S(2)}) collective-permute-start(bf16[2,32,1024]{2,1,0:T(8,128)(2,1)S(1)} %pad_maximum_fusion.12), channel_id=1, source_target_pairs={{0,2},{2,0},{4,6},{6,4},{8,10},{10,8},{12,14},{14,12},{16,18},{18,... | collective-permute-start | bytes 393224 | tf_op jit(solution)/shard_map/ppermute | solution.py:623
  56.4 34.2 %collective-permute-start.16 = (bf16[2,32,1024]{2,1,0:T(8,128)(2,1)S(1)}, bf16[2,32,1024]{2,1,0:T(8,128)(2,1)S(1)}, u32[]{:S(2)}, u32[]{:S(2)}) collective-permute-start(bf16[2,32,1024]{2,1,0:T(8,128)(2,1)S(1)} %pad_maximum_fusion.13), channel_id=1, source_target_pairs={{0,4},{2,6},{4,0},{6,2},{8,12},{10,14},{12,8},{14,10},{16,20},{18,... | collective-permute-start | bytes 393224 | tf_op jit(solution)/shard_map/ppermute | solution.py:623
  57.9 33.3 %collective-permute-start.6 = (bf16[2,32,1024]{2,1,0:T(8,128)(2,1)S(1)}, bf16[2,32,1024]{2,1,0:T(8,128)(2,1)S(1)}, u32[]{:S(2)}, u32[]{:S(2)}) collective-permute-start(bf16[2,32,1024]{2,1,0:T(8,128)(2,1)S(1)} %pad_maximum_fusion.11), channel_id=1, source_target_pairs={{0,8},{2,10},{4,12},{6,14},{8,0},{10,2},{12,4},{14,6},{16,24},{18,... | collective-permute-start | bytes 393224 | tf_op jit(solution)/shard_map/ppermute | solution.py:623
  58.7 22.0 %collective-permute-start.1 = (bf16[2,32,1152]{2,1,0:T(8,128)(2,1)S(1)}, bf16[2,32,1152]{2,1,0:T(8,128)(2,1)S(1)}, u32[]{:S(2)}, u32[]{:S(2)}) collective-permute-start(bf16[2,32,1152]{2,1,0:T(8,128)(2,1)S(1)} %pad_maximum_fusion.10), channel_id=1, source_target_pairs={{0,8},{2,10},{4,12},{6,14},{8,0},{10,2},{12,4},{14,6},{16,24},{18,... | collective-permute-start | bytes 442376 | tf_op jit(solution)/shard_map/ppermute | solution.py:623
  80.7 8.2 %collective-permute-start.2 = (bf16[4,32,1152]{2,1,0:T(8,128)(2,1)S(1)}, bf16[4,32,1152]{2,1,0:T(8,128)(2,1)S(1)}, u32[]{:S(2)}, u32[]{:S(2)}) collective-permute-start(bf16[4,32,1152]{2,1,0:T(8,128)(2,1)S(1)} %pad_maximum_fusion.6), channel_id=1, source_target_pairs={{0,4},{2,6},{4,0},{6,2},{8,12},{10,14},{12,8},{14,10},{16,20},{18,... | collective-permute-start | bytes 884744 | tf_op jit(solution)/shard_map/ppermute | solution.py:623
  82.0 17.8 %collective-permute-start.12 = (bf16[4,32,1024]{2,1,0:T(8,128)(2,1)S(1)}, bf16[4,32,1024]{2,1,0:T(8,128)(2,1)S(1)}, u32[]{:S(2)}, u32[]{:S(2)}) collective-permute-start(bf16[4,32,1024]{2,1,0:T(8,128)(2,1)S(1)} %pad_maximum_fusion.8), channel_id=1, source_target_pairs={{0,8},{2,10},{4,12},{6,14},{8,0},{10,2},{12,4},{14,6},{16,24},{18,... | collective-permute-start | bytes 786440 | tf_op jit(solution)/shard_map/ppermute | solution.py:623
  89.1 9.9 %collective-permute-start.3 = (bf16[8,32,1152]{2,1,0:T(8,128)(2,1)S(1)}, bf16[8,32,1152]{2,1,0:T(8,128)(2,1)S(1)}, u32[]{:S(2)}, u32[]{:S(2)}) collective-permute-start(bf16[8,32,1152]{2,1,0:T(8,128)(2,1)S(1)} %pad_maximum_fusion.1), channel_id=1, source_target_pairs={{0,2},{2,0},{4,6},{6,4},{8,10},{10,8},{12,14},{14,12},{16,18},{18,... | collective-permute-start | bytes 1769480 | tf_op jit(solution)/shard_map/ppermute | solution.py:623
  90.6 11.2 %collective-permute-start.17 = (bf16[4,32,1024]{2,1,0:T(8,128)(2,1)S(1)}, bf16[4,32,1024]{2,1,0:T(8,128)(2,1)S(1)}, u32[]{:S(2)}, u32[]{:S(2)}) collective-permute-start(bf16[4,32,1024]{2,1,0:T(8,128)(2,1)S(1)} %pad_maximum_fusion.9), channel_id=1, source_target_pairs={{0,2},{2,0},{4,6},{6,4},{8,10},{10,8},{12,14},{14,12},{16,18},{18,... | collective-permute-start | bytes 786440 | tf_op jit(solution)/shard_map/ppermute | solution.py:623
  91.3 10.7 %collective-permute-start.7 = (bf16[4,32,1024]{2,1,0:T(8,128)(2,1)S(1)}, bf16[4,32,1024]{2,1,0:T(8,128)(2,1)S(1)}, u32[]{:S(2)}, u32[]{:S(2)}) collective-permute-start(bf16[4,32,1024]{2,1,0:T(8,128)(2,1)S(1)} %pad_maximum_fusion.7), channel_id=1, source_target_pairs={{0,4},{2,6},{4,0},{6,2},{8,12},{10,14},{12,8},{14,10},{16,20},{18,... | collective-permute-start | bytes 786440 | tf_op jit(solution)/shard_map/ppermute | solution.py:623
  99.1 27.0 %collective-permute-start.4 = (bf16[512,1152]{1,0:T(8,128)(2,1)S(1)}, bf16[512,1152]{1,0:T(8,128)(2,1)S(1)}, u32[]{:S(2)}, u32[]{:S(2)}) collective-permute-start(bf16[512,1152]{1,0:T(8,128)(2,1)S(1)} %bitcast.187), channel_id=1, source_target_pairs={{0,1},{1,0},{2,3},{3,2},{4,5},{5,4},{6,7},{7,6},{8,9},{9,8},{10,11... | collective-permute-start | bytes 3538952 | tf_op jit(solution)/shard_map/ppermute | solution.py:623
  99.9 25.3 %collective-permute-start.13 = (bf16[8,32,1024]{2,1,0:T(8,128)(2,1)S(1)}, bf16[8,32,1024]{2,1,0:T(8,128)(2,1)S(1)}, u32[]{:S(2)}, u32[]{:S(2)}) collective-permute-start(bf16[8,32,1024]{2,1,0:T(8,128)(2,1)S(1)} %pad_maximum_fusion.3), channel_id=1, source_target_pairs={{0,4},{2,6},{4,0},{6,2},{8,12},{10,14},{12,8},{14,10},{16,20},{18,... | collective-permute-start | bytes 1572872 | tf_op jit(solution)/shard_map/ppermute | solution.py:623
  101.9 40.7 %collective-permute-start.18 = (bf16[8,32,1024]{2,1,0:T(8,128)(2,1)S(1)}, bf16[8,32,1024]{2,1,0:T(8,128)(2,1)}, u32[]{:S(2)}, u32[]{:S(2)}) collective-permute-start(bf16[8,32,1024]{2,1,0:T(8,128)(2,1)S(1)} %pad_maximum_fusion.4), channel_id=1, source_target_pairs={{0,8},{2,10},{4,12},{6,14},{8,0},{10,2},{12,4},{14,6},{16,24},{18,... | collective-permute-start | bytes 1572872 | tf_op jit(solution)/shard_map/ppermute | solution.py:623
  102.8 41.6 %collective-permute-start.8 = (bf16[8,32,1024]{2,1,0:T(8,128)(2,1)}, bf16[8,32,1024]{2,1,0:T(8,128)(2,1)}, u32[]{:S(2)}, u32[]{:S(2)}) collective-permute-start(bf16[8,32,1024]{2,1,0:T(8,128)(2,1)} %pad_maximum_fusion.2), channel_id=1, source_target_pairs={{0,2},{2,0},{4,6},{6,4},{8,10},{10,8},{12,14},{14,12},{16,18},{18,... | collective-permute-start | bytes 1572872 | tf_op jit(solution)/shard_map/ppermute | solution.py:623
  105.0 21.1 %copy-start.18 = (bf16[16,32,1024]{2,1,0:T(8,128)(2,1)}, bf16[16,32,1024]{2,1,0:T(8,128)(2,1)S(1)}, u32[]{:S(2)}) copy-start(bf16[16,32,1024]{2,1,0:T(8,128)(2,1)S(1)} %constant_dynamic-update-slice_fusion.16) | copy-start | bytes 3145732
  105.1 21.0 %copy-start.15 = (bf16[16,32,1024]{2,1,0:T(8,128)(2,1)}, bf16[16,32,1024]{2,1,0:T(8,128)(2,1)S(1)}, u32[]{:S(2)}) copy-start(bf16[16,32,1024]{2,1,0:T(8,128)(2,1)S(1)} %constant_dynamic-update-slice_fusion.6) | copy-start | bytes 3145732
  126.1 25.3 %collective-permute-start.14 = (bf16[512,1024]{1,0:T(8,128)(2,1)}, bf16[512,1024]{1,0:T(8,128)(2,1)}, u32[]{:S(2)}, u32[]{:S(2)}) collective-permute-start(bf16[512,1024]{1,0:T(8,128)(2,1)} %bitcast.21.refs_2_), channel_id=1, source_target_pairs={{0,1},{1,0},{2,3},{3,2},{4,5},{5,4},{6,7},{7,6},{8,9},{9,8},{10,11... | collective-permute-start | bytes 3145736 | tf_op jit(solution)/shard_map/ppermute | solution.py:623
  131.4 18.8 %all-to-all-start.1 = ((f32[32,6,192]{2,1,0:T(8,128)}), f32[32,6,192]{2,1,0:T(8,128)S(1)}, u32[]{:S(2)}, u32[]{:S(2)}) async-start(f32[32,6,192]{2,1,0:T(8,128)} %copy.153), calls=%async_computation.1 | async-start | bytes 524288 | tf_op jit(solution)/shard_map/all_to_all | solution.py:782
  134.8 338.9 %all-gather.7.cloned.1.call-start = ((), (), s32[]{:S(2)}) async-start(), calls=%async_computation.4 | async-start | bytes 2162688 | tf_op jit(solution)/shard_map/all_gather | solution.py:830
  144.4 6.9 %collective-permute-start.19 = (bf16[512,1024]{1,0:T(8,128)(2,1)}, bf16[512,1024]{1,0:T(8,128)(2,1)S(1)}, u32[]{:S(2)}, u32[]{:S(2)}) collective-permute-start(bf16[512,1024]{1,0:T(8,128)(2,1)} %bitcast.199), channel_id=1, source_target_pairs={{0,1},{1,0},{2,3},{3,2},{4,5},{5,4},{6,7},{7,6},{8,9},{9,8},{10,11... | collective-permute-start | bytes 3145736 | tf_op jit(solution)/shard_map/ppermute | solution.py:623
  145.6 5.8 collective-permute-start.9
  286.5 245.4 %collective-permute-start.35 = (bf16[512,4096]{1,0:T(8,128)(2,1)}, bf16[512,4096]{1,0:T(8,128)(2,1)}, u32[]{:S(2)}, u32[]{:S(2)}) collective-permute-start(bf16[512,4096]{1,0:T(8,128)(2,1)} %get-tuple-element.104), channel_id=1, source_target_pairs={{0,1},{1,0},{2,3},{3,2},{4,5},{5,4},{6,7},{7,6},{8,9},{9,8},{10,11... | collective-permute-start | bytes 12582920 | tf_op jit(solution)/shard_map/ppermute | solution.py:623
  286.5 265.5 %collective-permute-start.30 = (bf16[512,4096]{1,0:T(8,128)(2,1)}, bf16[512,4096]{1,0:T(8,128)(2,1)}, u32[]{:S(2)}, u32[]{:S(2)}) collective-permute-start(bf16[512,4096]{1,0:T(8,128)(2,1)} %get-tuple-element.102), channel_id=1, source_target_pairs={{0,1},{1,0},{2,3},{3,2},{4,5},{5,4},{6,7},{7,6},{8,9},{9,8},{10,11... | collective-permute-start | bytes 12582920 | tf_op jit(solution)/shard_map/ppermute | solution.py:623
  310.7 66.1 %collective-permute-start.25 = (bf16[512,1024]{1,0:T(8,128)(2,1)}, bf16[512,1024]{1,0:T(8,128)(2,1)S(1)}, u32[]{:S(2)}, u32[]{:S(2)}) collective-permute-start(bf16[512,1024]{1,0:T(8,128)(2,1)} %get-tuple-element.100), channel_id=1, source_target_pairs={{0,1},{1,0},{2,3},{3,2},{4,5},{5,4},{6,7},{7,6},{8,9},{9,8},{10,11... | collective-permute-start | bytes 3145736 | tf_op jit(solution)/shard_map/ppermute | solution.py:623
  375.3 103.8 %collective-permute-start.20 = (bf16[512,3072]{1,0:T(8,128)(2,1)}, bf16[512,3072]{1,0:T(8,128)(2,1)}, u32[]{:S(2)}, u32[]{:S(2)}) collective-permute-start(bf16[512,3072]{1,0:T(8,128)(2,1)} %get-tuple-element.97), channel_id=1, source_target_pairs={{0,1},{1,0},{2,3},{3,2},{4,5},{5,4},{6,7},{7,6},{8,9},{9,8},{10,11... | collective-permute-start | bytes 9437192 | tf_op jit(solution)/shard_map/ppermute | solution.py:623
  377.4 43.6 %collective-permute-start.26 = (bf16[2,2,2,32,1024]{4,3,0,1,2:T(8,128)(2,1)S(1)}, bf16[2,2,2,32,1024]{4,3,0,1,2:T(8,128)(2,1)S(1)}, u32[]{:S(2)}, u32[]{:S(2)}) collective-permute-start(bf16[2,2,2,32,1024]{4,3,0,1,2:T(8,128)(2,1)S(1)} %bitcast.192), channel_id=1, source_target_pairs={{0,8},{2,10},{4,12},{6,14},{8,0},{10,2},{12,4},{14,6},{16,24},{18,... | collective-permute-start | bytes 1572872 | tf_op jit(solution)/shard_map/ppermute | solution.py:623
  421.2 9.8 %collective-permute-start.27 = (bf16[2,2,32,1024]{3,2,0,1:T(8,128)(2,1)S(1)}, bf16[2,2,32,1024]{3,2,0,1:T(8,128)(2,1)S(1)}, u32[]{:S(2)}, u32[]{:S(2)}) collective-permute-start(bf16[2,2,32,1024]{3,2,0,1:T(8,128)(2,1)S(1)} %dynamic-slice_bitcast_fusion.10), channel_id=1, source_target_pairs={{0,2},{2,0},{4,6},{6,4},{8,10},{10,8},{12,14},{14,12},{16,18},{18,... | collective-permute-start | bytes 786440 | tf_op jit(solution)/shard_map/ppermute | solution.py:623
  431.2 42.4 %collective-permute-start.28 = (bf16[2,32,1024]{2,1,0:T(8,128)(2,1)S(1)}, bf16[2,32,1024]{2,1,0:T(8,128)(2,1)S(1)}, u32[]{:S(2)}, u32[]{:S(2)}) collective-permute-start(bf16[2,32,1024]{2,1,0:T(8,128)(2,1)S(1)} %dynamic-slice_bitcast_fusion.12), channel_id=1, source_target_pairs={{0,4},{2,6},{4,0},{6,2},{8,12},{10,14},{12,8},{14,10},{16,20},{18,... | collective-permute-start | bytes 393224 | tf_op jit(solution)/shard_map/ppermute | solution.py:623
  473.6 20.7 %collective-permute-start.29 = (bf16[32,1024]{1,0:T(8,128)(2,1)S(1)}, bf16[32,1024]{1,0:T(8,128)(2,1)S(1)}, u32[]{:S(2)}, u32[]{:S(2)}) collective-permute-start(bf16[32,1024]{1,0:T(8,128)(2,1)S(1)} %dynamic-slice_bitcast_fusion.13), channel_id=1, source_target_pairs={{0,16},{2,18},{4,20},{6,22},{8,24},{10,26},{12,28},{14,30},{16,0},... | collective-permute-start | bytes 196616 | tf_op jit(solution)/shard_map/ppermute | solution.py:623
  485.8 42.2 %collective-permute-start.21 = (bf16[2,2,2,32,3072]{4,3,0,1,2:T(8,128)(2,1)}, bf16[2,2,2,32,3072]{4,3,0,1,2:T(8,128)(2,1)}, u32[]{:S(2)}, u32[]{:S(2)}) collective-permute-start(bf16[2,2,2,32,3072]{4,3,0,1,2:T(8,128)(2,1)} %bitcast.167), channel_id=1, source_target_pairs={{0,2},{2,0},{4,6},{6,4},{8,10},{10,8},{12,14},{14,12},{16,18},{18,... | collective-permute-start | bytes 4718600 | tf_op jit(solution)/shard_map/ppermute | solution.py:623
  490.8 33.5 %all-to-all-start.2 = ((f32[32,1,1280]{2,1,0:T(1,128)}), f32[32,1,1280]{2,1,0:T(1,128)S(1)}, u32[]{:S(2)}, u32[]{:S(2)}) async-start(f32[32,1,1280]{2,1,0:T(1,128)} %reshape.687), calls=%async_computation.2 | async-start | bytes 327680 | tf_op jit(solution)/shard_map/all_to_all | solution.py:857
  497.3 30.7 %copy-start.1 = (bf16[2,2,2,1,32,3072]{5,4,3,2,1,0:T(8,128)(2,1)S(1)}, bf16[2,2,2,1,32,3072]{5,4,3,2,1,0:T(8,128)(2,1)}, u32[]{:S(2)}) copy-start(bf16[2,2,2,1,32,3072]{5,4,3,2,1,0:T(8,128)(2,1)} %get-tuple-element.145) | copy-start | bytes 4718596
  530.3 20.5 %collective-permute-start.22 = (bf16[2,2,32,3072]{3,2,0,1:T(8,128)(2,1)S(1)}, bf16[2,2,32,3072]{3,2,0,1:T(8,128)(2,1)S(1)}, u32[]{:S(2)}, u32[]{:S(2)}) collective-permute-start(bf16[2,2,32,3072]{3,2,0,1:T(8,128)(2,1)S(1)} %dynamic-slice_bitcast_fusion.4), channel_id=1, source_target_pairs={{0,4},{2,6},{4,0},{6,2},{8,12},{10,14},{12,8},{14,10},{16,20},{18,... | collective-permute-start | bytes 2359304 | tf_op jit(solution)/shard_map/ppermute | solution.py:623
  535.8 59.1 %collective-permute-start.36 = (bf16[2,2,2,32,4096]{4,3,2,1,0:T(8,128)(2,1)S(1)}, bf16[2,2,2,32,4096]{4,3,2,1,0:T(8,128)(2,1)S(1)}, u32[]{:S(2)}, u32[]{:S(2)}) collective-permute-start(bf16[2,2,2,32,4096]{4,3,2,1,0:T(8,128)(2,1)S(1)} %dynamic-slice_bitcast_fusion), channel_id=1, source_target_pairs={{0,4},{2,6},{4,0},{6,2},{8,12},{10,14},{12,8},{14,10},{16,20},{18,... | collective-permute-start | bytes 6291464 | tf_op jit(solution)/shard_map/ppermute | solution.py:623
  551.0 9.5 %collective-permute-start.23 = (bf16[2,32,3072]{2,1,0:T(8,128)(2,1)S(1)}, bf16[2,32,3072]{2,1,0:T(8,128)(2,1)S(1)}, u32[]{:S(2)}, u32[]{:S(2)}) collective-permute-start(bf16[2,32,3072]{2,1,0:T(8,128)(2,1)S(1)} %dynamic-slice_bitcast_fusion.7), channel_id=1, source_target_pairs={{0,8},{2,10},{4,12},{6,14},{8,0},{10,2},{12,4},{14,6},{16,24},{18,... | collective-permute-start | bytes 1179656 | tf_op jit(solution)/shard_map/ppermute | solution.py:623
  560.6 9.5 %collective-permute-start.24 = (bf16[32,3072]{1,0:T(8,128)(2,1)S(1)}, bf16[32,3072]{1,0:T(8,128)(2,1)S(1)}, u32[]{:S(2)}, u32[]{:S(2)}) collective-permute-start(bf16[32,3072]{1,0:T(8,128)(2,1)S(1)} %dynamic-slice_bitcast_fusion.11), channel_id=1, source_target_pairs={{0,16},{2,18},{4,20},{6,22},{8,24},{10,26},{12,28},{14,30},{16,0},... | collective-permute-start | bytes 589832 | tf_op jit(solution)/shard_map/ppermute | solution.py:623
  564.3 44.1 %collective-permute-start.31 = (bf16[2,2,2,32,4096]{4,3,2,1,0:T(8,128)(2,1)S(1)}, bf16[2,2,2,32,4096]{4,3,2,1,0:T(8,128)(2,1)S(1)}, u32[]{:S(2)}, u32[]{:S(2)}) collective-permute-start(bf16[2,2,2,32,4096]{4,3,2,1,0:T(8,128)(2,1)S(1)} %dynamic-slice_bitcast_fusion.1), channel_id=1, source_target_pairs={{0,2},{2,0},{4,6},{6,4},{8,10},{10,8},{12,14},{14,12},{16,18},{18,... | collective-permute-start | bytes 6291464 | tf_op jit(solution)/shard_map/ppermute | solution.py:623
  595.7 24.4 %collective-permute-start.37 = (bf16[2,2,32,4096]{3,2,1,0:T(8,128)(2,1)S(1)}, bf16[2,2,32,4096]{3,2,1,0:T(8,128)(2,1)S(1)}, u32[]{:S(2)}, u32[]{:S(2)}) collective-permute-start(bf16[2,2,32,4096]{3,2,1,0:T(8,128)(2,1)S(1)} %dynamic-slice_bitcast_fusion.2), channel_id=1, source_target_pairs={{0,8},{2,10},{4,12},{6,14},{8,0},{10,2},{12,4},{14,6},{16,24},{18,... | collective-permute-start | bytes 3145736 | tf_op jit(solution)/shard_map/ppermute | solution.py:623
  609.4 20.7 %collective-permute-start.32 = (bf16[2,2,32,4096]{3,2,1,0:T(8,128)(2,1)S(1)}, bf16[2,2,32,4096]{3,2,1,0:T(8,128)(2,1)S(1)}, u32[]{:S(2)}, u32[]{:S(2)}) collective-permute-start(bf16[2,2,32,4096]{3,2,1,0:T(8,128)(2,1)S(1)} %dynamic-slice_bitcast_fusion.3), channel_id=1, source_target_pairs={{0,4},{2,6},{4,0},{6,2},{8,12},{10,14},{12,8},{14,10},{16,20},{18,... | collective-permute-start | bytes 3145736 | tf_op jit(solution)/shard_map/ppermute | solution.py:623
  620.5 12.3 %collective-permute-start.38 = (bf16[2,32,4096]{2,1,0:T(8,128)(2,1)S(1)}, bf16[2,32,4096]{2,1,0:T(8,128)(2,1)S(1)}, u32[]{:S(2)}, u32[]{:S(2)}) collective-permute-start(bf16[2,32,4096]{2,1,0:T(8,128)(2,1)S(1)} %dynamic-slice_bitcast_fusion.5), channel_id=1, source_target_pairs={{0,2},{2,0},{4,6},{6,4},{8,10},{10,8},{12,14},{14,12},{16,18},{18,... | collective-permute-start | bytes 1572872 | tf_op jit(solution)/shard_map/ppermute | solution.py:623
  630.4 15.3 %collective-permute-start.33 = (bf16[2,32,4096]{2,1,0:T(8,128)(2,1)S(1)}, bf16[2,32,4096]{2,1,0:T(8,128)(2,1)S(1)}, u32[]{:S(2)}, u32[]{:S(2)}) collective-permute-start(bf16[2,32,4096]{2,1,0:T(8,128)(2,1)S(1)} %dynamic-slice_bitcast_fusion.6), channel_id=1, source_target_pairs={{0,8},{2,10},{4,12},{6,14},{8,0},{10,2},{12,4},{14,6},{16,24},{18,... | collective-permute-start | bytes 1572872 | tf_op jit(solution)/shard_map/ppermute | solution.py:623
  633.0 17.1 %collective-permute-start.39 = (bf16[32,4096]{1,0:T(8,128)(2,1)S(1)}, bf16[32,4096]{1,0:T(8,128)(2,1)S(1)}, u32[]{:S(2)}, u32[]{:S(2)}) collective-permute-start(bf16[32,4096]{1,0:T(8,128)(2,1)S(1)} %dynamic-slice_bitcast_fusion.8), channel_id=1, source_target_pairs={{0,16},{2,18},{4,20},{6,22},{8,24},{10,26},{12,28},{14,30},{16,0},... | collective-permute-start | bytes 786440 | tf_op jit(solution)/shard_map/ppermute | solution.py:623
  645.8 10.7 %collective-permute-start.34 = (bf16[32,4096]{1,0:T(8,128)(2,1)S(1)}, bf16[32,4096]{1,0:T(8,128)(2,1)S(1)}, u32[]{:S(2)}, u32[]{:S(2)}) collective-permute-start(bf16[32,4096]{1,0:T(8,128)(2,1)S(1)} %dynamic-slice_bitcast_fusion.9), channel_id=1, source_target_pairs={{0,16},{2,18},{4,20},{6,22},{8,24},{10,26},{12,28},{14,30},{16,0},... | collective-permute-start | bytes 786440 | tf_op jit(solution)/shard_map/ppermute | solution.py:623
  (21 other events, 146.9 us)
Sparse Core Ops, SparseCore 0:
  11.5 163.5 all-gather.4
  377.0 81.7 all-gather.6

commit v3 on v2

--- a/solution.py
+++ b/solution.py
@@ -43,6 +43,46 @@
     return pl.CostEstimate(flops=int(flops), bytes_accessed=int(size), transcendentals=int(exps))
 
 
+awaited, done = [], []
+
+
+def await_all(*values):
+    awaited.extend(values)
+
+
+def launch(kernel, grid_spec=None, grid=None, in_specs=None, out_specs=None, out_shape=None, **others):
+    spec = grid_spec or dict(num_scalar_prefetch=0, grid=grid, in_specs=in_specs, out_specs=out_specs)
+    waits = tuple(awaited)
+    awaited.clear()
+    given = spec["num_scalar_prefetch"] + len(spec["in_specs"])
+    single = not isinstance(out_shape, (list, tuple))
+    outs = [spec["out_specs"]] if single else list(spec["out_specs"])
+    shapes = [out_shape] if single else list(out_shape)
+
+    def body(*refs):
+        mark = refs[given + len(waits)]
+        mark[...] = jnp.zeros_like(mark)
+        kernel(*refs[:given], *refs[given + len(waits) + 1 :])
+
+    zeros = lambda *_: (0, 0)
+    spec = dict(
+        spec,
+        in_specs=list(spec["in_specs"]) + [pl.BlockSpec(memory_space=pl.ANY)] * len(waits),
+        out_specs=[pl.BlockSpec((8, PAIR), zeros)] + outs,
+    )
+    shapes = [jax.ShapeDtypeStruct((8, PAIR), F32)] + shapes
+    call = pl.pallas_call(
+        body, grid_spec=pltpu.PrefetchScalarGridSpec(**spec), out_shape=shapes, **others
+    )
+
+    def run(*args):
+        mark, *result = call(*args, *waits)
+        done[:] = [mark]
+        return result[0] if single else result
+
+    return run
+
+
 def head_ones(dtype=BF):
     row = lax.broadcasted_iota(jnp.int32, (PAIR, PAIR), 0) // HEAD
     column = lax.broadcasted_iota(jnp.int32, (PAIR, PAIR), 1) // HEAD
@@ -65,12 +105,132 @@
     return centred * rstd, rstd
 
 
-def qkv_kernel(places, tokens, member, modulation, *refs, pieces):
-    weights, (scale, hidden, q, k, v, rq, rk, ordered) = refs[: 3 * pieces], refs[3 * pieces :]
+def modulation_kernel(device, *refs, order, slots, rows, own, width):
+    *tables, ada, class_vec, lifted, labels, modulation = refs
+    me = device[0]
+    held = tables[0].shape[0]
+    count = rows * (held // own)
+    total = count * len(tables)
+    iota = lambda shape, axis: lax.broadcasted_iota(jnp.int32, shape, axis)
+
+    def place_of(owner):
+        return relative_place(owner, me, order) if len(tables) == 2 else owner
+
+    for index, table in enumerate(tables):
+        at = (iota((count, held), 0) // rows) * own
+        row = iota((count, held), 1)
+        edge = table[:, width:]
+        pick = lambda x: nn(jnp.where(row == x, 1.0, 0.0).astype(BF), edge)
+        both = 256.0 * pick(at) + pick(at + 1)
+        slot = iota(both.shape, 0) % rows
+        mine = (iota(both.shape, 1) == slot) & (slot < slots)
+        label = jnp.sum(jnp.where(mine, both, 0.0), axis=1, keepdims=True).astype(jnp.int32)
+        place = place_of(label // own) * own + label % own
+        place = jnp.where((iota(place.shape, 0) % rows) < slots, place, -1)
+        vec = jnp.zeros((count, width), F32)
+        for other, source in enumerate(tables):
+            vec += nn(jnp.where(place - other * held == row, 1.0, 0.0).astype(BF), source[:, :width])
+        here = slice(index * count, (index + 1) * count)
+        class_vec[here, :] = vec.astype(BF)
+        label = jnp.where((iota(label.shape, 0) % rows) < slots, label, -1)
+        labels[here, :] = jnp.broadcast_to(label, (count, PAIR))
+        lifted[here, :] = (vec / (1.0 + jnp.exp(-vec))).astype(BF)
+    slot = iota((total, total), 0)
+    wanted = place_of(slot // rows) * rows + slot % rows
+    swap = jnp.where(wanted == iota((total, total), 1), 1.0, 0.0).astype(BF)
+    modulation[...] = nn(nn(swap, lifted[...]).astype(BF), ada[...])
+
+
+def modulation_call(device, tables, ada, order, slots, rows, own):
+    width = ada.shape[0]
+    total = rows * (tables[0].shape[0] // own) * len(tables)
+    whole = lambda shape: pl.BlockSpec(shape, lambda s, d: (0, 0))
+    shapes = [(total, width), (total, width), (total, PAIR), (total, ada.shape[1])]
+    return launch(
+        functools.partial(
+            modulation_kernel, order=order, slots=slots, rows=rows, own=own, width=width
+        ),
+        grid_spec=dict(
+            num_scalar_prefetch=1,
+            grid=(1,),
+            in_specs=[whole(t.shape) for t in tables] + [whole(ada.shape)],
+            out_specs=[whole(s) for s in shapes],
+        ),
+        out_shape=[jax.ShapeDtypeStruct(s, d) for s, d in zip(shapes, (BF, BF, jnp.int32, F32))],
+        compiler_params=params(),
+        cost_estimate=cost(6 * total * width * width, 8 * width * width),
+        name="modulation",
+    )(device, *tables, ada)
+
+
+def ada_kernel(flags, *refs, devices, order):
+    early, *lates, lifted, class_vec, labels, ada, scale, ada_grad, outgoing = refs
+    own, width = outgoing.shape[1] - scale.shape[0], lifted.shape[1]
+    share = width // devices
+    size = max(share, PAIR)
+    row = lax.broadcasted_iota(jnp.int32, (width, size), 0)
+    lane = lax.broadcasted_iota(jnp.int32, (width, size), 1)
+    pick = jnp.where((row == flags[0] * share + lane) & (lane < share), 1.0, 0.0).astype(BF)
+    own_lifted = nn(lifted[...], pick).astype(BF)
+    own_vec = nn(class_vec[...], pick)[:, :share]
+    slots = early.shape[0]
+    slot = lax.broadcasted_iota(jnp.int32, (slots, slots), 1)
+    rows = slots // devices
+    place = relative_place(slot // rows, flags[0], order) * rows + slot % rows
+    place_of = lax.broadcasted_iota(jnp.int32, (slots, slots), 0)
+    early_grad = nn(jnp.where(place == place_of, 1.0, 0.0).astype(BF), early[...]).astype(BF)
+    late_grad = jnp.concatenate([late[...] for late in lates], axis=0)
+    cut = lambda x, i: x[:, i * width : (i + 1) * width]
+    grad = jnp.concatenate(
+        [cut(early_grad, 0), cut(early_grad, 1), cut(late_grad, 0)]
+        + [cut(early_grad, 2), cut(late_grad, 1), cut(early_grad, 3)],
+        axis=1,
+    )
+    total = tn(own_lifted, grad)
+    ada_grad[...] = total[:share]
+    gate = 1.0 / (1.0 + jnp.exp(-own_vec))
+    grad = nt(grad, ada[...]) * (gate * (1.0 + own_vec * (1.0 - gate)))
+    classes = devices * own
+    column = lax.broadcasted_iota(jnp.int32, (slots, classes), 1)
+    hot = jnp.where(labels[:, 0:1] == column, 1.0, 0.0).astype(BF)
+    high, low = halves(grad)
+    least = (grad - high.astype(F32) - low.astype(F32)).astype(BF)
+    table = tn(hot, high) + tn(hot, low) + tn(hot, least)
+    for device in range(devices):
+        outgoing[device, :own, :] = table[device * own : (device + 1) * own]
+        outgoing[device, own:, :] = scale[...]
+
+
+def ada_call(flags, early, lates, lifted, class_vec, labels, ada, scale, devices, order):
+    own, width = ada.shape[0], lifted.shape[1]
+    whole = lambda x: pl.BlockSpec(x.shape, lambda s, f: (0,) * len(x.shape))
+    shapes = [
+        jax.ShapeDtypeStruct(ada.shape, F32),
+        jax.ShapeDtypeStruct((devices, own + scale.shape[0], width // devices), F32),
+    ]
+    args = (early, *lates, lifted, class_vec, labels, ada, scale)
+    return launch(
+        functools.partial(ada_kernel, devices=devices, order=order),
+        grid_spec=dict(
+            num_scalar_prefetch=1,
+            grid=(1,),
+            in_specs=[whole(x) for x in args],
+            out_specs=[whole(x) for x in shapes],
+        ),
+        out_shape=shapes,
+        compiler_params=params(),
+        cost_estimate=cost(10**9, 10**7),
+        name="adaptive_norm_backward",
+    )(flags, *args)
+
+
+def qkv_kernel(places, tokens, member, modulation, *refs, pieces, parts):
+    weights, (scale, hidden, q, k, v, rq, rk, ordered) = refs[: pieces * parts], refs[pieces * parts :]
     step = pl.program_id(0)
     width = tokens.shape[1]
     block = ordered.shape[1]
     per = width // block
+    share = 3 * per // parts
     rows = 256
 
     @pl.when(step == 0)
@@ -82,61 +242,64 @@
             sh = nn(member[here, :], modulation[:, 4 * width : 5 * width])
             hidden[here, :] = (unit * (1.0 + sc) + sh).astype(BF)
 
+    for part in range(parts):
+
+        @pl.when((step >= part * share) & (step < (part + 1) * share))
+        def _():
+            if pieces == 1:
+                ordered[...] = weights[part][...]
+                return
+            own, other = weights[2 * part : 2 * part + 2]
+            owners = places.shape[1]
+            size = width // owners
+            for owner in range(owners):
+                place = places[part, owner]
+                second = place >= owners // 2
+                at = pl.multiple_of((place - jnp.where(second, owners // 2, 0)) * size, size)
+                put = slice(owner * size, (owner + 1) * size)
+
+                @pl.when(jnp.logical_not(second))
+                def _():
+                    ordered[put, :] = own[pl.ds(at, size), :]
+
+                @pl.when(second)
+                def _():
+                    ordered[put, :] = other[pl.ds(at, size), :]
+
     for which in range(3):
 
         @pl.when((step >= which * per) & (step < (which + 1) * per))
         def _():
-            if pieces == 1:
-                ordered[...] = weights[which][...]
-            else:
-                own, other = weights[2 * which : 2 * which + 2]
-                owners = places.shape[1]
-                size = width // owners
-                for owner in range(owners):
-                    place = places[which, owner]
-                    at = pl.multiple_of((place // 2) * size, size)
-                    put = slice(owner * size, (owner + 1) * size)
-
-                    @pl.when(place % 2 == 0)
-                    def _():
-                        ordered[put, :] = own[pl.ds(at, size), :]
-
-                    @pl.when(place % 2 == 1)
-                    def _():
-                        ordered[put, :] = other[pl.ds(at, size), :]
-
             for at in range(0, tokens.shape[0], rows):
                 here = pl.ds(at, rows)
                 out = nn(hidden[here, :], ordered[...])
+                if which < 2:
+                    r = lax.rsqrt(head_sums(out * out) + NORM_EPS)
+                    (rq, rk)[which][here, :] = r.astype(BF)
+                    out = out * r
                 if which == 0:
-                    r = lax.rsqrt(head_sums(out * out) + NORM_EPS)
-                    rq[here, :] = r.astype(BF)
-                    q[here, :] = (out * r * scale[0:1, :]).astype(BF)
-                if which == 1:
-                    r = lax.rsqrt(head_sums(out * out) + NORM_EPS)
-                    rk[here, :] = r.astype(BF)
-                    k[here, :] = (out * r).astype(BF)
-                if which == 2:
-                    v[here, :] = out.astype(BF)
+                    out = out * scale[0:1, :]
+                (q, k, v)[which][here, :] = out.astype(BF)
 
 
 def qkv_call(places, tokens, member, modulation, weights, scale_lanes, block=512):
     count, width = tokens.shape
     per = width // block
-    pieces = len(weights[0])
-    part = lambda rows, which: pl.BlockSpec(
-        (rows, block), lambda s, p: (0, jnp.clip(s - which * per, 0, per - 1))
+    pieces, parts = len(weights[0]), len(weights)
+    share = 3 * per // parts
+    column = lambda rows, first, number: pl.BlockSpec(
+        (rows, block), lambda s, p: (0, jnp.clip(s - first, 0, number - 1))
     )
     whole = lambda x: pl.BlockSpec(x.shape, lambda s, p: (0, 0))
-    columns = [part(count, i) for i in range(3)]
-    return pl.pallas_call(
-        functools.partial(qkv_kernel, pieces=pieces),
-        grid_spec=pltpu.PrefetchScalarGridSpec(
+    columns = [column(count, i * per, per) for i in range(3)]
+    return launch(
+        functools.partial(qkv_kernel, pieces=pieces, parts=parts),
+        grid_spec=dict(
             num_scalar_prefetch=1,
             grid=(3 * per,),
             in_specs=[whole(tokens), whole(member), whole(modulation)]
-            + [part(w.shape[0], i) for i in range(3) for w in weights[i]]
-            + [part(8, 0)],
+            + [column(w.shape[0], i * share, share) for i in range(parts) for w in weights[i]]
+            + [column(8, 0, per)],
             out_specs=[pl.BlockSpec((count, width), lambda s, p: (0, 0))]
             + columns
             + columns[:2]
@@ -210,9 +373,9 @@
     column = pl.BlockSpec((count, lanes), lambda g, s: (0, g))
     edge = pl.BlockSpec((count, 1), lambda g, s: (0, 0))
     heads = width // HEAD
-    return pl.pallas_call(
+    return launch(
         functools.partial(attn_fwd_kernel, qb=qb, kb=kb),
-        grid_spec=pltpu.PrefetchScalarGridSpec(
+        grid_spec=dict(
             num_scalar_prefetch=1,
             grid=(heads // GROUP,),
             in_specs=[column, column, column, edge, edge],
@@ -294,29 +457,35 @@
     dv[...] = dv_acc[...].astype(BF)
 
 
-def attn_bwd_call(span, q, k, v, do, start, end, inverse, delta, rq, rk, scale_lanes, qb=256, kb=256):
+def attn_bwd_call(
+    span, q, k, v, do, start, end, inverse, delta, rq, rk, scale_lanes, first, groups, qb=256, kb=256
+):
     count, width = q.shape
     lanes = GROUP * HEAD
-    column = pl.BlockSpec((count, lanes), lambda g, s: (0, g))
-    edge = pl.BlockSpec((8, count), lambda g, s: (0, 0))
-    row = pl.BlockSpec((1, 8, count), lambda g, s: (g, 0, 0))
-    small = pl.BlockSpec((8, lanes), lambda g, s: (0, g))
-    heads = width // HEAD
-    return pl.pallas_call(
+    column = pl.BlockSpec((count, lanes), lambda g, s: (0, first + g))
+    edge = pl.BlockSpec((1, count), lambda g, s: (0, 0))
+    row = pl.BlockSpec((1, 8, count), lambda g, s: (first + g, 0, 0))
+    out = pl.BlockSpec((count, lanes), lambda g, s: (0, g))
+    heads = groups * GROUP
+    return launch(
         functools.partial(attn_bwd_kernel, qb=qb, kb=kb),
-        grid_spec=pltpu.PrefetchScalarGridSpec(
+        grid_spec=dict(
             num_scalar_prefetch=1,
-            grid=(heads // GROUP,),
-            in_specs=[column] * 4 + [edge] * 2 + [row] * 2 + [column] * 2 + [small],
-            out_specs=[column] * 3 + [small],
+            grid=(groups,),
+            in_specs=[column] * 4
+            + [edge] * 2
+            + [row] * 2
+            + [column] * 2
+            + [pl.BlockSpec((8, lanes), lambda g, s: (0, first + g))],
+            out_specs=[out] * 3 + [pl.BlockSpec((8, lanes), lambda g, s: (0, g))],
             scratch_shapes=[pltpu.VMEM((GROUP, count, PAIR), BF)] * 3
             + [pltpu.VMEM((qb, lanes), F32)]
             + [pltpu.VMEM((count, lanes), F32)] * 2,
         ),
-        out_shape=[jax.ShapeDtypeStruct((count, width), BF)] * 3
-        + [jax.ShapeDtypeStruct((8, width), F32)],
+        out_shape=[jax.ShapeDtypeStruct((count, groups * lanes), BF)] * 3
+        + [jax.ShapeDtypeStruct((8, groups * lanes), F32)],
         compiler_params=params(),
-        cost_estimate=cost(40 * count * count * heads * HEAD, 18 * count * width, heads * count * count),
+        cost_estimate=cost(40 * count * count * heads * HEAD, 18 * count * heads * HEAD, heads * count * count),
         name="attention_backward",
     )(span, q, k, v, do, start, end, inverse, delta, rq, rk, scale_lanes)
 
@@ -337,7 +506,7 @@
     count, width = tokens.shape
     some = pl.BlockSpec((rows, width), lambda s: (s, 0))
     whole = lambda x: pl.BlockSpec(x.shape, lambda s: (0, 0))
-    return pl.pallas_call(
+    return launch(
         proj_kernel,
         grid=(count // rows,),
         in_specs=[
@@ -374,7 +543,7 @@
     grads = refs[2:-3]
     active, grad, turned = refs[-3:]
     step = pl.program_id(0)
-    odd = core[0] == 1
+    odd = core[1] == 1
 
     @pl.when(step == 0)
     def _():
@@ -404,25 +573,28 @@
         grads[0][...] = nn(turned[...], grad[...]).astype(BF)
 
 
-def mlp_call(core, hidden, down, packed, own, split, block=512, rows=256):
+def mlp_call(core, hidden, down, packed, own, split, first, count_of, block=512, rows=256):
     count, width = hidden.shape
     units = (packed.shape[1] - width) // 2
     per = width // block
     whole = pl.BlockSpec((count, width), lambda s, c: (0, 0))
-    first_up, first_down = width // block, (width + units) // width
-    wide = lambda n, first: pl.BlockSpec((n, block), lambda s, c: (0, first + s))
-    tall = lambda n, first: pl.BlockSpec((n, width), lambda s, c: (s % per, first + s // per))
+    first_up, first_down = width // block + first * per, (width + units) // width + first
     kept = 2 if split else 1
     copies = 2 if split else 1
-    return pl.pallas_call(
+    wide = pl.BlockSpec((width // kept, block), lambda s, c: (0, s))
+    tall = pl.BlockSpec((block // kept, width), lambda s, c: (s % per, s // per))
+    return launch(
         functools.partial(mlp_kernel, rows=rows, own=own),
-        grid_spec=pltpu.PrefetchScalarGridSpec(
+        grid_spec=dict(
             num_scalar_prefetch=1,
-            grid=(units // block,),
-            in_specs=[whole, whole, wide(width, first_up), tall(block, first_down)],
-            out_specs=[whole, whole]
-            + [wide(width // kept, 0)] * copies
-            + [tall(block // kept, 0)] * copies,
+            grid=(count_of * per,),
+            in_specs=[
+                whole,
+                whole,
+                pl.BlockSpec((width, block), lambda s, c: (0, first_up + s)),
+                pl.BlockSpec((block, width), lambda s, c: (s % per, first_down + s // per)),
+            ],
+            out_specs=[whole, whole] + [wide] * copies + [tall] * copies,
             scratch_shapes=[
                 pltpu.VMEM((count, block), BF),
                 pltpu.VMEM((count, block), BF),
@@ -430,9 +602,9 @@
             ],
         ),
         out_shape=[jax.ShapeDtypeStruct((count, width), F32)] * 2
-        + [jax.ShapeDtypeStruct((width // kept, units), BF)] * (2 * copies),
+        + [jax.ShapeDtypeStruct((width // kept, count_of * width), BF)] * (2 * copies),
         compiler_params=params(),
-        cost_estimate=cost(12 * count * width * units, 8 * width * units + 12 * count * width),
+        cost_estimate=cost(12 * count * width * width * count_of, 20 * count * width),
         name="feed_forward",
     )(core, hidden, down, packed, packed)
 
@@ -448,14 +620,15 @@
 
 
 def middle_kernel(
-    mlp, back, after, cotangent, branch, mixed, rest, member, turned, modulation, weight,
+    mlp_sum, back, after, cotangent, branch, mixed, rest, member, turned, modulation, weight,
     output, grad_in, branch_grad, mixed_grad, delta, sums,
 ):
     width = after.shape[1]
     part = lambda i: nn(member[...], modulation[:, i * width : (i + 1) * width])
     upstream = cotangent[...].astype(F32)
     v = after[...]
-    output[...] = (v + part(1) * mlp[...]).astype(BF)
+    mlp = mlp_sum[...]
+    output[...] = (v + part(1) * mlp).astype(BF)
     g = back[...]
     unit, rstd = centre(v)
     total = upstream + norm_back(unit, rstd, g * (1.0 + part(3)))
@@ -476,7 +649,7 @@
     def _():
         sums[...] = jnp.zeros_like(sums)
 
-    for i, x in enumerate((total * branch[...].astype(F32), upstream * mlp[...], g * unit, g)):
+    for i, x in enumerate((total * branch[...].astype(F32), upstream * mlp, g * unit, g)):
         sums[:, i * width : (i + 1) * width] += item_sums(turned[...], x)
 
 
@@ -486,7 +659,7 @@
     whole = lambda x: pl.BlockSpec(x.shape, lambda s: (0, 0))
     items = turned.shape[0]
     heads = 8 * (width // HEAD // GROUP)
-    return pl.pallas_call(
+    return launch(
         middle_kernel,
         grid=(count // rows,),
         in_specs=[some] * 7
@@ -512,13 +685,13 @@
     )(mlp, back, after, cotangent, branch, mixed, rest, member, turned, modulation, weight)
 
 
-def first_kernel(dq, dk, dv, weight, tokens, grad_in, member, turned, modulation, tokens_grad, sums):
+def first_kernel(*refs):
+    *parts, weight, tokens, grad_in, member, turned, modulation, tokens_grad, sums = refs
     width = tokens.shape[1]
-    g = (
-        nt(dq[...], weight[:, :width])
-        + nt(dk[...], weight[:, width : 2 * width])
-        + nt(dv[...], weight[:, 2 * width :])
-    )
+    g, at = 0.0, 0
+    for part in parts:
+        g = g + nt(part[...], weight[:, at : at + part.shape[1]])
+        at += part.shape[1]
     unit, rstd = centre(tokens[...].astype(F32))
     sc = nn(member[...], modulation[:, 2 * width : 3 * width])
     tokens_grad[...] = (grad_in[...] + norm_back(unit, rstd, g * (1.0 + sc))).astype(BF)
@@ -531,17 +704,17 @@
         sums[:, i * width : (i + 1) * width] += item_sums(turned[...], x)
 
 
-def first_call(dq, dk, dv, weight, tokens, grad_in, member, turned, modulation, rows=256):
+def first_call(parts, weight, tokens, grad_in, member, turned, modulation, rows=256):
     count, width = tokens.shape
     some = pl.BlockSpec((rows, width), lambda s: (s, 0))
     whole = lambda x: pl.BlockSpec(x.shape, lambda s: (0, 0))
     items = turned.shape[0]
-    return pl.pallas_call(
+    return launch(
         first_kernel,
         grid=(count // rows,),
-        in_specs=[some] * 3
+        in_specs=[pl.BlockSpec((rows, p.shape[1]), lambda s: (s, 0)) for p in parts]
         + [
-            whole(weight),
+            pl.BlockSpec((width, 3 * width), lambda s: (0, 0)),
             some,
             some,
             pl.BlockSpec((rows, member.shape[1]), lambda s: (s, 0)),
@@ -556,58 +729,66 @@
         compiler_params=params(),
         cost_estimate=cost(6 * count * width * width, 18 * count * width),
         name="first_norm_backward",
-    )(dq, dk, dv, weight, tokens, grad_in, member, turned, modulation)
-
-
-def weight_grad_kernel(core, *refs, rows, count):
-    split = (len(refs) - 2 - count) == 2
-    x = refs[0]
-    ys = refs[1 : 1 + count]
-    outs = refs[1 + count : -1]
-    turned = refs[-1]
+    )(*parts, weight, tokens, grad_in, member, turned, modulation)
+
+
+def weight_grad_kernel(core, *refs, rows, starts):
+    jobs = len(starts) - 1
+    xs, ys = refs[:jobs], refs[jobs : jobs + starts[-1][1]]
+    outs, turned = refs[jobs + starts[-1][1] : -1], refs[-1]
     step = pl.program_id(0)
-    per = pl.num_programs(0) // count
-
-    @pl.when(step == 0)
-    def _():
-        turned[...] = jnp.transpose(x[...])
-
-    for which in range(count):
-
-        @pl.when((step >= which * per) & (step < (which + 1) * per))
+    for job in range(jobs):
+
+        @pl.when(step == starts[job][0])
         def _():
-            result = nn(turned[...], ys[which][...])
-            if split:
-                split_blocks(core[0] == 1, result, rows, outs[0], outs[1])
-            else:
-                outs[0][...] = result.astype(BF)
-
-
-def weight_grad_call(core, x, ys, rows, split, block=512):
-    count, width = x.shape
-    columns = ys[0].shape[1]
-    per = columns // block
-    steps = per * len(ys)
+            turned[...] = jnp.transpose(xs[job][...])
+
+        (begin, first), (end, last) = starts[job], starts[job + 1]
+        per = (end - begin) // (last - first)
+        for which in range(first, last):
+            at = begin + (which - first) * per
+
+            @pl.when((step >= at) & (step < at + per))
+            def _():
+                result = nn(turned[...], ys[which][...])
+                if len(outs) == 2:
+                    split_blocks(core[1] == 1, result, rows, outs[0], outs[1])
+                else:
+                    outs[0][...] = result.astype(BF)
+
+
+def weight_grad_call(core, jobs, rows, split, block=512):
+    count, width = jobs[0][0].shape
+    starts, specs = [(0, 0)], []
+    for _, ys in jobs:
+        begin, number = starts[-1]
+        for y in ys:
+            per = y.shape[1] // block
+            specs.append(
+                pl.BlockSpec(
+                    (count, block), lambda s, c, at=begin, per=per: (0, jnp.clip(s - at, 0, per - 1))
+                )
+            )
+            begin, number = begin + per, number + 1
+        starts.append((begin, number))
+    steps = starts[-1][0]
+    columns = steps * block
     wide = lambda n: pl.BlockSpec((n, block), lambda s, c: (0, s))
-    shapes = [(width // 2, columns * len(ys))] * 2 if split else [(width, columns * len(ys))]
-    part = lambda which: pl.BlockSpec(
-        (count, block), lambda s, c: (0, jnp.clip(s - which * per, 0, per - 1))
-    )
-    return pl.pallas_call(
-        functools.partial(weight_grad_kernel, rows=rows, count=len(ys)),
-        grid_spec=pltpu.PrefetchScalarGridSpec(
+    shapes = [(width // 2, columns)] * 2 if split else [(width, columns)]
+    return launch(
+        functools.partial(weight_grad_kernel, rows=rows, starts=tuple(starts)),
+        grid_spec=dict(
             num_scalar_prefetch=1,
             grid=(steps,),
-            in_specs=[pl.BlockSpec((count, width), lambda s, c: (0, 0))]
-            + [part(i) for i in range(len(ys))],
+            in_specs=[pl.BlockSpec((count, width), lambda s, c: (0, 0)) for _ in jobs] + specs,
             out_specs=[wide(shape[0]) for shape in shapes],
             scratch_shapes=[pltpu.VMEM((width, count), BF)],
         ),
         out_shape=[jax.ShapeDtypeStruct(s, BF) for s in shapes],
         compiler_params=params(),
-        cost_estimate=cost(2 * count * width * columns * len(ys), 4 * count * columns * len(ys)),
+        cost_estimate=cost(2 * count * width * columns, 4 * count * columns),
         name="weight_grad",
-    )(core, x, *ys)
+    )(core, *[x for x, _ in jobs], *[y for _, ys in jobs for y in ys])
 
 
 BOTH = ("wide", "narrow")
@@ -630,54 +811,159 @@
     return turning[turn:] + turning[:turn] + last
 
 
-def sum_to_owners(block, dims, order, sizes):
-    dims = list(dims)
-    for step, (axis, bit) in enumerate(order):
-        at = dims.index((axis, bit))
-        dims.pop(at)
-        mine = (lax.axis_index(axis) >> bit) & 1
-        sent = lax.dynamic_index_in_dim(block, 1 - mine, at, keepdims=False)
-        kept = lax.dynamic_index_in_dim(block, mine, at, keepdims=False)
-        got = flip(sent, axis, sizes[axis], bit)
-        block = kept.astype(F32) + got.astype(F32)
-        if step < len(order) - 1:
-            block = block.astype(BF)
-    return block
-
-
-def scatter_sum(parts, sizes, turn):
-    wide, narrow = sizes["wide"], sizes["narrow"]
-    dims = [("wide", b) for b in reversed(range(bit_count(wide)))]
-    dims += [("narrow", b) for b in reversed(range(bit_count(narrow)))]
-    order = [("narrow", b) for b in range(bit_count(narrow))]
-    order += [("wide", b) for b in chip_order(wide, turn)]
-    if len(parts) == 2:
-        kept, sent = parts
-        got = flip(sent, "narrow", narrow, 0)
-        block = (kept.astype(F32) + got.astype(F32)).astype(BF)
-        dims.remove(("narrow", 0))
-        order = order[1:]
-    else:
-        (block,) = parts
-    own = block.shape[0] // 2 ** len(dims)
-    return sum_to_owners(block.reshape((2,) * len(dims) + (own, block.shape[1])), dims, order, sizes)
-
-
-def gather_halves(shard, sizes, order):
-    block = shard[None]
-    for bit in order:
-        got = flip(block, "wide", sizes["wide"], bit)
-        block = jnp.concatenate([block, got], axis=0)
-    block = block.reshape(-1, shard.shape[1])
-    return block, flip(block, "narrow", sizes["narrow"], 0)
+def halving_kernel(flags, *refs):
+    number = len(refs) // 6
+    inputs, outs = refs[: 4 * number], refs[4 * number :]
+    for i in range(number):
+        kept_here, got_here, kept_there, got_there = inputs[4 * i : 4 * i + 4]
+        kept, sent = outs[2 * i : 2 * i + 2]
+        add = lambda x, y: (x[:, 0].astype(F32) + y[:, 0].astype(F32)).astype(BF)
+        sent[...] = add(kept_there, got_there)
+        kept[...] = add(kept_here, got_here)
+
+
+class Chain:
+    def __init__(self, kept, got, sizes, turn, columns=None, index=0):
+        self.kept, self.got, self.index = kept, got, index
+        self.columns, self.wide = columns or kept.shape[1], sizes["wide"]
+        self.dims = list(reversed(range(bit_count(self.wide))))
+        self.order = chip_order(self.wide, turn)
+
+
+def finish_kernel(*refs, blocks):
+    number = len(refs) // 3
+    for index, (kept, got, out) in enumerate(
+        zip(refs[:number], refs[number : 2 * number], refs[2 * number :])
+    ):
+        total = kept[...].astype(F32) + got[...].astype(F32)
+        if not blocks:
+            out[...] = total
+            continue
+        own = total.shape[0]
+        width = total.shape[1] // blocks
+        if index == 0:
+            for owner in range(width // own):
+                at = [i * width + owner * own for i in range(blocks)]
+                out[:, owner * own * blocks : (owner + 1) * own * blocks] = jnp.concatenate(
+                    [total[:, x : x + own] for x in at], axis=1
+                )
+        else:
+            for i in range(blocks):
+                out[i * own : (i + 1) * own, :] = total[:, i * width : (i + 1) * width]
+
+
+def finish(chains, blocks=0):
+    whole = lambda x: pl.BlockSpec(x.shape, lambda s: (0, 0))
+    kept, got = [c.kept for c in chains], [c.got for c in chains]
+    shapes = [jax.ShapeDtypeStruct(x.shape, F32) for x in kept]
+    if blocks:
+        rows, columns = shapes[1].shape
+        shapes[1] = jax.ShapeDtypeStruct((rows * blocks, columns // blocks), F32)
+    size = sum(x.size for x in kept)
+    return launch(
+        functools.partial(finish_kernel, blocks=blocks),
+        grid=(1,),
+        in_specs=[whole(x) for x in (*kept, *got)],
+        out_specs=[whole(x) for x in shapes],
+        out_shape=shapes,
+        compiler_params=params(),
+        cost_estimate=cost(size, 8 * size),
+        name="last_sum",
+    )(*kept, *got)
+
+
+def halve(flags, chains, steps):
+    specs, args, outs, shapes = [], [], [], []
+    for chain in chains:
+        bit = chain.order.pop(0)
+        at = chain.dims.index(bit)
+        chain.dims.pop(at)
+        chain.bit = bit
+        lead, rows = 2**at, chain.kept.shape[0] // 2 ** (at + 1)
+        over = min(lead, steps)
+        within = steps // over
+        block = (lead // over, rows // within, chain.columns)
+        which, index = bit, chain.index
+        spec = lambda flip: pl.BlockSpec(
+            (block[0], 1, block[1], block[2]),
+            lambda s, b, within=within, which=which, index=index: (
+                s // within,
+                b[2 + which] ^ flip,
+                s % within,
+                index,
+            ),
+        )
+        kept, got = (x.reshape(lead, 2, rows, -1) for x in (chain.kept, chain.got))
+        specs += [spec(0), spec(0), spec(1), spec(1)]
+        args += [kept, got, kept, got]
+        outs += [pl.BlockSpec(block, lambda s, b, within=within: (s // within, s % within, 0))] * 2
+        shapes += [jax.ShapeDtypeStruct((lead, rows, chain.columns), BF)] * 2
+    size = sum(int(np.prod(x.shape)) for x in shapes)
+    result = launch(
+        halving_kernel,
+        grid_spec=dict(num_scalar_prefetch=1, grid=(steps,), in_specs=specs, out_specs=outs),
+        out_shape=shapes,
+        compiler_params=params(),
+        cost_estimate=cost(size, 6 * size),
+        name="halving_sum",
+    )(flags, *args)
+    for i, chain in enumerate(chains):
+        flat = lambda x: x.reshape(-1, chain.columns)
+        chain.kept, chain.index = flat(result[2 * i]), 0
+        chain.got = flip(flat(result[2 * i + 1]), "wide", chain.wide, chain.bit)
+    return result[0]
+
+
+def land_kernel(*refs):
+    number = len(refs) // 3
+    for block, got, out in zip(refs[:number], refs[number : 2 * number], refs[2 * number :]):
+        half = block.shape[0]
+        out[:half] = block[...]
+        out[half:] = got[...]
+
+
+def land(moves):
+    blocks, gots = [m.block for m in moves], [m.got for m in moves]
+    shapes = [(2 * x.shape[0],) + x.shape[1:] for x in blocks]
+    whole = lambda shape: pl.BlockSpec(shape, lambda s: (0, 0, 0))
+    joined = launch(
+        land_kernel,
+        grid=(1,),
+        in_specs=[whole(x.shape) for x in (*blocks, *gots)],
+        out_specs=[whole(x) for x in shapes],
+        out_shape=[jax.ShapeDtypeStruct(x, BF) for x in shapes],
+        compiler_params=params(),
+        cost_estimate=cost(0, 4 * sum(int(np.prod(x)) for x in shapes)),
+        name="land",
+    )(*blocks, *gots)
+    for move, block in zip(moves, joined):
+        move.block = block
+
+
+class Gather:
+    def __init__(self, block, sizes, order):
+        self.block, self.sizes, self.order = block, sizes, list(order) + [None]
+
+    def send(self):
+        bit = self.order.pop(0)
+        axis = "narrow" if bit is None else "wide"
+        self.got = flip(self.block, axis, self.sizes[axis], 0 if bit is None else bit)
+
+
+    def halves(self):
+        return [self.block, self.got]
+
+
+def owner_sum(x, axis):
+    return lax.psum_scatter(x, axis, scatter_dimension=0, tiled=True)
 
 
 def relative_place(owner, me, order):
     apart = owner ^ me
-    place = jnp.zeros_like(apart)
+    place = (apart & 1) << len(order)
     for at, bit in enumerate(order):
         place = place | (((apart >> (bit + 1)) & 1) << at)
-    return 2 * place + (apart & 1)
+    return place
 
 
 def layout(level_row, count):
@@ -720,78 +1006,84 @@
     sizes = {"wide": lax.axis_size("wide"), "narrow": lax.axis_size("narrow")}
     devices = sizes["wide"] * sizes["narrow"]
     me = lax.axis_index("wide") * sizes["narrow"] + lax.axis_index("narrow")
-    core = (lax.axis_index("narrow") & 1).reshape(1).astype(jnp.int32)
-    owners = jnp.arange(devices, dtype=jnp.int32)
+    chip = lax.axis_index("wide")
+    flags = [me, lax.axis_index("narrow") & 1]
+    flags += [(chip >> i) & 1 for i in range(bit_count(sizes["wide"]))]
+    flags = jnp.stack(flags).astype(jnp.int32)
     slots = labels.shape[1]
+    rows = 8
     own = proj_weight.shape[0]
     blocks = fc2_weight.shape[0] // own
-    paired = own % 16 == 0 and sizes["narrow"] == 2
+    paired = own % 32 == 0 and sizes["narrow"] == 2
 
     label_block = jnp.zeros((own, PAIR), BF)
     label_block = label_block.at[0, :slots].set((labels[0] // 256).astype(BF))
     label_block = label_block.at[1, :slots].set((labels[0] % 256).astype(BF))
     table_shard = jnp.concatenate([class_table, label_block], axis=1)
+    up_shard = fc1_weight.reshape(own, devices, blocks, own).transpose(0, 2, 1, 3)
+    feed_shard = jnp.concatenate(
+        [proj_weight, up_shard.reshape(own, -1)]
+        + [fc2_weight[i * own : (i + 1) * own] for i in range(blocks)],
+        axis=1,
+    )
+    ada_columns = lax.all_to_all(ada_weight, BOTH, 1, 0, tiled=True)
     if paired:
-        orders = [chip_order(sizes["wide"], turn)[::-1] for turn in range(3)]
-        table_halves = gather_halves(table_shard, sizes, orders[0])
-        table_all = jnp.stack([h.reshape(-1, own, width + PAIR) for h in table_halves], axis=1)
-        table_all = table_all.reshape(devices, own, width + PAIR)
-        weights = [
-            gather_halves(qkv_weight[:, i * width : (i + 1) * width], sizes, orders[i])
-            for i in range(3)
-        ]
-        table_places = relative_place(owners, me, orders[0])
-        places = jnp.stack([relative_place(owners, me, o) for o in orders]).astype(jnp.int32)
+        orders = [chip_order(sizes["wide"], turn)[::-1] for turn in (0, 1)]
+        orders.append([orders[0][0]] + orders[0][1:])
+        stages = len(orders[0])
+        both = Gather(jnp.concatenate([table_shard, qkv_weight], axis=1)[None], sizes, orders[0][:1])
+        both.send()
+        land([both])
+        cuts = (0, width + PAIR, width + PAIR + 3 * width // 2, 4 * width + PAIR)
+        table_move, *moves = (
+            Gather(both.block[:, :, low:high], sizes, order[1:])
+            for low, high, order in zip(cuts, cuts[1:], orders)
+        )
+        for move in (table_move, *moves):
+            move.send()
+        for step in range(1, stages):
+            land([table_move])
+            table_move.send()
+            if step < stages - 1:
+                await_all(done[0])
+                if step == 1:
+                    await_all(ada_columns)
+                land(moves)
+                for move in moves:
+                    move.send()
+                await_all(done[0])
+            if step == stages - 2:
+                feed_shard, table_move.got = lax.optimization_barrier((feed_shard, table_move.got))
+        tables = [h.reshape(-1, width + PAIR) for h in table_move.halves()]
     else:
-        table_all = lax.all_gather(table_shard, BOTH, axis=0, tiled=False)
-        qkv_all = lax.all_gather(qkv_weight, BOTH, axis=0, tiled=True)
-        weights = [(qkv_all[:, i * width : (i + 1) * width],) for i in range(3)]
-        table_places = owners
-        places = jnp.stack([owners] * 3)
-    up_shard = fc1_weight.reshape(own, devices, blocks, own).transpose(0, 2, 1, 3)
-    packed = lax.all_gather(
-        jnp.concatenate(
-            [proj_weight, up_shard.reshape(own, -1)]
-            + [fc2_weight[i * own : (i + 1) * own] for i in range(blocks)],
-            axis=1,
-        ),
-        BOTH,
-        axis=0,
-        tiled=True,
-    )
-
-    picked = (table_places[:, None] == owners[None, :]).astype(F32)
-    label_parts = jnp.dot(
-        picked, table_all[:, :2, width : width + 2 * slots].reshape(devices, -1).astype(F32)
-    ).reshape(devices, 2, 2 * slots)
-    labels_all = (256.0 * label_parts[:, 0, :slots] + label_parts[:, 1, :slots]).astype(jnp.int32)
-    labels_all = labels_all.reshape(-1)
-    label_owner = labels_all // own
+        orders = [()]
+        tables = [lax.all_gather(table_shard, BOTH, axis=0, tiled=True)]
+    class_vec, lifted, slot_labels, modulation_columns = modulation_call(
+        flags, tables, ada_columns, orders[0], slots, rows, own
+    )
     if paired:
-        label_place = relative_place(label_owner, me, orders[0]) * own + labels_all % own
+        await_all(done[0])
+        land(moves)
+        for move in moves:
+            move.send()
+        weights = [[h.reshape(width // 2, -1) for h in move.halves()] for move in moves]
+        owners = jnp.arange(devices, dtype=jnp.int32)
+        places = jnp.stack([relative_place(owners, me, o) for o in orders[1:]]).astype(jnp.int32)
     else:
-        label_place = labels_all
-    label_pick = (
-        label_place[:, None] == jnp.arange(devices * own, dtype=jnp.int32)[None, :]
-    ).astype(BF)
-    class_vec = jnp.dot(
-        label_pick, table_all[:, :, :width].reshape(-1, width), preferred_element_type=F32
-    )
-    lifted = jax.nn.silu(class_vec).astype(BF)
-    ada_columns = lax.all_to_all(ada_weight, BOTH, 1, 0, tiled=True)
-    modulation = lax.all_to_all(
-        jnp.dot(lifted, ada_columns, preferred_element_type=F32), BOTH, 0, 1, tiled=True
-    )
+        weights = [(lax.all_gather(qkv_weight, BOTH, axis=0, tiled=True),)]
+        places = jnp.zeros((1, devices), jnp.int32)
+    feed_weight = lax.all_gather(feed_shard, BOTH, axis=0, tiled=True)
+
+    modulation = lax.all_to_all(modulation_columns, BOTH, 0, 1, tiled=True)
     high = lax.reduce_precision(modulation, 8, 7)
     middle = lax.reduce_precision(modulation - high, 8, 7)
     low = modulation - high - middle
-    terms = jnp.pad(jnp.concatenate([high, middle, low]), ((0, 32 - 3 * slots), (0, 0))).astype(BF)
+    terms = jnp.pad(jnp.concatenate([high, middle, low]), ((0, 8), (0, 0))).astype(BF)
 
     inside, first, last = layout(levels[0], count)
     turned = jnp.pad(inside.astype(BF), ((0, 16 - slots), (0, 0)))
-    member = jnp.pad(jnp.concatenate([inside] * 3).astype(BF), ((0, 32 - 3 * slots), (0, 0))).T
-    starts = jnp.broadcast_to(first, (8, count))
-    ends = jnp.broadcast_to(last, (8, count))
+    inside = jnp.pad(inside.astype(BF), ((0, rows - slots), (0, 0)))
+    member = jnp.concatenate([inside] * 3 + [jnp.zeros_like(inside)]).T
     tile = 256
     span = jnp.concatenate(
         [first[:, ::tile] // tile, (last[:, tile - 1 :: tile] + tile - 1) // tile]
@@ -804,61 +1096,118 @@
     mixed, rest, inverse = attn_fwd_call(
         span, q, k, v, first.reshape(count, 1), last.reshape(count, 1), tile, tile
     )
-    after, branch, hidden_two, down = proj_call(tokens, mixed, cotangent, member, terms, packed)
-    mlp, back, *grads = mlp_call(core, hidden_two, down, packed, own, paired)
-    split = 2 if paired else 1
-    fc1_grad = scatter_sum(grads[:split], sizes, 0)
-    fc2_grad = scatter_sum(grads[split:], sizes, 1)
-    fc1_grad = fc1_grad.reshape(own, blocks, devices, own).transpose(0, 2, 1, 3).reshape(own, -1)
-    fc2_grad = fc2_grad.reshape(own, blocks, width).transpose(1, 0, 2).reshape(-1, width)
+    after, branch, hidden_two, down = proj_call(
+        tokens, mixed, cotangent, member, terms, feed_weight
+    )
+    mlp, back, *grads = mlp_call(flags, hidden_two, down, feed_weight, own, paired, 0, blocks)
+    swap = lambda x: flip(x, "narrow", sizes["narrow"], 0)
+    if paired:
+        up, down = (
+            Chain(kept, swap(sent), sizes, turn)
+            for turn, kept, sent in ((0, *grads[:2]), (1, *grads[2:]))
+        )
     output, grad_in, branch_grad, mixed_grad, delta, sums = middle_call(
-        mlp, back, after, cotangent, branch, mixed, rest, member, turned, terms, packed
-    )
-    proj_grad = scatter_sum(
-        weight_grad_call(core, mixed, [branch_grad], own, paired), sizes, 2
-    )
-    dq, dk, dv, scale_part = attn_bwd_call(
-        span, q, k, v, mixed_grad, starts, ends, inverse,
-        delta.reshape(-1, 8, count), rq, rk, scale_lanes, tile, tile,
-    )
-    qkv_grad = scatter_sum(weight_grad_call(core, hidden_one, [dq, dk, dv], own, paired), sizes, 0)
+        mlp, back, after, cotangent, branch, mixed, rest, member, turned, terms, feed_weight
+    )
+    early = jnp.pad(sums[:slots], ((0, rows - slots), (0, 0))).astype(BF)
+    early = lax.all_gather(early, BOTH, axis=0, tiled=True)
+    if paired:
+        await_all(done[0])
+        halve(flags, [up, down], 8)
+        await_all(done[0])
+    else:
+        feed = owner_sum(jnp.concatenate(grads, axis=1), BOTH).astype(F32)
+        units = blocks * width
+        fc1_grad = feed[:, :units].reshape(own, blocks, devices, own).transpose(0, 2, 1, 3)
+        fc1_grad = fc1_grad.reshape(own, -1)
+        fc2_grad = jnp.concatenate(
+            [feed[:, units + i * width : units + (i + 1) * width] for i in range(blocks)]
+        )
+    *heads, scale_part = attn_bwd_call(
+        span, q, k, v, mixed_grad, first, last, inverse, delta.reshape(-1, 8, count), rq, rk,
+        scale_lanes, 0, head_count // GROUP, tile, tile,
+    )
+    if paired:
+        await_all(done[0])
+        halve(flags, [up, down], 4)
+        await_all(done[0])
+    qkv_parts = weight_grad_call(flags, [(hidden_one, heads)], own, paired)
+    if paired:
+        qkv_got = swap(qkv_parts[1])
+        await_all(done[0])
+    proj_parts = weight_grad_call(flags, [(mixed, [branch_grad])], own, paired)
+    if paired:
+        qkv = [Chain(qkv_parts[0], qkv_got, sizes, i, 3 * width // 2, i) for i in range(2)]
+        proj = Chain(proj_parts[0], swap(proj_parts[1]), sizes, 2)
+        await_all(done[0])
+        halve(flags, [*qkv, proj], 4)
+        await_all(done[0])
+    else:
+        qkv_grad = owner_sum(qkv_parts[0], BOTH).astype(F32)
+        proj_grad = owner_sum(proj_parts[0], BOTH).astype(F32)
     tokens_grad, first_sums = first_call(
-        dq, dk, dv, qkv_full, tokens, grad_in, member, turned, terms
-    )
-
-    early, late = sums[:slots].astype(BF), first_sums[:slots].astype(BF)
-    early_all = lax.all_gather(early, BOTH, axis=0, tiled=True)
-    late_all = lax.all_gather(late, BOTH, axis=0, tiled=True)
-    cut = lambda x, i: x[:, i * width : (i + 1) * width]
-    pieces = [cut(early_all, 0), cut(early_all, 1), cut(late_all, 0), cut(early_all, 2), cut(late_all, 1), cut(early_all, 3)]
-    modulation_grad = jnp.concatenate(pieces, axis=1)
+        heads, qkv_full, tokens, grad_in, member, turned, terms
+    )
+    late = jnp.pad(first_sums[:slots], ((0, rows - slots), (0, 0))).astype(BF)
     own_width = width // devices
-    own_lifted = lax.dynamic_slice_in_dim(lifted, me * own_width, own_width, 1)
-    own_vec = lax.dynamic_slice_in_dim(class_vec, me * own_width, own_width, 1)
-    ada_grad = tn(own_lifted, modulation_grad)
-    lifted_grad = nt(modulation_grad, ada_weight)
-    _, silu_pull = jax.vjp(jax.nn.silu, own_vec)
-    class_grad = silu_pull(lifted_grad)[0]
-    label_true = (labels_all[:, None] == jnp.arange(devices * own, dtype=jnp.int32)[None, :]).astype(F32)
-    table_columns = jnp.einsum("ic,id->cd", label_true, class_grad, precision=lax.Precision.HIGHEST)
     scale_sums = scale_part[0].reshape(head_count, HEAD)[:, 0]
     head_rows = -(-head_count // own_width)
     head_rows += -head_rows % 8
     scale_rows = jnp.pad(scale_sums, (0, head_rows * own_width - head_count)).reshape(
-        1, head_rows, own_width
-    )
-    outgoing = jnp.concatenate(
-        [
-            table_columns.reshape(devices, own, own_width),
-            jnp.broadcast_to(scale_rows, (devices, head_rows, own_width)),
-        ],
-        axis=1,
-    ).reshape(-1, own_width)
+        head_rows, own_width
+    )
+    if paired:
+        move = Gather(late[None], sizes, orders[0])
+        move.send()
+        await_all(done[0])
+        halve(flags, [*qkv, proj, up, down], 2)
+        for step in range(stages):
+            await_all(done[0])
+            land([move])
+            move.send()
+            if step == 2:
+                await_all(done[0])
+                halve(flags, [*qkv, proj, up, down], 2)
+        lates = [h.reshape(-1, h.shape[-1]) for h in move.halves()]
+        await_all(done[0])
+        ada_grad, outgoing = ada_call(
+            flags, early, lates, lifted, class_vec, slot_labels, ada_weight, scale_rows, devices,
+            orders[0],
+        )
+        await_all(done[0])
+        halve(flags, [*qkv, proj], 2)
+        await_all(done[0])
+        fc1_grad, fc2_grad = finish([up, down], blocks)
+        await_all(done[0])
+        *parts, proj_grad = finish([*qkv, proj])
+        qkv_grad = jnp.concatenate(parts, axis=1)
+    else:
+        late = lax.all_gather(late, BOTH, axis=0, tiled=True)
+        cut = lambda x, i: x[:, i * width : (i + 1) * width]
+        item_grad = jnp.concatenate(
+            [cut(early, 0), cut(early, 1), cut(late, 0), cut(early, 2), cut(late, 1), cut(early, 3)],
+            axis=1,
+        )
+        ada_grad = tn(lax.dynamic_slice_in_dim(lifted, me * own_width, own_width, 1), item_grad)
+        own_vec = lax.dynamic_slice_in_dim(class_vec, me * own_width, own_width, 1).astype(F32)
+        _, silu_pull = jax.vjp(jax.nn.silu, own_vec)
+        class_grad = silu_pull(nt(item_grad, ada_weight))[0]
+        hot = (slot_labels[:, :1] == jnp.arange(devices * own, dtype=jnp.int32)[None, :]).astype(F32)
+        table_columns = jnp.einsum("ic,id->cd", hot, class_grad, precision=lax.Precision.HIGHEST)
+        outgoing = jnp.concatenate(
+            [
+                table_columns.reshape(devices, own, own_width),
+                jnp.broadcast_to(scale_rows[None], (devices,) + scale_rows.shape),
+            ],
+            axis=1,
+        )
+    outgoing = outgoing.reshape(-1, own_width)
     incoming = lax.all_to_all(outgoing, BOTH, 0, 1, tiled=True)
     table_grad = incoming[:own]
     scale_grad = jnp.sum(incoming[own:].reshape(head_rows, devices, own_width), axis=1).reshape(-1)[
         :head_count
     ]
+    units = blocks * width
     return (
         output,
         tokens_grad,

time: 680 us -> 563 us (0.83)
  waiting for transfers between devices: 217 us -> 105 us
  Pallas kernels: 237 us -> 330 us
  blocking collectives: 40.9 us -> 0 us
  starting transfers between devices: 82.1 us -> 61.7 us
  other arithmetic: 26.3 us -> 11.3 us
  local copies, waits for them, and re-layouts: 46.8 us -> 33 us
    ppermute x40 -> x42, waiting for transfers between devices: 188 us -> 93.7 us  [flip(): return lax.ppermute(values, axis, [(i, i ^ 1 << bit) for i in range(size)])]
    pallas_call x9 -> x30, Pallas kernels: 237 us -> 330 us  [run(): mark, *result = call(*args, *waits)]
    all_gather x1 -> x0, blocking collectives: 40.9 us -> none  [per_device(): late_all = lax.all_gather(late, BOTH, axis=0, tiled=True)]
    all_to_all x1, waiting for transfers between devices: 27 us -> 0.01 us  [per_device(): incoming = lax.all_to_all(outgoing, BOTH, 0, 1, tiled=True)]
    ppermute x40 -> x42, starting transfers between devices: 71.2 us -> 50 us  [flip(): return lax.ppermute(values, axis, [(i, i ^ 1 << bit) for i in range(size)])]
    convert_element_type x17 -> x2, other arithmetic: 16.9 us -> 1.68 us  [the longest x1 1.61 us: per_device(): early = jnp.pad(sums[:slots], ((0, rows - slots), (0, 0))).astype(BF)]
    all_gather x2, waiting for transfers between devices: 0.03 us -> 10.9 us  [the longest x1 10.9 us: per_device(): feed_weight = lax.all_gather(feed_shard, BOTH, axis=0, tiled=True)]
    reshape x8 -> x1, local copies, waits for them, and re-layouts: 9.68 us -> 0.67 us  [per_device(): jnp.pad(scale_sums, (0, head_rows * own_width - head_count))]
  transfers between devices with their start and end apart: 45 -> 47, of which waited for: 22 -> 21; matrix products, arithmetic and copies ran while one was open for 10% -> 4% of each run, Pallas kernels for 24% -> 40%
where the time goes in v3:
time: 563 us; the launch traced here: 556 us
  Pallas kernels  330 us (59%)
  waiting for transfers between devices  105 us (19%)
  starting transfers between devices  61.7 us (11%)
  local copies, waits for them, and re-layouts  33 us (6%)
  between operations  15.2 us (3%)
  other arithmetic  11.3 us (2%)
    pallas_call x30, Pallas kernels, run(): mark, *result = call(*args, *waits)  330 us
    ppermute x42, waiting for transfers between devices, flip(): return lax.ppermute(values, axis, [(i, i ^ 1 << bit) for i in range(size)])  93.7 us
    ppermute x42, starting transfers between devices, flip(): return lax.ppermute(values, axis, [(i, i ^ 1 << bit) for i in range(size)])  50 us
    unnamed x118, local copies, waits for them, and re-layouts  18.5 us
  transfers between devices with their start and end apart: 47, of which 21 were waited for; matrix products, arithmetic and copies ran while one was open for 4% of the time, Pallas kernels for 40%

profile of v3, /device:TPU:0, one launch (start us, length us, event | category | flops | bytes accessed | tf_op | source)
XLA Modules:
  0.0 556.0 jit_solution(5448168787368388545)
XLA Ops:
  9.0 4.1 collective-permute-start
  15.9 3.8 all-to-all-start
  22.0 7.6 %collective-permute-done.refs_1_ = bf16[1,32,4224]{2,1,0:T(8,128)(2,1)} collective-permute-done((bf16[1,32,4224]{2,1,0:T(8,128)(2,1)S(1)}, bf16[1,32,4224]{2,1,0:T(8,128)(2,1)}, u32[]{:S(2)}, u32[]{:S(2)}) %collective-permute-start) | collective-permute-done | bytes 270368 | tf_op jit(solution)/shard_map/ppermute | solution.py:804
  32.4 2.4 collective-permute-start.1
  34.8 4.7 collective-permute-done.1.refs_1_
  46.9 3.1 collective-permute-done.3.refs_2_
  52.4 2.1 land.13
  57.8 12.4 %collective-permute-done.5.refs_1_ = bf16[8,32,1152]{2,1,0:T(8,128)(2,1)S(1)} collective-permute-done((bf16[8,32,1152]{2,1,0:T(8,128)(2,1)}, bf16[8,32,1152]{2,1,0:T(8,128)(2,1)S(1)}, u32[]{:S(2)}, u32[]{:S(2)}) %collective-permute-start.5) | collective-permute-done | bytes 589856 | tf_op jit(solution)/shard_map/ppermute | solution.py:804
  72.3 6.0 %collective-permute-done.6.refs_2_ = bf16[4,32,1536]{2,1,0:T(8,128)(2,1)S(1)} collective-permute-done((bf16[4,32,1536]{2,1,0:T(8,128)(2,1)}, bf16[4,32,1536]{2,1,0:T(8,128)(2,1)S(1)}, u32[]{:S(2)}, u32[]{:S(2)}) %collective-permute-start.6) | collective-permute-done | bytes 393248 | tf_op jit(solution)/shard_map/ppermute | solution.py:804
  80.1 2.6 land.15
  82.7 2.3 land.16
  88.5 5.3 modulation.1
  93.8 4.7 all-to-all-start.1
  102.7 9.0 %collective-permute-done.10.refs_3_ = bf16[8,32,1536]{2,1,0:T(8,128)(2,1)S(1)} collective-permute-done((bf16[8,32,1536]{2,1,0:T(8,128)(2,1)}, bf16[8,32,1536]{2,1,0:T(8,128)(2,1)S(1)}, u32[]{:S(2)}, u32[]{:S(2)}) %collective-permute-start.10) | collective-permute-done | bytes 786464 | tf_op jit(solution)/shard_map/ppermute | solution.py:804
  114.1 3.6 land.17
  119.3 4.3 collective-permute-done.11
  124.8 23.9 %qkv_forward.1 = (f32[8,128]{1,0:T(8,128)}, bf16[1024,1024]{1,0:T(8,128)(2,1)}, bf16[1024,1024]{1,0:T(8,128)(2,1)}, bf16[1024,1024]{1,0:T(8,128)(2,1)}, bf16[102...) custom-call(s32[2,32]{1,0:T(2,128)} %pad_add_fusion.1.refs_0_, ...), custom_call_target="tpu_custom_call" | custom-call | flops 6442450944 | bytes 27262976 | tf_op jit(solution)/shard_map/qkv_forward/pallas_call | solution.py:79
  148.7 41.6 %attention_forward.1 = (f32[8,128]{1,0:T(8,128)}, bf16[1024,1024]{1,0:T(8,128)(2,1)}, bf16[1024,1024]{1,0:T(8,128)(2,1)}, f32[4,8,1024]{2,1,0:T(8,128)}) custom-call(s32[2,4]{1,0:T(2,128)} %pad_add_fusion.refs_0_, bf16[1024,1024]{1,0:T(8,128)(2,1)} %get-tuple-element.175.refs_1_, bf16[1024,1024]{1,0:T(8,128)(2,1)} %get-tuple-element.176.refs_2_, ...), custom_call_target="tpu_custom_call" | custom-call | flops 17179869184 | bytes 8388608 | tf_op jit(solution)/shard_map/attention_forward/pallas_call | solution.py:79
  190.3 10.9 %all-gather.3.cloned.1.call-done.refs_5_.refs_3_.refs_4_.refs_10_ = bf16[1024,9216]{1,0:T(8,128)(2,1)} async-done(((bf16[32,9216]{1,0:T(8,128)(2,1)}), bf16[1024,9216]{1,0:T(8,128)(2,1)}) %all-gather.3.cloned.1.call-update) | async-done | bytes 18874384 | tf_op jit(solution)/shard_map/all_gather | solution.py:1075
  201.2 10.0 %projection.1 = (f32[8,128]{1,0:T(8,128)}, f32[1024,1024]{1,0:T(8,128)}, bf16[1024,1024]{1,0:T(8,128)(2,1)}, bf16[1024,1024]{1,0:T(8,128)(2,1)}, bf16[1024,1024]{1,0:T(8,128)(2,1)}) custom-call(bf16[1024,1024]{1,0:T(8,128)(2,1)} %refs_4_.1, bf16[1024,1024]{1,0:T(8,128)(2,1)} %get-tuple-element.178.refs_1_.refs_5_, bf16[1024,1024]{1,0:T(8,128)(2,1)} %refs_3_.1, ...), custom_call_target="tpu_custom_call" | custom-call | flops 2147483648 | bytes 16777216 | tf_op jit(solution)/shard_map/projection/pallas_call | solution.py:79
  211.1 64.1 %feed_forward.1 = (f32[8,128]{1,0:T(8,128)}, f32[1024,1024]{1,0:T(8,128)}, f32[1024,1024]{1,0:T(8,128)}, bf16[512,4096]{1,0:T(8,128)(2,1)}, bf16[512,4096]{1,0:T...) custom-call(s32[6]{0:T(128)} %stack.32.refs_0_, bf16[1024,1024]{1,0:T(8,128)(2,1)} %get-tuple-element.180.refs_1_, ...), custom_call_target="tpu_custom_call" | custom-call | flops 51539607552 | bytes 20971520 | tf_op jit(solution)/shard_map/feed_forward/pallas_call | solution.py:79
  276.4 17.5 %middle.1 = (f32[8,128]{1,0:T(8,128)}, bf16[1024,1024]{1,0:T(8,128)(2,1)}, f32[1024,1024]{1,0:T(8,128)}, bf16[1024,1024]{1,0:T(8,128)(2,1)}, bf16[1024,1024]{1,0...) custom-call(f32[1024,1024]{1,0:T(8,128)} %get-tuple-element.182.refs_0_, ...), custom_call_target="tpu_custom_call" | custom-call | flops 4294967296 | bytes 31457280 | tf_op jit(solution)/shard_map/middle/pallas_call | solution.py:79
  295.9 11.5 %halving_sum.6 = (f32[8,128]{1,0:T(8,128)}, bf16[8,32,4096]{2,1,0:T(8,128)(2,1)}, bf16[8,32,4096]{2,1,0:T(8,128)(2,1)}, bf16[4,64,4096]{2,1,0:T(8,128)(2,1)}, bf16[4,64,4096]{2,1,0:T(8,128)(2,1)}) custom-call(s32[6]{0:T(128)} %stack.32.refs_0_, bf16[8,2,32,4096]{3,2,1,0:T(8,128)(2,1)} %bitcast.119, bf16[8,2,32,4096]{3,2,1,0:T(8,128)(2,1)} %bitcast.123, ...), custom_call_target="tpu_custom_call" | custom-call | flops 4194304 | bytes 25165824 | tf_op jit(solution)/shard_map/halving_sum/pallas_call | solution.py:79
  309.5 58.7 %attention_backward.1 = (f32[8,128]{1,0:T(8,128)}, bf16[1024,1024]{1,0:T(8,128)(2,1)}, bf16[1024,1024]{1,0:T(8,128)(2,1)}, bf16[1024,1024]{1,0:T(8,128)(2,1)}, f32[8,1024]{1,0:T(8,128)}) custom-call(s32[2,4]{1,0:T(2,128)} %pad_add_fusion.refs_0_, bf16[1024,1024]{1,0:T(8,128)(2,1)} %get-tuple-element.175.refs_1_, ...), custom_call_target="tpu_custom_call" | custom-call | flops 42949672960 | bytes 18874368 | tf_op jit(solution)/shard_map/attention_backward/pallas_call | solution.py:79
  370.3 6.5 %halving_sum.7 = (f32[8,128]{1,0:T(8,128)}, bf16[4,32,4096]{2,1,0:T(8,128)(2,1)}, bf16[4,32,4096]{2,1,0:T(8,128)(2,1)}, bf16[2,64,4096]{2,1,0:T(8,128)(2,1)}, bf16[2,64,4096]{2,1,0:T(8,128)(2,1)}) custom-call(s32[6]{0:T(128)} %stack.32.refs_0_, bf16[4,2,32,4096]{3,2,1,0:T(8,128)(2,1)} %bitcast.125, bf16[4,2,32,4096]{3,2,1,0:T(8,128)(2,1)} %bitcast.129, ...), custom_call_target="tpu_custom_call" | custom-call | flops 2097152 | bytes 12582912 | tf_op jit(solution)/shard_map/halving_sum/pallas_call | solution.py:79
  376.8 13.3 %weight_grad.2 = (f32[8,128]{1,0:T(8,128)}, bf16[512,3072]{1,0:T(8,128)(2,1)}, bf16[512,3072]{1,0:T(8,128)(2,1)}) custom-call(s32[6]{0:T(128)} %stack.32.refs_0_, bf16[1024,1024]{1,0:T(8,128)(2,1)} %get-tuple-element.204.refs_1_, bf16[1024,1024]{1,0:T(8,128)(2,1)} %get-tuple-element.199.refs_2_.refs_0_, ...), custom_call_target="tpu_custom_call" | custom-call | flops 6442450944 | bytes 12582912 | tf_op jit(solution)/shard_map/weight_grad/pallas_call | solution.py:79
  391.7 6.8 %weight_grad.3 = (f32[8,128]{1,0:T(8,128)}, bf16[512,1024]{1,0:T(8,128)(2,1)}, bf16[512,1024]{1,0:T(8,128)(2,1)}) custom-call(s32[6]{0:T(128)} %stack.32.refs_0_, bf16[1024,1024]{1,0:T(8,128)(2,1)} %get-tuple-element.178.refs_1_.refs_5_, bf16[1024,1024]{1,0:T(8,128)(2,1)} %get-tuple-element.213.refs_2_, f32[8,128]{1,0:T(8,128)} %get-tuple-element.214.refs_3_), custom_call_target="tpu_custom_call" | custom-call | flops 2147483648 | bytes 4194304 | tf_op jit(solution)/shard_map/weight_grad/pallas_call | solution.py:79
  399.0 5.4 collective-permute-start.23
  406.4 6.7 %halving_sum.8 = (f32[8,128]{1,0:T(8,128)}, bf16[8,32,1536]{2,1,0:T(8,128)(2,1)}, bf16[8,32,1536]{2,1,0:T(8,128)(2,1)}, bf16[4,64,1536]{2,1,0:T(8,128)(2,1)}, bf...) custom-call(s32[6]{0:T(128)} %stack.32.refs_0_, ...), custom_call_target="tpu_custom_call" | custom-call | flops 2097152 | bytes 12582912 | tf_op jit(solution)/shard_map/halving_sum/pallas_call | solution.py:79
  413.2 2.6 collective-permute-start.21
  415.8 16.1 %first_norm_backward.1 = (f32[8,128]{1,0:T(8,128)}, bf16[1024,1024]{1,0:T(8,128)(2,1)}, f32[16,2048]{1,0:T(8,128)}) custom-call(bf16[1024,1024]{1,0:T(8,128)(2,1)} %get-tuple-element.199.refs_2_.refs_0_, bf16[1024,1024]{1,0:T(8,128)(2,1)} %get-tuple-element.200.refs_3_.refs_1_, bf16[1024,1024]{1,0:T(8,128)(2,1)} %get-tuple-element.201.refs_4_.refs_2_, ...), custom_call_target="tpu_custom_call" | custom-call | flops 6442450944 | bytes 18874368 | tf_op jit(solution)/shard_map/first_norm_backward/pallas_call | solution.py:79
  432.8 5.8 %collective-permute-start.19 = (bf16[1,8,2048]{2,1,0:T(8,128)(2,1)S(1)}, bf16[1,8,2048]{2,1,0:T(8,128)(2,1)S(1)}, u32[]{:S(2)}, u32[]{:S(2)}) collective-permute-start(bf16[1,8,2048]{2,1,0:T(8,128)(2,1)S(1)} %fusion.14.refs_0_), channel_id=1, source_target_pairs={{0,16},{2,18},{4,20},{6,22},{8,24},{10,26},{12,28},{14,30},{16,0},... | collective-permute-start | bytes 98312 | tf_op jit(solution)/shard_map/ppermute | solution.py:804
  438.6 9.0 %collective-permute-done.22 = bf16[256,1024]{1,0:T(8,128)(2,1)S(1)} collective-permute-done((bf16[256,1024]{1,0:T(8,128)(2,1)}, bf16[256,1024]{1,0:T(8,128)(2,1)S(1)}, u32[]{:S(2)}, u32[]{:S(2)}) %collective-permute-start.22) | collective-permute-done | bytes 524320 | tf_op jit(solution)/shard_map/ppermute | solution.py:804
  447.6 2.3 collective-permute-done.21
  450.8 6.4 %halving_sum.9 = (f32[8,128]{1,0:T(8,128)}, bf16[4,32,1536]{2,1,0:T(8,128)(2,1)}, bf16[4,32,1536]{2,1,0:T(8,128)(2,1)}, bf16[2,64,1536]{2,1,0:T(8,128)(2,1)}, bf...) custom-call(s32[6]{0:T(128)} %stack.32.refs_0_, ...), custom_call_target="tpu_custom_call" | custom-call | flops 2097152 | bytes 12582912 | tf_op jit(solution)/shard_map/halving_sum/pallas_call | solution.py:79
  459.3 4.5 collective-permute-done.25.refs_1_
  470.0 2.4 collective-permute-done.26.refs_1_
  474.7 10.6 %collective-permute-done.30 = bf16[128,1024]{1,0:T(8,128)(2,1)S(1)} collective-permute-done((bf16[128,1024]{1,0:T(8,128)(2,1)}, bf16[128,1024]{1,0:T(8,128)(2,1)S(1)}, u32[]{:S(2)}, u32[]{:S(2)}) %collective-permute-start.30) | collective-permute-done | bytes 262176 | tf_op jit(solution)/shard_map/ppermute | solution.py:804
  485.4 2.5 collective-permute-done.29
  489.1 4.3 halving_sum.10
  497.8 5.7 %collective-permute-start.40 = (bf16[32,4096]{1,0:T(8,128)(2,1)}, bf16[32,4096]{1,0:T(8,128)(2,1)S(1)}, u32[]{:S(2)}, u32[]{:S(2)}) collective-permute-start(bf16[32,4096]{1,0:T(8,128)(2,1)} %bitcast.223), channel_id=1, source_target_pairs={{0,16},{2,18},{4,20},{6,22},{8,24},{10,26},{12,28},{14,30},{16,0},... | collective-permute-start | bytes 786440 | tf_op jit(solution)/shard_map/ppermute | solution.py:804
  505.2 7.8 %adaptive_norm_backward.1 = (f32[8,128]{1,0:T(8,128)}, f32[32,6144]{1,0:T(8,128)}, f32[32,40,32]{2,1,0:T(8,128)}) custom-call(s32[6]{0:T(128)} %stack.32.refs_0_, bf16[256,4096]{1,0:T(8,128)(2,1)} %all-gather.5.cloned.1.call-done.refs_1_, bf16[128,2048]{1,0:T(8,128)(2,1)} %bitcast.191, bf16[128,2048]{1,0:T(8,128)(2,1)} %bitcast.192, ...), custom_call_target="tpu_custom_call" | custom-call | flops 1000000000 | bytes 10000000 | tf_op jit(solution)/shard_map/adaptive_norm_backward/pallas_call | solution.py:79
  513.9 2.8 halving_sum.11
  516.6 2.9 collective-permute-start.37
  519.6 2.8 collective-permute-start.39
  523.8 2.7 all-to-all-start.2
  527.7 7.4 %collective-permute-done.41.refs_3_ = bf16[32,4096]{1,0:T(8,128)(2,1)S(1)} collective-permute-done((bf16[32,4096]{1,0:T(8,128)(2,1)}, bf16[32,4096]{1,0:T(8,128)(2,1)S(1)}, u32[]{:S(2)}, u32[]{:S(2)}) %collective-permute-start.41) | collective-permute-done | bytes 262176 | tf_op jit(solution)/shard_map/ppermute | solution.py:804
  535.9 2.7 last_sum.2
  (253 shorter events, 84.8 us)
Async XLA Ops:
  9.0 20.5 %collective-permute-start = (bf16[1,32,4224]{2,1,0:T(8,128)(2,1)S(1)}, bf16[1,32,4224]{2,1,0:T(8,128)(2,1)}, u32[]{:S(2)}, u32[]{:S(2)}) collective-permute-start(bf16[1,32,4224]{2,1,0:T(8,128)(2,1)S(1)} %maximum_bitcast_fusion.refs_0_), channel_id=1, source_target_pairs={{0,16},{2,18},{4,20},{6,22},{8,24},{10,26},{12,28},{14,30},{16,0},... | collective-permute-start | bytes 811016 | tf_op jit(solution)/shard_map/ppermute | solution.py:804
  15.9 35.7 %all-to-all-start = ((bf16[32,32,192]{2,0,1:T(8,128)(2,1)}), bf16[32,32,192]{2,0,1:T(8,128)(2,1)S(1)}, u32[]{:S(2)}, u32[]{:S(2)}) async-start(bf16[32,32,192]{2,0,1:T(8,128)(2,1)} %copy.81), calls=%async_computation | async-start | bytes 1048576 | tf_op jit(solution)/shard_map/all_to_all | solution.py:1029
  19.7 181.5 %all-gather.3.cloned.1.call-start = ((), (), s32[]{:S(2)}) async-start(), calls=%async_computation.3 | async-start | bytes 19464192 | tf_op jit(solution)/shard_map/all_gather | solution.py:1075
  32.4 7.1 %collective-permute-start.1 = (bf16[2,32,1152]{2,1,0:T(8,128)(2,1)S(1)}, bf16[2,32,1152]{2,1,0:T(8,128)(2,1)S(1)}, u32[]{:S(2)}, u32[]{:S(2)}) collective-permute-start(bf16[2,32,1152]{2,1,0:T(8,128)(2,1)S(1)} %slice.91.refs_0_), channel_id=1, source_target_pairs={{0,8},{2,10},{4,12},{6,14},{8,0},{10,2},{12,4},{14,6},{16,24},{18,... | collective-permute-start | bytes 442376 | tf_op jit(solution)/shard_map/ppermute | solution.py:804
  34.7 37.2 %copy-start.53 = (s32[1,6]{1,0:T(1,128)S(1)}, s32[1,6]{1,0:T(1,128)}, u32[]{:S(2)}) copy-start(s32[1,6]{1,0:T(1,128)} %param.24) | copy-start | bytes 76
  41.9 12.7 %collective-permute-start.2 = (bf16[4,32,1152]{2,1,0:T(8,128)(2,1)}, bf16[4,32,1152]{2,1,0:T(8,128)(2,1)S(1)}, u32[]{:S(2)}, u32[]{:S(2)}) collective-permute-start(bf16[4,32,1152]{2,1,0:T(8,128)(2,1)} %get-tuple-element.159.refs_0_), channel_id=1, source_target_pairs={{0,4},{2,6},{4,0},{6,2},{8,12},{10,14},{12,8},{14,10},{16,20},{18,... | collective-permute-start | bytes 884744 | tf_op jit(solution)/shard_map/ppermute | solution.py:804
  44.4 5.7 %collective-permute-start.3 = (bf16[2,32,1536]{2,1,0:T(8,128)(2,1)S(1)}, bf16[2,32,1536]{2,1,0:T(8,128)(2,1)S(1)}, u32[]{:S(2)}, u32[]{:S(2)}) collective-permute-start(bf16[2,32,1536]{2,1,0:T(8,128)(2,1)S(1)} %get-tuple-element.286.refs_0_), channel_id=1, source_target_pairs={{0,2},{2,0},{4,6},{6,4},{8,10},{10,8},{12,14},{14,12},{16,18},{18,... | collective-permute-start | bytes 589832 | tf_op jit(solution)/shard_map/ppermute | solution.py:804
  45.9 5.7 %collective-permute-start.4 = (bf16[2,32,1536]{2,1,0:T(8,128)(2,1)S(1)}, bf16[2,32,1536]{2,1,0:T(8,128)(2,1)S(1)}, u32[]{:S(2)}, u32[]{:S(2)}) collective-permute-start(bf16[2,32,1536]{2,1,0:T(8,128)(2,1)S(1)} %get-tuple-element.285.refs_1_), channel_id=1, source_target_pairs={{0,8},{2,10},{4,12},{6,14},{8,0},{10,2},{12,4},{14,6},{16,24},{18,... | collective-permute-start | bytes 589832 | tf_op jit(solution)/shard_map/ppermute | solution.py:804
  57.2 13.0 %collective-permute-start.5 = (bf16[8,32,1152]{2,1,0:T(8,128)(2,1)}, bf16[8,32,1152]{2,1,0:T(8,128)(2,1)S(1)}, u32[]{:S(2)}, u32[]{:S(2)}) collective-permute-start(bf16[8,32,1152]{2,1,0:T(8,128)(2,1)} %get-tuple-element.162.refs_0_), channel_id=1, source_target_pairs={{0,2},{2,0},{4,6},{6,4},{8,10},{10,8},{12,14},{14,12},{16,18},{18,... | collective-permute-start | bytes 1769480 | tf_op jit(solution)/shard_map/ppermute | solution.py:804
  70.2 8.1 %collective-permute-start.6 = (bf16[4,32,1536]{2,1,0:T(8,128)(2,1)}, bf16[4,32,1536]{2,1,0:T(8,128)(2,1)S(1)}, u32[]{:S(2)}, u32[]{:S(2)}) collective-permute-start(bf16[4,32,1536]{2,1,0:T(8,128)(2,1)} %get-tuple-element.164.refs_0_), channel_id=1, source_target_pairs={{0,8},{2,10},{4,12},{6,14},{8,0},{10,2},{12,4},{14,6},{16,24},{18,... | collective-permute-start | bytes 1179656 | tf_op jit(solution)/shard_map/ppermute | solution.py:804
  71.4 8.0 %collective-permute-start.7 = (bf16[4,32,1536]{2,1,0:T(8,128)(2,1)}, bf16[4,32,1536]{2,1,0:T(8,128)(2,1)S(1)}, u32[]{:S(2)}, u32[]{:S(2)}) collective-permute-start(bf16[4,32,1536]{2,1,0:T(8,128)(2,1)} %get-tuple-element.165.refs_1_), channel_id=1, source_target_pairs={{0,4},{2,6},{4,0},{6,2},{8,12},{10,14},{12,8},{14,10},{16,20},{18,... | collective-permute-start | bytes 1179656 | tf_op jit(solution)/shard_map/ppermute | solution.py:804
  85.1 3.4 collective-permute-start.8
  85.7 26.0 %collective-permute-start.10 = (bf16[8,32,1536]{2,1,0:T(8,128)(2,1)}, bf16[8,32,1536]{2,1,0:T(8,128)(2,1)S(1)}, u32[]{:S(2)}, u32[]{:S(2)}) collective-permute-start(bf16[8,32,1536]{2,1,0:T(8,128)(2,1)} %get-tuple-element.171.refs_1_), channel_id=1, source_target_pairs={{0,2},{2,0},{4,6},{6,4},{8,10},{10,8},{12,14},{14,12},{16,18},{18,... | collective-permute-start | bytes 2359304 | tf_op jit(solution)/shard_map/ppermute | solution.py:804
  86.3 27.0 %collective-permute-start.9 = (bf16[8,32,1536]{2,1,0:T(8,128)(2,1)}, bf16[8,32,1536]{2,1,0:T(8,128)(2,1)S(1)}, u32[]{:S(2)}, u32[]{:S(2)}) collective-permute-start(bf16[8,32,1536]{2,1,0:T(8,128)(2,1)} %get-tuple-element.170.refs_0_), channel_id=1, source_target_pairs={{0,4},{2,6},{4,0},{6,2},{8,12},{10,14},{12,8},{14,10},{16,20},{18,... | collective-permute-start | bytes 2359304 | tf_op jit(solution)/shard_map/ppermute | solution.py:804
  93.8 24.5 %all-to-all-start.1 = ((f32[32,8,192]{2,1,0:T(8,128)}), f32[32,8,192]{2,1,0:T(8,128)S(1)}, u32[]{:S(2)}, u32[]{:S(2)}) async-start(f32[32,8,192]{2,1,0:T(8,128)} %bitcast.197), calls=%async_computation.1 | async-start | bytes 524288 | tf_op jit(solution)/shard_map/all_to_all | solution.py:1077
  98.4 406.8 %all-gather.5.cloned.1.call-start = ((), (), s32[]{:S(2)}) async-start(), calls=%async_computation.4 | async-start | bytes 2162688 | tf_op jit(solution)/shard_map/all_gather | solution.py:1113
  117.8 5.8 %collective-permute-start.11 = (bf16[16,32,1536]{2,1,0:T(8,128)(2,1)}, bf16[16,32,1536]{2,1,0:T(8,128)(2,1)S(1)}, u32[]{:S(2)}, u32[]{:S(2)}) collective-permute-start(bf16[16,32,1536]{2,1,0:T(8,128)(2,1)} %get-tuple-element.173), channel_id=1, source_target_pairs={{0,1},{1,0},{2,3},{3,2},{4,5},{5,4},{6,7},{7,6},{8,9},{9,8},{10,11... | collective-permute-start | bytes 4718600 | tf_op jit(solution)/shard_map/ppermute | solution.py:804
  117.8 6.0 %collective-permute-start.12 = (bf16[16,32,1536]{2,1,0:T(8,128)(2,1)}, bf16[16,32,1536]{2,1,0:T(8,128)(2,1)}, u32[]{:S(2)}, u32[]{:S(2)}) collective-permute-start(bf16[16,32,1536]{2,1,0:T(8,128)(2,1)} %get-tuple-element.174), channel_id=1, source_target_pairs={{0,1},{1,0},{2,3},{3,2},{4,5},{5,4},{6,7},{7,6},{8,9},{9,8},{10,11... | collective-permute-start | bytes 4718600 | tf_op jit(solution)/shard_map/ppermute | solution.py:804
  275.2 18.7 %collective-permute-start.13 = (bf16[512,4096]{1,0:T(8,128)(2,1)}, bf16[512,4096]{1,0:T(8,128)(2,1)S(1)}, u32[]{:S(2)}, u32[]{:S(2)}) collective-permute-start(bf16[512,4096]{1,0:T(8,128)(2,1)} %get-tuple-element.194), channel_id=1, source_target_pairs={{0,1},{1,0},{2,3},{3,2},{4,5},{5,4},{6,7},{7,6},{8,9},{9,8},{10,11... | collective-permute-start | bytes 12582920 | tf_op jit(solution)/shard_map/ppermute | solution.py:804
  275.5 18.4 %collective-permute-start.14 = (bf16[512,4096]{1,0:T(8,128)(2,1)}, bf16[512,4096]{1,0:T(8,128)(2,1)}, u32[]{:S(2)}, u32[]{:S(2)}) collective-permute-start(bf16[512,4096]{1,0:T(8,128)(2,1)} %get-tuple-element.196), channel_id=1, source_target_pairs={{0,1},{1,0},{2,3},{3,2},{4,5},{5,4},{6,7},{7,6},{8,9},{9,8},{10,11... | collective-permute-start | bytes 12582920 | tf_op jit(solution)/shard_map/ppermute | solution.py:804
  307.4 60.9 %collective-permute-start.15 = (bf16[256,4096]{1,0:T(8,128)(2,1)}, bf16[256,4096]{1,0:T(8,128)(2,1)S(1)}, u32[]{:S(2)}, u32[]{:S(2)}) collective-permute-start(bf16[256,4096]{1,0:T(8,128)(2,1)} %bitcast.210), channel_id=1, source_target_pairs={{0,2},{2,0},{4,6},{6,4},{8,10},{10,8},{12,14},{14,12},{16,18},{18,... | collective-permute-start | bytes 6291464 | tf_op jit(solution)/shard_map/ppermute | solution.py:804
  308.9 59.4 %collective-permute-start.16 = (bf16[256,4096]{1,0:T(8,128)(2,1)}, bf16[256,4096]{1,0:T(8,128)(2,1)S(1)}, u32[]{:S(2)}, u32[]{:S(2)}) collective-permute-start(bf16[256,4096]{1,0:T(8,128)(2,1)} %bitcast.209), channel_id=1, source_target_pairs={{0,4},{2,6},{4,0},{6,2},{8,12},{10,14},{12,8},{14,10},{16,20},{18,... | collective-permute-start | bytes 6291464 | tf_op jit(solution)/shard_map/ppermute | solution.py:804
  390.1 14.4 %collective-permute-start.17 = (bf16[512,3072]{1,0:T(8,128)(2,1)}, bf16[512,3072]{1,0:T(8,128)(2,1)S(1)}, u32[]{:S(2)}, u32[]{:S(2)}) collective-permute-start(bf16[512,3072]{1,0:T(8,128)(2,1)} %get-tuple-element.212), channel_id=1, source_target_pairs={{0,1},{1,0},{2,3},{3,2},{4,5},{5,4},{6,7},{7,6},{8,9},{9,8},{10,11... | collective-permute-start | bytes 9437192 | tf_op jit(solution)/shard_map/ppermute | solution.py:804
  398.5 6.0 %collective-permute-start.18 = (bf16[512,1024]{1,0:T(8,128)(2,1)}, bf16[512,1024]{1,0:T(8,128)(2,1)S(1)}, u32[]{:S(2)}, u32[]{:S(2)}) collective-permute-start(bf16[512,1024]{1,0:T(8,128)(2,1)} %get-tuple-element.216), channel_id=1, source_target_pairs={{0,1},{1,0},{2,3},{3,2},{4,5},{5,4},{6,7},{7,6},{8,9},{9,8},{10,11... | collective-permute-start | bytes 3145736 | tf_op jit(solution)/shard_map/ppermute | solution.py:804
  399.0 33.8 %collective-permute-start.23 = (bf16[128,4096]{1,0:T(8,128)(2,1)}, bf16[128,4096]{1,0:T(8,128)(2,1)S(1)}, u32[]{:S(2)}, u32[]{:S(2)}) collective-permute-start(bf16[128,4096]{1,0:T(8,128)(2,1)} %bitcast.52), channel_id=1, source_target_pairs={{0,4},{2,6},{4,0},{6,2},{8,12},{10,14},{12,8},{14,10},{16,20},{18,... | collective-permute-start | bytes 3145736 | tf_op jit(solution)/shard_map/ppermute | solution.py:804
  404.4 34.1 %collective-permute-start.24 = (bf16[128,4096]{1,0:T(8,128)(2,1)}, bf16[128,4096]{1,0:T(8,128)(2,1)S(1)}, u32[]{:S(2)}, u32[]{:S(2)}) collective-permute-start(bf16[128,4096]{1,0:T(8,128)(2,1)} %bitcast.55), channel_id=1, source_target_pairs={{0,8},{2,10},{4,12},{6,14},{8,0},{10,2},{12,4},{14,6},{16,24},{18,... | collective-permute-start | bytes 3145736 | tf_op jit(solution)/shard_map/ppermute | solution.py:804
  413.1 34.5 %collective-permute-start.20 = (bf16[256,1536]{1,0:T(8,128)(2,1)}, bf16[256,1536]{1,0:T(8,128)(2,1)S(1)}, u32[]{:S(2)}, u32[]{:S(2)}) collective-permute-start(bf16[256,1536]{1,0:T(8,128)(2,1)} %bitcast.216), channel_id=1, source_target_pairs={{0,2},{2,0},{4,6},{6,4},{8,10},{10,8},{12,14},{14,12},{16,18},{18,... | collective-permute-start | bytes 2359304 | tf_op jit(solution)/shard_map/ppermute | solution.py:804
  413.2 36.7 %collective-permute-start.21 = (bf16[256,1536]{1,0:T(8,128)(2,1)}, bf16[256,1536]{1,0:T(8,128)(2,1)S(1)}, u32[]{:S(2)}, u32[]{:S(2)}) collective-permute-start(bf16[256,1536]{1,0:T(8,128)(2,1)} %bitcast.215), channel_id=1, source_target_pairs={{0,4},{2,6},{4,0},{6,2},{8,12},{10,14},{12,8},{14,10},{16,20},{18,... | collective-permute-start | bytes 2359304 | tf_op jit(solution)/shard_map/ppermute | solution.py:804
  415.8 31.8 %collective-permute-start.22 = (bf16[256,1024]{1,0:T(8,128)(2,1)}, bf16[256,1024]{1,0:T(8,128)(2,1)S(1)}, u32[]{:S(2)}, u32[]{:S(2)}) collective-permute-start(bf16[256,1024]{1,0:T(8,128)(2,1)} %bitcast.219), channel_id=1, source_target_pairs={{0,8},{2,10},{4,12},{6,14},{8,0},{10,2},{12,4},{14,6},{16,24},{18,... | collective-permute-start | bytes 1572872 | tf_op jit(solution)/shard_map/ppermute | solution.py:804
  432.8 24.4 %collective-permute-start.19 = (bf16[1,8,2048]{2,1,0:T(8,128)(2,1)S(1)}, bf16[1,8,2048]{2,1,0:T(8,128)(2,1)S(1)}, u32[]{:S(2)}, u32[]{:S(2)}) collective-permute-start(bf16[1,8,2048]{2,1,0:T(8,128)(2,1)S(1)} %fusion.14.refs_0_), channel_id=1, source_target_pairs={{0,16},{2,18},{4,20},{6,22},{8,24},{10,26},{12,28},{14,30},{16,0},... | collective-permute-start | bytes 98312 | tf_op jit(solution)/shard_map/ppermute | solution.py:804
  459.3 4.5 collective-permute-start.25
  465.9 6.5 %collective-permute-start.26 = (bf16[4,8,2048]{2,1,0:T(8,128)(2,1)}, bf16[4,8,2048]{2,1,0:T(8,128)(2,1)S(1)}, u32[]{:S(2)}, u32[]{:S(2)}) collective-permute-start(bf16[4,8,2048]{2,1,0:T(8,128)(2,1)} %get-tuple-element.236.refs_0_), channel_id=1, source_target_pairs={{0,4},{2,6},{4,0},{6,2},{8,12},{10,14},{12,8},{14,10},{16,20},{18,... | collective-permute-start | bytes 393224 | tf_op jit(solution)/shard_map/ppermute | solution.py:804
  467.7 20.3 %collective-permute-start.31 = (bf16[64,4096]{1,0:T(8,128)(2,1)}, bf16[64,4096]{1,0:T(8,128)(2,1)S(1)}, u32[]{:S(2)}, u32[]{:S(2)}) collective-permute-start(bf16[64,4096]{1,0:T(8,128)(2,1)} %bitcast.218), channel_id=1, source_target_pairs={{0,8},{2,10},{4,12},{6,14},{8,0},{10,2},{12,4},{14,6},{16,24},{18,... | collective-permute-start | bytes 1572872 | tf_op jit(solution)/shard_map/ppermute | solution.py:804
  467.7 20.3 %collective-permute-start.32 = (bf16[64,4096]{1,0:T(8,128)(2,1)}, bf16[64,4096]{1,0:T(8,128)(2,1)S(1)}, u32[]{:S(2)}, u32[]{:S(2)}) collective-permute-start(bf16[64,4096]{1,0:T(8,128)(2,1)} %bitcast.217), channel_id=1, source_target_pairs={{0,2},{2,0},{4,6},{6,4},{8,10},{10,8},{12,14},{14,12},{16,18},{18,... | collective-permute-start | bytes 1572872 | tf_op jit(solution)/shard_map/ppermute | solution.py:804
  467.7 17.7 %collective-permute-start.30 = (bf16[128,1024]{1,0:T(8,128)(2,1)}, bf16[128,1024]{1,0:T(8,128)(2,1)S(1)}, u32[]{:S(2)}, u32[]{:S(2)}) collective-permute-start(bf16[128,1024]{1,0:T(8,128)(2,1)} %bitcast.224), channel_id=1, source_target_pairs={{0,2},{2,0},{4,6},{6,4},{8,10},{10,8},{12,14},{14,12},{16,18},{18,... | collective-permute-start | bytes 786440 | tf_op jit(solution)/shard_map/ppermute | solution.py:804
  469.7 15.7 %collective-permute-start.28 = (bf16[128,1536]{1,0:T(8,128)(2,1)}, bf16[128,1536]{1,0:T(8,128)(2,1)S(1)}, u32[]{:S(2)}, u32[]{:S(2)}) collective-permute-start(bf16[128,1536]{1,0:T(8,128)(2,1)} %bitcast.221), channel_id=1, source_target_pairs={{0,4},{2,6},{4,0},{6,2},{8,12},{10,14},{12,8},{14,10},{16,20},{18,... | collective-permute-start | bytes 1179656 | tf_op jit(solution)/shard_map/ppermute | solution.py:804
  472.4 15.6 %collective-permute-start.29 = (bf16[128,1536]{1,0:T(8,128)(2,1)}, bf16[128,1536]{1,0:T(8,128)(2,1)S(1)}, u32[]{:S(2)}, u32[]{:S(2)}) collective-permute-start(bf16[128,1536]{1,0:T(8,128)(2,1)} %bitcast.220), channel_id=1, source_target_pairs={{0,8},{2,10},{4,12},{6,14},{8,0},{10,2},{12,4},{14,6},{16,24},{18,... | collective-permute-start | bytes 1179656 | tf_op jit(solution)/shard_map/ppermute | solution.py:804
  485.4 8.0 %collective-permute-start.27 = (bf16[8,8,2048]{2,1,0:T(8,128)(2,1)}, bf16[8,8,2048]{2,1,0:T(8,128)(2,1)S(1)}, u32[]{:S(2)}, u32[]{:S(2)}) collective-permute-start(bf16[8,8,2048]{2,1,0:T(8,128)(2,1)} %get-tuple-element.238.refs_0_), channel_id=1, source_target_pairs={{0,2},{2,0},{4,6},{6,4},{8,10},{10,8},{12,14},{14,12},{16,18},{18,... | collective-permute-start | bytes 786440 | tf_op jit(solution)/shard_map/ppermute | solution.py:804
  495.9 7.6 %collective-permute-start.33 = (bf16[16,8,2048]{2,1,0:T(8,128)(2,1)}, bf16[16,8,2048]{2,1,0:T(8,128)(2,1)S(1)}, u32[]{:S(2)}, u32[]{:S(2)}) collective-permute-start(bf16[16,8,2048]{2,1,0:T(8,128)(2,1)} %get-tuple-element.251), channel_id=1, source_target_pairs={{0,1},{1,0},{2,3},{3,2},{4,5},{5,4},{6,7},{7,6},{8,9},{9,8},{10,11... | collective-permute-start | bytes 1572872 | tf_op jit(solution)/shard_map/ppermute | solution.py:804
  495.9 17.1 %collective-permute-start.34 = (bf16[64,1536]{1,0:T(8,128)(2,1)}, bf16[64,1536]{1,0:T(8,128)(2,1)S(1)}, u32[]{:S(2)}, u32[]{:S(2)}) collective-permute-start(bf16[64,1536]{1,0:T(8,128)(2,1)} %bitcast.226), channel_id=1, source_target_pairs={{0,8},{2,10},{4,12},{6,14},{8,0},{10,2},{12,4},{14,6},{16,24},{18,... | collective-permute-start | bytes 589832 | tf_op jit(solution)/shard_map/ppermute | solution.py:804
  496.6 16.5 %collective-permute-start.35 = (bf16[64,1536]{1,0:T(8,128)(2,1)}, bf16[64,1536]{1,0:T(8,128)(2,1)S(1)}, u32[]{:S(2)}, u32[]{:S(2)}) collective-permute-start(bf16[64,1536]{1,0:T(8,128)(2,1)} %bitcast.225), channel_id=1, source_target_pairs={{0,2},{2,0},{4,6},{6,4},{8,10},{10,8},{12,14},{14,12},{16,18},{18,... | collective-permute-start | bytes 589832 | tf_op jit(solution)/shard_map/ppermute | solution.py:804
  497.6 15.5 %collective-permute-start.36 = (bf16[64,1024]{1,0:T(8,128)(2,1)}, bf16[64,1024]{1,0:T(8,128)(2,1)S(1)}, u32[]{:S(2)}, u32[]{:S(2)}) collective-permute-start(bf16[64,1024]{1,0:T(8,128)(2,1)} %bitcast.227), channel_id=1, source_target_pairs={{0,4},{2,6},{4,0},{6,2},{8,12},{10,14},{12,8},{14,10},{16,20},{18,... | collective-permute-start | bytes 393224 | tf_op jit(solution)/shard_map/ppermute | solution.py:804
  497.8 29.9 %collective-permute-start.40 = (bf16[32,4096]{1,0:T(8,128)(2,1)}, bf16[32,4096]{1,0:T(8,128)(2,1)S(1)}, u32[]{:S(2)}, u32[]{:S(2)}) collective-permute-start(bf16[32,4096]{1,0:T(8,128)(2,1)} %bitcast.223), channel_id=1, source_target_pairs={{0,16},{2,18},{4,20},{6,22},{8,24},{10,26},{12,28},{14,30},{16,0},... | collective-permute-start | bytes 786440 | tf_op jit(solution)/shard_map/ppermute | solution.py:804
  503.5 31.6 %collective-permute-start.41 = (bf16[32,4096]{1,0:T(8,128)(2,1)}, bf16[32,4096]{1,0:T(8,128)(2,1)S(1)}, u32[]{:S(2)}, u32[]{:S(2)}) collective-permute-start(bf16[32,4096]{1,0:T(8,128)(2,1)} %bitcast.222), channel_id=1, source_target_pairs={{0,16},{2,18},{4,20},{6,22},{8,24},{10,26},{12,28},{14,30},{16,0},... | collective-permute-start | bytes 786440 | tf_op jit(solution)/shard_map/ppermute | solution.py:804
  516.6 24.0 %collective-permute-start.37 = (bf16[32,1536]{1,0:T(8,128)(2,1)}, bf16[32,1536]{1,0:T(8,128)(2,1)S(1)}, u32[]{:S(2)}, u32[]{:S(2)}) collective-permute-start(bf16[32,1536]{1,0:T(8,128)(2,1)} %bitcast.230), channel_id=1, source_target_pairs={{0,16},{2,18},{4,20},{6,22},{8,24},{10,26},{12,28},{14,30},{16,0},... | collective-permute-start | bytes 294920 | tf_op jit(solution)/shard_map/ppermute | solution.py:804
  519.5 21.1 %collective-permute-start.38 = (bf16[32,1536]{1,0:T(8,128)(2,1)}, bf16[32,1536]{1,0:T(8,128)(2,1)S(1)}, u32[]{:S(2)}, u32[]{:S(2)}) collective-permute-start(bf16[32,1536]{1,0:T(8,128)(2,1)} %bitcast.229), channel_id=1, source_target_pairs={{0,16},{2,18},{4,20},{6,22},{8,24},{10,26},{12,28},{14,30},{16,0},... | collective-permute-start | bytes 294920 | tf_op jit(solution)/shard_map/ppermute | solution.py:804
  519.6 21.0 %collective-permute-start.39 = (bf16[32,1024]{1,0:T(8,128)(2,1)}, bf16[32,1024]{1,0:T(8,128)(2,1)S(1)}, u32[]{:S(2)}, u32[]{:S(2)}) collective-permute-start(bf16[32,1024]{1,0:T(8,128)(2,1)} %bitcast.231), channel_id=1, source_target_pairs={{0,16},{2,18},{4,20},{6,22},{8,24},{10,26},{12,28},{14,30},{16,0},... | collective-permute-start | bytes 196616 | tf_op jit(solution)/shard_map/ppermute | solution.py:804
  523.8 21.2 %all-to-all-start.2 = ((f32[32,1,1280]{2,1,0:T(1,128)}), f32[32,1,1280]{2,1,0:T(1,128)S(1)}, u32[]{:S(2)}, u32[]{:S(2)}) async-start(f32[32,1,1280]{2,1,0:T(1,128)} %reshape.669), calls=%async_computation.2 | async-start | bytes 327680 | tf_op jit(solution)/shard_map/all_to_all | solution.py:1205
  (54 other events, 289.1 us)
Sparse Core Ops, SparseCore 0:
  70.3 130.8 all-gather.2
  391.8 65.4 all-gather.4

commit v4 on v3

--- a/solution.py
+++ b/solution.py
@@ -230,7 +230,7 @@
     width = tokens.shape[1]
     block = ordered.shape[1]
     per = width // block
-    share = 3 * per // parts
+    share = 4 * per // parts
     rows = 256
 
     @pl.when(step == 0)
@@ -286,7 +286,7 @@
     count, width = tokens.shape
     per = width // block
     pieces, parts = len(weights[0]), len(weights)
-    share = 3 * per // parts
+    share = 4 * per // parts
     column = lambda rows, first, number: pl.BlockSpec(
         (rows, block), lambda s, p: (0, jnp.clip(s - first, 0, number - 1))
     )
@@ -296,7 +296,7 @@
         functools.partial(qkv_kernel, pieces=pieces, parts=parts),
         grid_spec=dict(
             num_scalar_prefetch=1,
-            grid=(3 * per,),
+            grid=(4 * per,),
             in_specs=[whole(tokens), whole(member), whole(modulation)]
             + [column(w.shape[0], i * share, share) for i in range(parts) for w in weights[i]]
             + [column(8, 0, per)],
@@ -306,7 +306,7 @@
             + [pl.BlockSpec((width, block), lambda s, p: (0, s))],
         ),
         out_shape=[jax.ShapeDtypeStruct((count, width), BF)] * 6
-        + [jax.ShapeDtypeStruct((width, 3 * width), BF)],
+        + [jax.ShapeDtypeStruct((width, 4 * width), BF)],
         compiler_params=params(),
         cost_estimate=cost(6 * count * width * width, 2 * (13 * count * width)),
         name="qkv_forward",
@@ -338,14 +338,13 @@
             at = pl.multiple_of(j * kb, kb)
             there = pl.ds(at, kb)
             place = at + lax.broadcasted_iota(jnp.int32, (qb, kb), 1)
-            seen = (place >= low) & (place < high)
-            out = []
-            for h in range(2 * pairs):
-                pair = h // 2
-                s = nt(qm[h, here, :], k[there, pair * PAIR : (pair + 1) * PAIR])
-                p = jnp.where(seen, jnp.exp(s), 0.0).astype(BF)
-                out.append(totals[h] + nn(p, v_ext[h, there, :]))
-            return tuple(out)
+            seen = jnp.where((place >= low) & (place < high), 1.0, 0.0).astype(BF)
+            lanes = [slice(h // 2 * PAIR, (h // 2 + 1) * PAIR) for h in range(2 * pairs)]
+            scores = [nt(qm[h, here, :], k[there, lanes[h]]) for h in range(2 * pairs)]
+            probs = [jnp.exp(s).astype(BF) * seen for s in scores]
+            return tuple(
+                total + nn(p, v_ext[h, there, :]) for h, (total, p) in enumerate(zip(totals, probs))
+            )
 
         totals = lax.fori_loop(
             span[0, i], span[1, i], step, tuple(jnp.zeros((qb, PAIR), F32) for _ in range(2 * pairs))
@@ -398,22 +397,25 @@
 
 def attn_bwd_kernel(
     span, q, k, v, do, start, end, inverse, delta, rq, rk, scale,
-    dq, dk, dv, scale_grad, qm, km, dom, dq_acc, dk_acc, dv_acc, *, qb, kb,
+    dq, dk, dv, scale_grad, qm, dom, kt, dq_acc, dk_acc, dv_acc, *, qb, kb,
 ):
     count = q.shape[0]
     pairs = q.shape[1] // PAIR
     for pair in range(pairs):
         lanes = slice(pair * PAIR, (pair + 1) * PAIR)
-        for h in range(2):
-            qm[2 * pair + h] = lane_masked(q[:, lanes], h)
-            km[2 * pair + h] = lane_masked(k[:, lanes], h)
-            dom[2 * pair + h] = lane_masked(do[:, lanes], h)
+        for at in range(0, count, qb):
+            for h in range(2):
+                put = slice(2 * at + h * qb, 2 * at + (h + 1) * qb)
+                qm[pair, put, :] = lane_masked(q[at : at + qb, lanes], h)
+                dom[pair, put, :] = lane_masked(do[at : at + qb, lanes], h)
+    kt[...] = jnp.transpose(k[...])
     dk_acc[...] = jnp.zeros_like(dk_acc)
     dv_acc[...] = jnp.zeros_like(dv_acc)
 
-    def one_block(i, _):
-        first = pl.multiple_of(i * qb, qb)
-        here = pl.ds(first, qb)
+    def one_block(i, total):
+        here = pl.ds(pl.multiple_of(i * qb, qb), qb)
+        twice = pl.ds(pl.multiple_of(i * (2 * qb), 2 * qb), 2 * qb)
+        one = [pl.ds(pl.multiple_of(i * (2 * qb) + h * qb, qb), qb) for h in range(2)]
         low, high = start[0:1, here], end[0:1, here]
         dq_acc[...] = jnp.zeros_like(dq_acc)
 
@@ -421,33 +423,32 @@
             at = pl.multiple_of(j * kb, kb)
             there = pl.ds(at, kb)
             place = at + lax.broadcasted_iota(jnp.int32, (kb, qb), 0)
-            seen = (place >= low) & (place < high)
+            seen = jnp.where((place >= low) & (place < high), 1.0, 0.0).astype(BF)
             for pair in range(pairs):
                 lanes = slice(pair * PAIR, (pair + 1) * PAIR)
-                ps, dss = [], []
-                for h in (2 * pair, 2 * pair + 1):
-                    s = nt(k[there, lanes], qm[h, here, :])
-                    p = jnp.where(seen, jnp.exp(s) * inverse[0, h : h + 1, here], 0.0)
-                    dp = nt(v[there, lanes], dom[h, here, :])
-                    ps.append(p.astype(BF))
-                    dss.append((p * (dp - delta[0, h : h + 1, here])).astype(BF))
-                dv_acc[there, lanes] += nn(ps[0], dom[2 * pair, here, :]) + nn(ps[1], dom[2 * pair + 1, here, :])
-                dk_acc[there, lanes] += nn(dss[0], qm[2 * pair, here, :]) + nn(dss[1], qm[2 * pair + 1, here, :])
-                dq_acc[:, lanes] += tn(dss[0], km[2 * pair, there, :]) + tn(dss[1], km[2 * pair + 1, there, :])
+                heads = (2 * pair, 2 * pair + 1)
+                s = [nt(k[there, lanes], qm[pair, x, :]) for x in one]
+                dp = [nt(v[there, lanes], dom[pair, x, :]) for x in one]
+                p = [jnp.exp(x) * inverse[0, h : h + 1, here] for x, h in zip(s, heads)]
+                ds = [x * (y - delta[0, h : h + 1, here]) for x, y, h in zip(p, dp, heads)]
+                p = [x.astype(BF) * seen for x in p]
+                ds = [x.astype(BF) * seen for x in ds]
+                dv_acc[there, lanes] += nn(jnp.concatenate(p, axis=1), dom[pair, twice, :])
+                dk_acc[there, lanes] += nn(jnp.concatenate(ds, axis=1), qm[pair, twice, :])
+                for x, h in zip(ds, heads):
+                    rows = slice(h * HEAD, (h + 1) * HEAD)
+                    dq_acc[rows, :] += nn(kt[rows, there], x)
             return 0
 
         lax.fori_loop(span[0, i], span[1, i], step, 0)
-        g = dq_acc[...]
+        g = jnp.transpose(dq_acc[...])
         sc = scale[0:1, :]
         unit = q[here, :].astype(F32) / sc
         inner = head_sums(unit * g)
         dq[here, :] = (sc * rq[here, :].astype(F32) * (g - unit * inner)).astype(BF)
-        return jnp.sum(inner, axis=0, keepdims=True)
-
-    def looped(i, total):
-        return total + one_block(i, 0)
-
-    total = lax.fori_loop(0, count // qb, looped, jnp.zeros((1, q.shape[1]), F32))
+        return total + jnp.sum(inner, axis=0, keepdims=True)
+
+    total = lax.fori_loop(0, count // qb, one_block, jnp.zeros((1, q.shape[1]), F32))
     scale_grad[...] = jnp.broadcast_to(total, scale_grad.shape)
     for at in range(0, count, qb):
         here = pl.ds(at, qb)
@@ -478,8 +479,8 @@
             + [column] * 2
             + [pl.BlockSpec((8, lanes), lambda g, s: (0, first + g))],
             out_specs=[out] * 3 + [pl.BlockSpec((8, lanes), lambda g, s: (0, g))],
-            scratch_shapes=[pltpu.VMEM((GROUP, count, PAIR), BF)] * 3
-            + [pltpu.VMEM((qb, lanes), F32)]
+            scratch_shapes=[pltpu.VMEM((GROUP // 2, 2 * count, PAIR), BF)] * 2
+            + [pltpu.VMEM((lanes, count), BF), pltpu.VMEM((lanes, qb), F32)]
             + [pltpu.VMEM((count, lanes), F32)] * 2,
         ),
         out_shape=[jax.ShapeDtypeStruct((count, groups * lanes), BF)] * 3
@@ -515,7 +516,7 @@
             some,
             pl.BlockSpec((rows, member.shape[1]), lambda s: (s, 0)),
             whole(modulation),
-            pl.BlockSpec((width, width), lambda s: (0, 0)),
+            pl.BlockSpec((width, width), lambda s: (0, 3)),
         ],
         out_specs=[some] * 4,
         out_shape=[
@@ -575,10 +576,10 @@
 
 def mlp_call(core, hidden, down, packed, own, split, first, count_of, block=512, rows=256):
     count, width = hidden.shape
-    units = (packed.shape[1] - width) // 2
+    units = packed.shape[1] // 2
     per = width // block
     whole = pl.BlockSpec((count, width), lambda s, c: (0, 0))
-    first_up, first_down = width // block + first * per, (width + units) // width + first
+    first_up, first_down = first * per, units // width + first
     kept = 2 if split else 1
     copies = 2 if split else 1
     wide = pl.BlockSpec((width // kept, block), lambda s, c: (0, s))
@@ -667,7 +668,7 @@
             pl.BlockSpec((rows, member.shape[1]), lambda s: (s, 0)),
             pl.BlockSpec((items, rows), lambda s: (0, s)),
             whole(modulation),
-            pl.BlockSpec((width, width), lambda s: (0, 0)),
+            pl.BlockSpec((width, width), lambda s: (0, 3)),
         ],
         out_specs=[some] * 4
         + [
@@ -1022,7 +1023,7 @@
     table_shard = jnp.concatenate([class_table, label_block], axis=1)
     up_shard = fc1_weight.reshape(own, devices, blocks, own).transpose(0, 2, 1, 3)
     feed_shard = jnp.concatenate(
-        [proj_weight, up_shard.reshape(own, -1)]
+        [up_shard.reshape(own, -1)]
         + [fc2_weight[i * own : (i + 1) * own] for i in range(blocks)],
         axis=1,
     )
@@ -1031,29 +1032,25 @@
         orders = [chip_order(sizes["wide"], turn)[::-1] for turn in (0, 1)]
         orders.append([orders[0][0]] + orders[0][1:])
         stages = len(orders[0])
-        both = Gather(jnp.concatenate([table_shard, qkv_weight], axis=1)[None], sizes, orders[0][:1])
+        both = Gather(jnp.concatenate([table_shard, qkv_weight, proj_weight], axis=1)[None], sizes, orders[0][:1])
         both.send()
         land([both])
-        cuts = (0, width + PAIR, width + PAIR + 3 * width // 2, 4 * width + PAIR)
+        cuts = (0, width + PAIR, 3 * width + PAIR, 5 * width + PAIR)
         table_move, *moves = (
             Gather(both.block[:, :, low:high], sizes, order[1:])
             for low, high, order in zip(cuts, cuts[1:], orders)
         )
-        for move in (table_move, *moves):
-            move.send()
+        table_move.send()
+        land([table_move])
         for step in range(1, stages):
-            land([table_move])
-            table_move.send()
+            for move in (table_move, *moves):
+                move.send()
+            if step == 1:
+                await_all(ada_columns)
             if step < stages - 1:
-                await_all(done[0])
-                if step == 1:
-                    await_all(ada_columns)
-                land(moves)
-                for move in moves:
-                    move.send()
-                await_all(done[0])
+                land([table_move, *moves])
             if step == stages - 2:
-                feed_shard, table_move.got = lax.optimization_barrier((feed_shard, table_move.got))
+                feed_shard, table_move.block = lax.optimization_barrier((feed_shard, table_move.block))
         tables = [h.reshape(-1, width + PAIR) for h in table_move.halves()]
     else:
         orders = [()]
@@ -1070,7 +1067,9 @@
         owners = jnp.arange(devices, dtype=jnp.int32)
         places = jnp.stack([relative_place(owners, me, o) for o in orders[1:]]).astype(jnp.int32)
     else:
-        weights = [(lax.all_gather(qkv_weight, BOTH, axis=0, tiled=True),)]
+        weights = [
+            (lax.all_gather(jnp.concatenate([qkv_weight, proj_weight], axis=1), BOTH, axis=0, tiled=True),)
+        ]
         places = jnp.zeros((1, devices), jnp.int32)
     feed_weight = lax.all_gather(feed_shard, BOTH, axis=0, tiled=True)
 
@@ -1090,14 +1089,14 @@
     ).astype(jnp.int32)
     scale_lanes = jnp.broadcast_to(jnp.repeat(head_scale, width // head_count)[None], (8, width))
 
-    hidden_one, q, k, v, rq, rk, qkv_full = qkv_call(
+    hidden_one, q, k, v, rq, rk, ordered = qkv_call(
         places, tokens, member, terms, weights, scale_lanes
     )
     mixed, rest, inverse = attn_fwd_call(
         span, q, k, v, first.reshape(count, 1), last.reshape(count, 1), tile, tile
     )
     after, branch, hidden_two, down = proj_call(
-        tokens, mixed, cotangent, member, terms, feed_weight
+        tokens, mixed, cotangent, member, terms, ordered
     )
     mlp, back, *grads = mlp_call(flags, hidden_two, down, feed_weight, own, paired, 0, blocks)
     swap = lambda x: flip(x, "narrow", sizes["narrow"], 0)
@@ -1107,7 +1106,7 @@
             for turn, kept, sent in ((0, *grads[:2]), (1, *grads[2:]))
         )
     output, grad_in, branch_grad, mixed_grad, delta, sums = middle_call(
-        mlp, back, after, cotangent, branch, mixed, rest, member, turned, terms, feed_weight
+        mlp, back, after, cotangent, branch, mixed, rest, member, turned, terms, ordered
     )
     early = jnp.pad(sums[:slots], ((0, rows - slots), (0, 0))).astype(BF)
     early = lax.all_gather(early, BOTH, axis=0, tiled=True)
@@ -1146,7 +1145,7 @@
         qkv_grad = owner_sum(qkv_parts[0], BOTH).astype(F32)
         proj_grad = owner_sum(proj_parts[0], BOTH).astype(F32)
     tokens_grad, first_sums = first_call(
-        heads, qkv_full, tokens, grad_in, member, turned, terms
+        heads, ordered, tokens, grad_in, member, turned, terms
     )
     late = jnp.pad(first_sums[:slots], ((0, rows - slots), (0, 0))).astype(BF)
     own_width = width // devices

time: 563 us -> 539 us (0.957)
  waiting for transfers between devices: 105 us -> 83.4 us
  Pallas kernels: 330 us -> 313 us
  starting transfers between devices: 61.7 us -> 73.9 us
    pallas_call x30 -> x28, Pallas kernels: 330 us -> 313 us  [run(): mark, *result = call(*args, *waits)]
    ppermute x42, waiting for transfers between devices: 93.7 us -> 79.3 us  [flip(): return lax.ppermute(values, axis, [(i, i ^ 1 << bit) for i in range(size)])]
    ppermute x42, starting transfers between devices: 50 us -> 59.7 us  [flip(): return lax.ppermute(values, axis, [(i, i ^ 1 << bit) for i in range(size)])]
    all_gather x1, waiting for transfers between devices: 10.9 us -> 4.01 us  [per_device(): feed_weight = lax.all_gather(feed_shard, BOTH, axis=0, tiled=True)]
    unnamed x118 -> x117, local copies, waits for them, and re-layouts: 18.5 us -> 18.9 us
  transfers between devices with their start and end apart: 47 -> 47, of which waited for: 21 -> 18; matrix products, arithmetic and copies ran while one was open for 4% -> 4% of each run, Pallas kernels for 40% -> 40%
where the time goes in v4:
time: 539 us; the launch traced here: 530 us
  Pallas kernels  313 us (58%)
  waiting for transfers between devices  83.4 us (15%)
  starting transfers between devices  73.9 us (14%)
  local copies, waits for them, and re-layouts  33.6 us (6%)
  between operations  15.2 us (3%)
  other arithmetic  11.3 us (2%)
    pallas_call x28, Pallas kernels, run(): mark, *result = call(*args, *waits)  313 us
    ppermute x42, waiting for transfers between devices, flip(): return lax.ppermute(values, axis, [(i, i ^ 1 << bit) for i in range(size)])  79.3 us
    ppermute x42, starting transfers between devices, flip(): return lax.ppermute(values, axis, [(i, i ^ 1 << bit) for i in range(size)])  59.7 us
    unnamed x117, local copies, waits for them, and re-layouts  18.9 us
  transfers between devices with their start and end apart: 47, of which 18 were waited for; matrix products, arithmetic and copies ran while one was open for 4% of the time, Pallas kernels for 40%

profile of v4, /device:TPU:0, one launch (start us, length us, event | category | flops | bytes accessed | tf_op | source)
XLA Modules:
  0.0 530.4 jit_solution(17980202216742779937)
XLA Ops:
  9.1 4.1 collective-permute-start
  15.9 3.8 all-to-all-start
  22.0 12.8 %collective-permute-done.refs_1_ = bf16[1,32,5248]{2,1,0:T(8,128)(2,1)S(1)} collective-permute-done((bf16[1,32,5248]{2,1,0:T(8,128)(2,1)S(1)}, bf16[1,32,5248]{2,1,0:T(8,128)(2,1)S(1)}, u32[]{:S(2)}, u32[]{:S(2)}) %collective-permute-start) | collective-permute-done | bytes 335904 | tf_op jit(solution)/shard_map/ppermute | solution.py:805
  41.5 2.0 collective-permute-start.4
  46.6 2.2 collective-permute-start.2
  49.2 4.5 collective-permute-done.2.refs_3_
  54.4 2.6 land.11
  57.0 2.6 collective-permute-start.5
  61.3 7.8 %collective-permute-done.6.refs_4_ = bf16[4,32,2048]{2,1,0:T(8,128)(2,1)S(1)} collective-permute-done((bf16[4,32,2048]{2,1,0:T(8,128)(2,1)}, bf16[4,32,2048]{2,1,0:T(8,128)(2,1)S(1)}, u32[]{:S(2)}, u32[]{:S(2)}) %collective-permute-start.6) | collective-permute-done | bytes 524320 | tf_op jit(solution)/shard_map/ppermute | solution.py:805
  70.8 3.7 land.12
  78.2 5.2 modulation.1
  83.4 6.8 %all-to-all-start.1 = ((f32[32,8,192]{2,1,0:T(8,128)}), f32[32,8,192]{2,1,0:T(8,128)S(1)}, u32[]{:S(2)}, u32[]{:S(2)}) async-start(f32[32,8,192]{2,1,0:T(8,128)} %bitcast.197), calls=%async_computation.1 | async-start | bytes 524288 | tf_op jit(solution)/shard_map/all_to_all | solution.py:1076
  94.0 14.1 %collective-permute-done.10.refs_3_ = bf16[8,32,2048]{2,1,0:T(8,128)(2,1)S(1)} collective-permute-done((bf16[8,32,2048]{2,1,0:T(8,128)(2,1)}, bf16[8,32,2048]{2,1,0:T(8,128)(2,1)S(1)}, u32[]{:S(2)}, u32[]{:S(2)}) %collective-permute-start.10) | collective-permute-done | bytes 1048608 | tf_op jit(solution)/shard_map/ppermute | solution.py:805
  110.5 4.8 land.13
  117.3 5.2 collective-permute-done.11
  124.0 26.4 %qkv_forward.1 = (f32[8,128]{1,0:T(8,128)}, bf16[1024,1024]{1,0:T(8,128)(2,1)}, bf16[1024,1024]{1,0:T(8,128)(2,1)}, bf16[1024,1024]{1,0:T(8,128)(2,1)}, bf16[102...) custom-call(s32[2,32]{1,0:T(2,128)} %pad_add_fusion.1.refs_0_, ...), custom_call_target="tpu_custom_call" | custom-call | flops 6442450944 | bytes 27262976 | tf_op jit(solution)/shard_map/qkv_forward/pallas_call | solution.py:79
  150.3 32.6 %attention_forward.1 = (f32[8,128]{1,0:T(8,128)}, bf16[1024,1024]{1,0:T(8,128)(2,1)}, bf16[1024,1024]{1,0:T(8,128)(2,1)}, f32[4,8,1024]{2,1,0:T(8,128)}) custom-call(s32[2,4]{1,0:T(2,128)} %pad_add_fusion.refs_0_, bf16[1024,1024]{1,0:T(8,128)(2,1)} %get-tuple-element.167.refs_1_, bf16[1024,1024]{1,0:T(8,128)(2,1)} %get-tuple-element.168.refs_2_, ...), custom_call_target="tpu_custom_call" | custom-call | flops 17179869184 | bytes 8388608 | tf_op jit(solution)/shard_map/attention_forward/pallas_call | solution.py:79
  182.9 10.0 %projection.1 = (f32[8,128]{1,0:T(8,128)}, f32[1024,1024]{1,0:T(8,128)}, bf16[1024,1024]{1,0:T(8,128)(2,1)}, bf16[1024,1024]{1,0:T(8,128)(2,1)}, bf16[1024,1024]{1,0:T(8,128)(2,1)}) custom-call(bf16[1024,1024]{1,0:T(8,128)(2,1)} %refs_4_.1, bf16[1024,1024]{1,0:T(8,128)(2,1)} %get-tuple-element.170.refs_1_.refs_5_, bf16[1024,1024]{1,0:T(8,128)(2,1)} %refs_3_.1, ...), custom_call_target="tpu_custom_call" | custom-call | flops 2147483648 | bytes 16777216 | tf_op jit(solution)/shard_map/projection/pallas_call | solution.py:79
  192.9 4.0 all-gather.3.cloned.1.call-done.refs_3_.refs_4_
  196.9 64.0 %feed_forward.1 = (f32[8,128]{1,0:T(8,128)}, f32[1024,1024]{1,0:T(8,128)}, f32[1024,1024]{1,0:T(8,128)}, bf16[512,4096]{1,0:T(8,128)(2,1)}, bf16[512,4096]{1,0:T...) custom-call(s32[6]{0:T(128)} %stack.32.refs_0_, bf16[1024,1024]{1,0:T(8,128)(2,1)} %get-tuple-element.172.refs_1_, ...), custom_call_target="tpu_custom_call" | custom-call | flops 51539607552 | bytes 20971520 | tf_op jit(solution)/shard_map/feed_forward/pallas_call | solution.py:79
  262.1 17.5 %middle.1 = (f32[8,128]{1,0:T(8,128)}, bf16[1024,1024]{1,0:T(8,128)(2,1)}, f32[1024,1024]{1,0:T(8,128)}, bf16[1024,1024]{1,0:T(8,128)(2,1)}, bf16[1024,1024]{1,0...) custom-call(f32[1024,1024]{1,0:T(8,128)} %get-tuple-element.175.refs_0_, ...), custom_call_target="tpu_custom_call" | custom-call | flops 4294967296 | bytes 31457280 | tf_op jit(solution)/shard_map/middle/pallas_call | solution.py:79
  281.6 11.5 %halving_sum.6 = (f32[8,128]{1,0:T(8,128)}, bf16[8,32,4096]{2,1,0:T(8,128)(2,1)}, bf16[8,32,4096]{2,1,0:T(8,128)(2,1)}, bf16[4,64,4096]{2,1,0:T(8,128)(2,1)}, bf16[4,64,4096]{2,1,0:T(8,128)(2,1)}) custom-call(s32[6]{0:T(128)} %stack.32.refs_0_, bf16[8,2,32,4096]{3,2,1,0:T(8,128)(2,1)} %bitcast.119, bf16[8,2,32,4096]{3,2,1,0:T(8,128)(2,1)} %bitcast.123, ...), custom_call_target="tpu_custom_call" | custom-call | flops 4194304 | bytes 25165824 | tf_op jit(solution)/shard_map/halving_sum/pallas_call | solution.py:79
  295.2 49.6 %attention_backward.1 = (f32[8,128]{1,0:T(8,128)}, bf16[1024,1024]{1,0:T(8,128)(2,1)}, bf16[1024,1024]{1,0:T(8,128)(2,1)}, bf16[1024,1024]{1,0:T(8,128)(2,1)}, f32[8,1024]{1,0:T(8,128)}) custom-call(s32[2,4]{1,0:T(2,128)} %pad_add_fusion.refs_0_, bf16[1024,1024]{1,0:T(8,128)(2,1)} %get-tuple-element.167.refs_1_, ...), custom_call_target="tpu_custom_call" | custom-call | flops 42949672960 | bytes 18874368 | tf_op jit(solution)/shard_map/attention_backward/pallas_call | solution.py:79
  346.9 6.5 %halving_sum.7 = (f32[8,128]{1,0:T(8,128)}, bf16[4,32,4096]{2,1,0:T(8,128)(2,1)}, bf16[4,32,4096]{2,1,0:T(8,128)(2,1)}, bf16[2,64,4096]{2,1,0:T(8,128)(2,1)}, bf16[2,64,4096]{2,1,0:T(8,128)(2,1)}) custom-call(s32[6]{0:T(128)} %stack.32.refs_0_, bf16[4,2,32,4096]{3,2,1,0:T(8,128)(2,1)} %bitcast.125, bf16[4,2,32,4096]{3,2,1,0:T(8,128)(2,1)} %bitcast.129, ...), custom_call_target="tpu_custom_call" | custom-call | flops 2097152 | bytes 12582912 | tf_op jit(solution)/shard_map/halving_sum/pallas_call | solution.py:79
  353.4 13.2 %weight_grad.2 = (f32[8,128]{1,0:T(8,128)}, bf16[512,3072]{1,0:T(8,128)(2,1)}, bf16[512,3072]{1,0:T(8,128)(2,1)}) custom-call(s32[6]{0:T(128)} %stack.32.refs_0_, bf16[1024,1024]{1,0:T(8,128)(2,1)} %get-tuple-element.196.refs_1_, bf16[1024,1024]{1,0:T(8,128)(2,1)} %get-tuple-element.192.refs_2_.refs_0_, ...), custom_call_target="tpu_custom_call" | custom-call | flops 6442450944 | bytes 12582912 | tf_op jit(solution)/shard_map/weight_grad/pallas_call | solution.py:79
  368.2 6.8 %weight_grad.3 = (f32[8,128]{1,0:T(8,128)}, bf16[512,1024]{1,0:T(8,128)(2,1)}, bf16[512,1024]{1,0:T(8,128)(2,1)}) custom-call(s32[6]{0:T(128)} %stack.32.refs_0_, bf16[1024,1024]{1,0:T(8,128)(2,1)} %get-tuple-element.170.refs_1_.refs_5_, bf16[1024,1024]{1,0:T(8,128)(2,1)} %get-tuple-element.205.refs_2_, f32[8,128]{1,0:T(8,128)} %get-tuple-element.206.refs_3_), custom_call_target="tpu_custom_call" | custom-call | flops 2147483648 | bytes 4194304 | tf_op jit(solution)/shard_map/weight_grad/pallas_call | solution.py:79
  377.0 2.2 collective-permute-start.24
  381.1 6.7 %halving_sum.8 = (f32[8,128]{1,0:T(8,128)}, bf16[8,32,1536]{2,1,0:T(8,128)(2,1)}, bf16[8,32,1536]{2,1,0:T(8,128)(2,1)}, bf16[4,64,1536]{2,1,0:T(8,128)(2,1)}, bf...) custom-call(s32[6]{0:T(128)} %stack.32.refs_0_, ...), custom_call_target="tpu_custom_call" | custom-call | flops 2097152 | bytes 12582912 | tf_op jit(solution)/shard_map/halving_sum/pallas_call | solution.py:79
  389.4 2.1 collective-permute-start.21
  391.9 16.0 %first_norm_backward.1 = (f32[8,128]{1,0:T(8,128)}, bf16[1024,1024]{1,0:T(8,128)(2,1)}, f32[16,2048]{1,0:T(8,128)}) custom-call(bf16[1024,1024]{1,0:T(8,128)(2,1)} %get-tuple-element.192.refs_2_.refs_0_, bf16[1024,1024]{1,0:T(8,128)(2,1)} %get-tuple-element.193.refs_3_.refs_1_, bf16[1024,1024]{1,0:T(8,128)(2,1)} %get-tuple-element.194.refs_4_.refs_2_, ...), custom_call_target="tpu_custom_call" | custom-call | flops 6442450944 | bytes 18874368 | tf_op jit(solution)/shard_map/first_norm_backward/pallas_call | solution.py:79
  408.8 3.7 collective-permute-start.19
  412.5 8.3 %collective-permute-done.22 = bf16[256,1024]{1,0:T(8,128)(2,1)S(1)} collective-permute-done((bf16[256,1024]{1,0:T(8,128)(2,1)}, bf16[256,1024]{1,0:T(8,128)(2,1)S(1)}, u32[]{:S(2)}, u32[]{:S(2)}) %collective-permute-start.22) | collective-permute-done | bytes 524320 | tf_op jit(solution)/shard_map/ppermute | solution.py:805
  423.0 6.4 %halving_sum.9 = (f32[8,128]{1,0:T(8,128)}, bf16[4,32,1536]{2,1,0:T(8,128)(2,1)}, bf16[4,32,1536]{2,1,0:T(8,128)(2,1)}, bf16[2,64,1536]{2,1,0:T(8,128)(2,1)}, bf...) custom-call(s32[6]{0:T(128)} %stack.32.refs_0_, ...), custom_call_target="tpu_custom_call" | custom-call | flops 2097152 | bytes 12582912 | tf_op jit(solution)/shard_map/halving_sum/pallas_call | solution.py:79
  431.4 4.4 collective-permute-start.25
  435.8 2.5 collective-permute-done.25.refs_1_
  440.7 2.0 collective-permute-start.31
  446.5 2.2 collective-permute-start.29
  450.5 9.7 %collective-permute-done.30 = bf16[128,1024]{1,0:T(8,128)(2,1)S(1)} collective-permute-done((bf16[128,1024]{1,0:T(8,128)(2,1)}, bf16[128,1024]{1,0:T(8,128)(2,1)S(1)}, u32[]{:S(2)}, u32[]{:S(2)}) %collective-permute-start.30) | collective-permute-done | bytes 262176 | tf_op jit(solution)/shard_map/ppermute | solution.py:805
  463.2 4.3 halving_sum.10
  473.7 4.3 collective-permute-start.40
  479.7 7.8 %adaptive_norm_backward.1 = (f32[8,128]{1,0:T(8,128)}, f32[32,6144]{1,0:T(8,128)}, f32[32,40,32]{2,1,0:T(8,128)}) custom-call(s32[6]{0:T(128)} %stack.32.refs_0_, bf16[256,4096]{1,0:T(8,128)(2,1)} %all-gather.5.cloned.1.call-done.refs_1_, bf16[128,2048]{1,0:T(8,128)(2,1)} %bitcast.191, bf16[128,2048]{1,0:T(8,128)(2,1)} %bitcast.192, ...), custom_call_target="tpu_custom_call" | custom-call | flops 1000000000 | bytes 10000000 | tf_op jit(solution)/shard_map/adaptive_norm_backward/pallas_call | solution.py:79
  488.3 2.8 halving_sum.11
  491.1 2.9 collective-permute-start.37
  494.1 2.8 collective-permute-start.39
  498.2 3.0 all-to-all-start.2
  502.2 7.4 %collective-permute-done.41.refs_3_ = bf16[32,4096]{1,0:T(8,128)(2,1)S(1)} collective-permute-done((bf16[32,4096]{1,0:T(8,128)(2,1)}, bf16[32,4096]{1,0:T(8,128)(2,1)S(1)}, u32[]{:S(2)}, u32[]{:S(2)}) %collective-permute-start.41) | collective-permute-done | bytes 262176 | tf_op jit(solution)/shard_map/ppermute | solution.py:805
  510.3 2.7 last_sum.2
  513.0 2.1 collective-permute-done.39.refs_5_
  (250 shorter events, 84.6 us)
Async XLA Ops:
  9.1 25.7 %collective-permute-start = (bf16[1,32,5248]{2,1,0:T(8,128)(2,1)S(1)}, bf16[1,32,5248]{2,1,0:T(8,128)(2,1)S(1)}, u32[]{:S(2)}, u32[]{:S(2)}) collective-permute-start(bf16[1,32,5248]{2,1,0:T(8,128)(2,1)S(1)} %maximum_bitcast_fusion.refs_0_), channel_id=1, source_target_pairs={{0,16},{2,18},{4,20},{6,22},{8,24},{10,26},{12,28},{14,30},{16,0},... | collective-permute-start | bytes 1007624 | tf_op jit(solution)/shard_map/ppermute | solution.py:805
  15.9 33.3 %all-to-all-start = ((bf16[32,32,192]{2,0,1:T(8,128)(2,1)}), bf16[32,32,192]{2,0,1:T(8,128)(2,1)S(1)}, u32[]{:S(2)}, u32[]{:S(2)}) async-start(bf16[32,32,192]{2,0,1:T(8,128)(2,1)} %copy.82), calls=%async_computation | async-start | bytes 1048576 | tf_op jit(solution)/shard_map/all_to_all | solution.py:1030
  19.7 177.2 %all-gather.3.cloned.1.call-start = ((), (), s32[]{:S(2)}) async-start(), calls=%async_computation.3 | async-start | bytes 17301504 | tf_op jit(solution)/shard_map/all_gather | solution.py:1074
  20.8 28.0 %copy-start.36 = (bf16[128,1024]{1,0:T(8,128)(2,1)S(1)}, bf16[128,1024]{1,0:T(8,128)(2,1)}, u32[]{:S(2)}) copy-start(bf16[128,1024]{1,0:T(8,128)(2,1)} %param.23) | copy-start | bytes 786436
  38.4 5.8 %collective-permute-start.1 = (bf16[2,32,1152]{2,1,0:T(8,128)(2,1)S(1)}, bf16[2,32,1152]{2,1,0:T(8,128)(2,1)S(1)}, u32[]{:S(2)}, u32[]{:S(2)}) collective-permute-start(bf16[2,32,1152]{2,1,0:T(8,128)(2,1)S(1)} %slice.95.refs_0_), channel_id=1, source_target_pairs={{0,8},{2,10},{4,12},{6,14},{8,0},{10,2},{12,4},{14,6},{16,24},{18,... | collective-permute-start | bytes 442376 | tf_op jit(solution)/shard_map/ppermute | solution.py:805
  39.6 9.3 %collective-permute-start.3 = (bf16[2,32,2048]{2,1,0:T(8,128)(2,1)S(1)}, bf16[2,32,2048]{2,1,0:T(8,128)(2,1)S(1)}, u32[]{:S(2)}, u32[]{:S(2)}) collective-permute-start(bf16[2,32,2048]{2,1,0:T(8,128)(2,1)S(1)} %get-tuple-element.278.refs_1_), channel_id=1, source_target_pairs={{0,2},{2,0},{4,6},{6,4},{8,10},{10,8},{12,14},{14,12},{16,18},{18,... | collective-permute-start | bytes 786440 | tf_op jit(solution)/shard_map/ppermute | solution.py:805
  41.5 7.8 %collective-permute-start.4 = (bf16[2,32,2048]{2,1,0:T(8,128)(2,1)S(1)}, bf16[2,32,2048]{2,1,0:T(8,128)(2,1)S(1)}, u32[]{:S(2)}, u32[]{:S(2)}) collective-permute-start(bf16[2,32,2048]{2,1,0:T(8,128)(2,1)S(1)} %get-tuple-element.277.refs_2_), channel_id=1, source_target_pairs={{0,8},{2,10},{4,12},{6,14},{8,0},{10,2},{12,4},{14,6},{16,24},{18,... | collective-permute-start | bytes 786440 | tf_op jit(solution)/shard_map/ppermute | solution.py:805
  46.6 7.2 %collective-permute-start.2 = (bf16[4,32,1152]{2,1,0:T(8,128)(2,1)}, bf16[4,32,1152]{2,1,0:T(8,128)(2,1)S(1)}, u32[]{:S(2)}, u32[]{:S(2)}) collective-permute-start(bf16[4,32,1152]{2,1,0:T(8,128)(2,1)} %get-tuple-element.155.refs_0_), channel_id=1, source_target_pairs={{0,4},{2,6},{4,0},{6,2},{8,12},{10,14},{12,8},{14,10},{16,20},{18,... | collective-permute-start | bytes 884744 | tf_op jit(solution)/shard_map/ppermute | solution.py:805
  57.0 12.1 %collective-permute-start.5 = (bf16[8,32,1152]{2,1,0:T(8,128)(2,1)}, bf16[8,32,1152]{2,1,0:T(8,128)(2,1)S(1)}, u32[]{:S(2)}, u32[]{:S(2)}) collective-permute-start(bf16[8,32,1152]{2,1,0:T(8,128)(2,1)} %get-tuple-element.156.refs_0_), channel_id=1, source_target_pairs={{0,2},{2,0},{4,6},{6,4},{8,10},{10,8},{12,14},{14,12},{16,18},{18,... | collective-permute-start | bytes 1769480 | tf_op jit(solution)/shard_map/ppermute | solution.py:805
  59.6 9.4 %collective-permute-start.6 = (bf16[4,32,2048]{2,1,0:T(8,128)(2,1)}, bf16[4,32,2048]{2,1,0:T(8,128)(2,1)S(1)}, u32[]{:S(2)}, u32[]{:S(2)}) collective-permute-start(bf16[4,32,2048]{2,1,0:T(8,128)(2,1)} %get-tuple-element.157.refs_1_), channel_id=1, source_target_pairs={{0,8},{2,10},{4,12},{6,14},{8,0},{10,2},{12,4},{14,6},{16,24},{18,... | collective-permute-start | bytes 1572872 | tf_op jit(solution)/shard_map/ppermute | solution.py:805
  59.6 9.5 %collective-permute-start.7 = (bf16[4,32,2048]{2,1,0:T(8,128)(2,1)}, bf16[4,32,2048]{2,1,0:T(8,128)(2,1)S(1)}, u32[]{:S(2)}, u32[]{:S(2)}) collective-permute-start(bf16[4,32,2048]{2,1,0:T(8,128)(2,1)} %get-tuple-element.158.refs_2_), channel_id=1, source_target_pairs={{0,4},{2,6},{4,0},{6,2},{8,12},{10,14},{12,8},{14,10},{16,20},{18,... | collective-permute-start | bytes 1572872 | tf_op jit(solution)/shard_map/ppermute | solution.py:805
  74.9 3.2 collective-permute-start.8
  76.1 32.0 %collective-permute-start.10 = (bf16[8,32,2048]{2,1,0:T(8,128)(2,1)}, bf16[8,32,2048]{2,1,0:T(8,128)(2,1)S(1)}, u32[]{:S(2)}, u32[]{:S(2)}) collective-permute-start(bf16[8,32,2048]{2,1,0:T(8,128)(2,1)} %get-tuple-element.163.refs_1_), channel_id=1, source_target_pairs={{0,2},{2,0},{4,6},{6,4},{8,10},{10,8},{12,14},{14,12},{16,18},{18,... | collective-permute-start | bytes 3145736 | tf_op jit(solution)/shard_map/ppermute | solution.py:805
  77.6 31.9 %collective-permute-start.9 = (bf16[8,32,2048]{2,1,0:T(8,128)(2,1)}, bf16[8,32,2048]{2,1,0:T(8,128)(2,1)S(1)}, u32[]{:S(2)}, u32[]{:S(2)}) collective-permute-start(bf16[8,32,2048]{2,1,0:T(8,128)(2,1)} %get-tuple-element.162.refs_0_), channel_id=1, source_target_pairs={{0,4},{2,6},{4,0},{6,2},{8,12},{10,14},{12,8},{14,10},{16,20},{18,... | collective-permute-start | bytes 3145736 | tf_op jit(solution)/shard_map/ppermute | solution.py:805
  83.4 32.9 %all-to-all-start.1 = ((f32[32,8,192]{2,1,0:T(8,128)}), f32[32,8,192]{2,1,0:T(8,128)S(1)}, u32[]{:S(2)}, u32[]{:S(2)}) async-start(f32[32,8,192]{2,1,0:T(8,128)} %bitcast.197), calls=%async_computation.1 | async-start | bytes 524288 | tf_op jit(solution)/shard_map/all_to_all | solution.py:1076
  90.2 389.5 %all-gather.5.cloned.1.call-start = ((), (), s32[]{:S(2)}) async-start(), calls=%async_computation.4 | async-start | bytes 2162688 | tf_op jit(solution)/shard_map/all_gather | solution.py:1112
  115.3 7.3 %collective-permute-start.11 = (bf16[16,32,2048]{2,1,0:T(8,128)(2,1)}, bf16[16,32,2048]{2,1,0:T(8,128)(2,1)S(1)}, u32[]{:S(2)}, u32[]{:S(2)}) collective-permute-start(bf16[16,32,2048]{2,1,0:T(8,128)(2,1)} %get-tuple-element.165), channel_id=1, source_target_pairs={{0,1},{1,0},{2,3},{3,2},{4,5},{5,4},{6,7},{7,6},{8,9},{9,8},{10,11... | collective-permute-start | bytes 6291464 | tf_op jit(solution)/shard_map/ppermute | solution.py:805
  115.3 7.5 %collective-permute-start.12 = (bf16[16,32,2048]{2,1,0:T(8,128)(2,1)}, bf16[16,32,2048]{2,1,0:T(8,128)(2,1)}, u32[]{:S(2)}, u32[]{:S(2)}) collective-permute-start(bf16[16,32,2048]{2,1,0:T(8,128)(2,1)} %get-tuple-element.166), channel_id=1, source_target_pairs={{0,1},{1,0},{2,3},{3,2},{4,5},{5,4},{6,7},{7,6},{8,9},{9,8},{10,11... | collective-permute-start | bytes 6291464 | tf_op jit(solution)/shard_map/ppermute | solution.py:805
  260.9 18.7 %collective-permute-start.13 = (bf16[512,4096]{1,0:T(8,128)(2,1)}, bf16[512,4096]{1,0:T(8,128)(2,1)S(1)}, u32[]{:S(2)}, u32[]{:S(2)}) collective-permute-start(bf16[512,4096]{1,0:T(8,128)(2,1)} %get-tuple-element.187), channel_id=1, source_target_pairs={{0,1},{1,0},{2,3},{3,2},{4,5},{5,4},{6,7},{7,6},{8,9},{9,8},{10,11... | collective-permute-start | bytes 12582920 | tf_op jit(solution)/shard_map/ppermute | solution.py:805
  261.2 18.4 %collective-permute-start.14 = (bf16[512,4096]{1,0:T(8,128)(2,1)}, bf16[512,4096]{1,0:T(8,128)(2,1)}, u32[]{:S(2)}, u32[]{:S(2)}) collective-permute-start(bf16[512,4096]{1,0:T(8,128)(2,1)} %get-tuple-element.189), channel_id=1, source_target_pairs={{0,1},{1,0},{2,3},{3,2},{4,5},{5,4},{6,7},{7,6},{8,9},{9,8},{10,11... | collective-permute-start | bytes 12582920 | tf_op jit(solution)/shard_map/ppermute | solution.py:805
  293.1 51.7 %collective-permute-start.15 = (bf16[256,4096]{1,0:T(8,128)(2,1)}, bf16[256,4096]{1,0:T(8,128)(2,1)S(1)}, u32[]{:S(2)}, u32[]{:S(2)}) collective-permute-start(bf16[256,4096]{1,0:T(8,128)(2,1)} %bitcast.213), channel_id=1, source_target_pairs={{0,2},{2,0},{4,6},{6,4},{8,10},{10,8},{12,14},{14,12},{16,18},{18,... | collective-permute-start | bytes 6291464 | tf_op jit(solution)/shard_map/ppermute | solution.py:805
  294.6 50.2 %collective-permute-start.16 = (bf16[256,4096]{1,0:T(8,128)(2,1)}, bf16[256,4096]{1,0:T(8,128)(2,1)S(1)}, u32[]{:S(2)}, u32[]{:S(2)}) collective-permute-start(bf16[256,4096]{1,0:T(8,128)(2,1)} %bitcast.212), channel_id=1, source_target_pairs={{0,4},{2,6},{4,0},{6,2},{8,12},{10,14},{12,8},{14,10},{16,20},{18,... | collective-permute-start | bytes 6291464 | tf_op jit(solution)/shard_map/ppermute | solution.py:805
  366.6 12.6 %collective-permute-start.17 = (bf16[512,3072]{1,0:T(8,128)(2,1)}, bf16[512,3072]{1,0:T(8,128)(2,1)S(1)}, u32[]{:S(2)}, u32[]{:S(2)}) collective-permute-start(bf16[512,3072]{1,0:T(8,128)(2,1)} %get-tuple-element.204), channel_id=1, source_target_pairs={{0,1},{1,0},{2,3},{3,2},{4,5},{5,4},{6,7},{7,6},{8,9},{9,8},{10,11... | collective-permute-start | bytes 9437192 | tf_op jit(solution)/shard_map/ppermute | solution.py:805
  375.1 4.1 collective-permute-start.18
  375.6 33.2 %collective-permute-start.23 = (bf16[128,4096]{1,0:T(8,128)(2,1)}, bf16[128,4096]{1,0:T(8,128)(2,1)S(1)}, u32[]{:S(2)}, u32[]{:S(2)}) collective-permute-start(bf16[128,4096]{1,0:T(8,128)(2,1)} %bitcast.52), channel_id=1, source_target_pairs={{0,4},{2,6},{4,0},{6,2},{8,12},{10,14},{12,8},{14,10},{16,20},{18,... | collective-permute-start | bytes 3145736 | tf_op jit(solution)/shard_map/ppermute | solution.py:805
  377.0 35.5 %collective-permute-start.24 = (bf16[128,4096]{1,0:T(8,128)(2,1)}, bf16[128,4096]{1,0:T(8,128)(2,1)S(1)}, u32[]{:S(2)}, u32[]{:S(2)}) collective-permute-start(bf16[128,4096]{1,0:T(8,128)(2,1)} %bitcast.55), channel_id=1, source_target_pairs={{0,8},{2,10},{4,12},{6,14},{8,0},{10,2},{12,4},{14,6},{16,24},{18,... | collective-permute-start | bytes 3145736 | tf_op jit(solution)/shard_map/ppermute | solution.py:805
  387.8 33.0 %collective-permute-start.20 = (bf16[256,1536]{1,0:T(8,128)(2,1)}, bf16[256,1536]{1,0:T(8,128)(2,1)S(1)}, u32[]{:S(2)}, u32[]{:S(2)}) collective-permute-start(bf16[256,1536]{1,0:T(8,128)(2,1)} %bitcast.216), channel_id=1, source_target_pairs={{0,2},{2,0},{4,6},{6,4},{8,10},{10,8},{12,14},{14,12},{16,18},{18,... | collective-permute-start | bytes 2359304 | tf_op jit(solution)/shard_map/ppermute | solution.py:805
  389.4 32.7 %collective-permute-start.21 = (bf16[256,1536]{1,0:T(8,128)(2,1)}, bf16[256,1536]{1,0:T(8,128)(2,1)S(1)}, u32[]{:S(2)}, u32[]{:S(2)}) collective-permute-start(bf16[256,1536]{1,0:T(8,128)(2,1)} %bitcast.215), channel_id=1, source_target_pairs={{0,4},{2,6},{4,0},{6,2},{8,12},{10,14},{12,8},{14,10},{16,20},{18,... | collective-permute-start | bytes 2359304 | tf_op jit(solution)/shard_map/ppermute | solution.py:805
  391.5 29.3 %collective-permute-start.22 = (bf16[256,1024]{1,0:T(8,128)(2,1)}, bf16[256,1024]{1,0:T(8,128)(2,1)S(1)}, u32[]{:S(2)}, u32[]{:S(2)}) collective-permute-start(bf16[256,1024]{1,0:T(8,128)(2,1)} %bitcast.219), channel_id=1, source_target_pairs={{0,8},{2,10},{4,12},{6,14},{8,0},{10,2},{12,4},{14,6},{16,24},{18,... | collective-permute-start | bytes 1572872 | tf_op jit(solution)/shard_map/ppermute | solution.py:805
  408.8 20.5 %collective-permute-start.19 = (bf16[1,8,2048]{2,1,0:T(8,128)(2,1)S(1)}, bf16[1,8,2048]{2,1,0:T(8,128)(2,1)S(1)}, u32[]{:S(2)}, u32[]{:S(2)}) collective-permute-start(bf16[1,8,2048]{2,1,0:T(8,128)(2,1)S(1)} %fusion.14.refs_0_), channel_id=1, source_target_pairs={{0,16},{2,18},{4,20},{6,22},{8,24},{10,26},{12,28},{14,30},{16,0},... | collective-permute-start | bytes 98312 | tf_op jit(solution)/shard_map/ppermute | solution.py:805
  431.4 6.9 %collective-permute-start.25 = (bf16[2,8,2048]{2,1,0:T(8,128)(2,1)}, bf16[2,8,2048]{2,1,0:T(8,128)(2,1)S(1)}, u32[]{:S(2)}, u32[]{:S(2)}) collective-permute-start(bf16[2,8,2048]{2,1,0:T(8,128)(2,1)} %get-tuple-element.226.refs_0_), channel_id=1, source_target_pairs={{0,8},{2,10},{4,12},{6,14},{8,0},{10,2},{12,4},{14,6},{16,24},{18,... | collective-permute-start | bytes 196616 | tf_op jit(solution)/shard_map/ppermute | solution.py:805
  440.4 6.1 %collective-permute-start.26 = (bf16[4,8,2048]{2,1,0:T(8,128)(2,1)}, bf16[4,8,2048]{2,1,0:T(8,128)(2,1)S(1)}, u32[]{:S(2)}, u32[]{:S(2)}) collective-permute-start(bf16[4,8,2048]{2,1,0:T(8,128)(2,1)} %get-tuple-element.228.refs_0_), channel_id=1, source_target_pairs={{0,4},{2,6},{4,0},{6,2},{8,12},{10,14},{12,8},{14,10},{16,20},{18,... | collective-permute-start | bytes 393224 | tf_op jit(solution)/shard_map/ppermute | solution.py:805
  440.7 21.3 %collective-permute-start.31 = (bf16[64,4096]{1,0:T(8,128)(2,1)}, bf16[64,4096]{1,0:T(8,128)(2,1)S(1)}, u32[]{:S(2)}, u32[]{:S(2)}) collective-permute-start(bf16[64,4096]{1,0:T(8,128)(2,1)} %bitcast.218), channel_id=1, source_target_pairs={{0,8},{2,10},{4,12},{6,14},{8,0},{10,2},{12,4},{14,6},{16,24},{18,... | collective-permute-start | bytes 1572872 | tf_op jit(solution)/shard_map/ppermute | solution.py:805
  442.7 19.3 %collective-permute-start.32 = (bf16[64,4096]{1,0:T(8,128)(2,1)}, bf16[64,4096]{1,0:T(8,128)(2,1)S(1)}, u32[]{:S(2)}, u32[]{:S(2)}) collective-permute-start(bf16[64,4096]{1,0:T(8,128)(2,1)} %bitcast.217), channel_id=1, source_target_pairs={{0,2},{2,0},{4,6},{6,4},{8,10},{10,8},{12,14},{14,12},{16,18},{18,... | collective-permute-start | bytes 1572872 | tf_op jit(solution)/shard_map/ppermute | solution.py:805
  444.2 16.0 %collective-permute-start.30 = (bf16[128,1024]{1,0:T(8,128)(2,1)}, bf16[128,1024]{1,0:T(8,128)(2,1)S(1)}, u32[]{:S(2)}, u32[]{:S(2)}) collective-permute-start(bf16[128,1024]{1,0:T(8,128)(2,1)} %bitcast.224), channel_id=1, source_target_pairs={{0,2},{2,0},{4,6},{6,4},{8,10},{10,8},{12,14},{14,12},{16,18},{18,... | collective-permute-start | bytes 786440 | tf_op jit(solution)/shard_map/ppermute | solution.py:805
  444.8 17.2 %collective-permute-start.28 = (bf16[128,1536]{1,0:T(8,128)(2,1)}, bf16[128,1536]{1,0:T(8,128)(2,1)S(1)}, u32[]{:S(2)}, u32[]{:S(2)}) collective-permute-start(bf16[128,1536]{1,0:T(8,128)(2,1)} %bitcast.221), channel_id=1, source_target_pairs={{0,4},{2,6},{4,0},{6,2},{8,12},{10,14},{12,8},{14,10},{16,20},{18,... | collective-permute-start | bytes 1179656 | tf_op jit(solution)/shard_map/ppermute | solution.py:805
  446.5 15.4 %collective-permute-start.29 = (bf16[128,1536]{1,0:T(8,128)(2,1)}, bf16[128,1536]{1,0:T(8,128)(2,1)S(1)}, u32[]{:S(2)}, u32[]{:S(2)}) collective-permute-start(bf16[128,1536]{1,0:T(8,128)(2,1)} %bitcast.220), channel_id=1, source_target_pairs={{0,8},{2,10},{4,12},{6,14},{8,0},{10,2},{12,4},{14,6},{16,24},{18,... | collective-permute-start | bytes 1179656 | tf_op jit(solution)/shard_map/ppermute | solution.py:805
  460.2 7.3 %collective-permute-start.27 = (bf16[8,8,2048]{2,1,0:T(8,128)(2,1)}, bf16[8,8,2048]{2,1,0:T(8,128)(2,1)S(1)}, u32[]{:S(2)}, u32[]{:S(2)}) collective-permute-start(bf16[8,8,2048]{2,1,0:T(8,128)(2,1)} %get-tuple-element.230.refs_0_), channel_id=1, source_target_pairs={{0,2},{2,0},{4,6},{6,4},{8,10},{10,8},{12,14},{14,12},{16,18},{18,... | collective-permute-start | bytes 786440 | tf_op jit(solution)/shard_map/ppermute | solution.py:805
  470.1 7.9 %collective-permute-start.33 = (bf16[16,8,2048]{2,1,0:T(8,128)(2,1)}, bf16[16,8,2048]{2,1,0:T(8,128)(2,1)S(1)}, u32[]{:S(2)}, u32[]{:S(2)}) collective-permute-start(bf16[16,8,2048]{2,1,0:T(8,128)(2,1)} %get-tuple-element.243), channel_id=1, source_target_pairs={{0,1},{1,0},{2,3},{3,2},{4,5},{5,4},{6,7},{7,6},{8,9},{9,8},{10,11... | collective-permute-start | bytes 1572872 | tf_op jit(solution)/shard_map/ppermute | solution.py:805
  470.1 17.5 %collective-permute-start.34 = (bf16[64,1536]{1,0:T(8,128)(2,1)}, bf16[64,1536]{1,0:T(8,128)(2,1)S(1)}, u32[]{:S(2)}, u32[]{:S(2)}) collective-permute-start(bf16[64,1536]{1,0:T(8,128)(2,1)} %bitcast.226), channel_id=1, source_target_pairs={{0,8},{2,10},{4,12},{6,14},{8,0},{10,2},{12,4},{14,6},{16,24},{18,... | collective-permute-start | bytes 589832 | tf_op jit(solution)/shard_map/ppermute | solution.py:805
  471.7 15.8 %collective-permute-start.35 = (bf16[64,1536]{1,0:T(8,128)(2,1)}, bf16[64,1536]{1,0:T(8,128)(2,1)S(1)}, u32[]{:S(2)}, u32[]{:S(2)}) collective-permute-start(bf16[64,1536]{1,0:T(8,128)(2,1)} %bitcast.225), channel_id=1, source_target_pairs={{0,2},{2,0},{4,6},{6,4},{8,10},{10,8},{12,14},{14,12},{16,18},{18,... | collective-permute-start | bytes 589832 | tf_op jit(solution)/shard_map/ppermute | solution.py:805
  472.9 14.6 %collective-permute-start.36 = (bf16[64,1024]{1,0:T(8,128)(2,1)}, bf16[64,1024]{1,0:T(8,128)(2,1)S(1)}, u32[]{:S(2)}, u32[]{:S(2)}) collective-permute-start(bf16[64,1024]{1,0:T(8,128)(2,1)} %bitcast.227), channel_id=1, source_target_pairs={{0,4},{2,6},{4,0},{6,2},{8,12},{10,14},{12,8},{14,10},{16,20},{18,... | collective-permute-start | bytes 393224 | tf_op jit(solution)/shard_map/ppermute | solution.py:805
  473.7 28.5 %collective-permute-start.40 = (bf16[32,4096]{1,0:T(8,128)(2,1)}, bf16[32,4096]{1,0:T(8,128)(2,1)S(1)}, u32[]{:S(2)}, u32[]{:S(2)}) collective-permute-start(bf16[32,4096]{1,0:T(8,128)(2,1)} %bitcast.223), channel_id=1, source_target_pairs={{0,16},{2,18},{4,20},{6,22},{8,24},{10,26},{12,28},{14,30},{16,0},... | collective-permute-start | bytes 786440 | tf_op jit(solution)/shard_map/ppermute | solution.py:805
  478.0 31.6 %collective-permute-start.41 = (bf16[32,4096]{1,0:T(8,128)(2,1)}, bf16[32,4096]{1,0:T(8,128)(2,1)S(1)}, u32[]{:S(2)}, u32[]{:S(2)}) collective-permute-start(bf16[32,4096]{1,0:T(8,128)(2,1)} %bitcast.222), channel_id=1, source_target_pairs={{0,16},{2,18},{4,20},{6,22},{8,24},{10,26},{12,28},{14,30},{16,0},... | collective-permute-start | bytes 786440 | tf_op jit(solution)/shard_map/ppermute | solution.py:805
  491.1 24.0 %collective-permute-start.37 = (bf16[32,1536]{1,0:T(8,128)(2,1)}, bf16[32,1536]{1,0:T(8,128)(2,1)S(1)}, u32[]{:S(2)}, u32[]{:S(2)}) collective-permute-start(bf16[32,1536]{1,0:T(8,128)(2,1)} %bitcast.230), channel_id=1, source_target_pairs={{0,16},{2,18},{4,20},{6,22},{8,24},{10,26},{12,28},{14,30},{16,0},... | collective-permute-start | bytes 294920 | tf_op jit(solution)/shard_map/ppermute | solution.py:805
  493.9 21.1 %collective-permute-start.38 = (bf16[32,1536]{1,0:T(8,128)(2,1)}, bf16[32,1536]{1,0:T(8,128)(2,1)S(1)}, u32[]{:S(2)}, u32[]{:S(2)}) collective-permute-start(bf16[32,1536]{1,0:T(8,128)(2,1)} %bitcast.229), channel_id=1, source_target_pairs={{0,16},{2,18},{4,20},{6,22},{8,24},{10,26},{12,28},{14,30},{16,0},... | collective-permute-start | bytes 294920 | tf_op jit(solution)/shard_map/ppermute | solution.py:805
  494.1 21.0 %collective-permute-start.39 = (bf16[32,1024]{1,0:T(8,128)(2,1)}, bf16[32,1024]{1,0:T(8,128)(2,1)S(1)}, u32[]{:S(2)}, u32[]{:S(2)}) collective-permute-start(bf16[32,1024]{1,0:T(8,128)(2,1)} %bitcast.231), channel_id=1, source_target_pairs={{0,16},{2,18},{4,20},{6,22},{8,24},{10,26},{12,28},{14,30},{16,0},... | collective-permute-start | bytes 196616 | tf_op jit(solution)/shard_map/ppermute | solution.py:805
  498.2 21.2 %all-to-all-start.2 = ((f32[32,1,1280]{2,1,0:T(1,128)}), f32[32,1,1280]{2,1,0:T(1,128)S(1)}, u32[]{:S(2)}, u32[]{:S(2)}) async-start(f32[32,1,1280]{2,1,0:T(1,128)} %reshape.669), calls=%async_computation.2 | async-start | bytes 327680 | tf_op jit(solution)/shard_map/all_to_all | solution.py:1204
  (54 other events, 255.7 us)
Sparse Core Ops, SparseCore 0:
  74.7 122.1 all-gather.2
  368.4 63.8 all-gather.4

commit v5 on v4

--- a/solution.py
+++ b/solution.py
@@ -9,7 +9,7 @@
 
 NORM_EPS = 1e-06
 BF, F32 = jnp.bfloat16, jnp.float32
-VMEM_BYTES = 56 * 2**20
+VMEM_BYTES = 60 * 2**20
 HEAD = 64
 PAIR = 2 * HEAD
 GROUP = 4

time: 539 us -> 537 us (level)
  waiting for transfers between devices: 83.4 us -> 97.7 us
  Pallas kernels: 313 us -> 303 us
    ppermute x42, waiting for transfers between devices: 79.3 us -> 89.8 us  [flip(): return lax.ppermute(values, axis, [(i, i ^ 1 << bit) for i in range(size)])]
    pallas_call x28, Pallas kernels: 313 us -> 303 us  [run(): mark, *result = call(*args, *waits)]
    unnamed x117 -> x109, local copies, waits for them, and re-layouts: 18.9 us -> 15.6 us
  transfers between devices with their start and end apart: 47 -> 47, of which waited for: 18 -> 20; matrix products, arithmetic and copies ran while one was open for 4% -> 4% of each run, Pallas kernels for 40% -> 38%
where the time goes in v5:
time: 537 us; the launch traced here: 529 us
  Pallas kernels  303 us (56%)
  waiting for transfers between devices  97.7 us (18%)
  starting transfers between devices  72.4 us (13%)
  local copies, waits for them, and re-layouts  30.2 us (6%)
  between operations  15.2 us (3%)
  other arithmetic  11.3 us (2%)
    pallas_call x28, Pallas kernels, run(): mark, *result = call(*args, *waits)  303 us
    ppermute x42, waiting for transfers between devices, flip(): return lax.ppermute(values, axis, [(i, i ^ 1 << bit) for i in range(size)])  89.8 us
    ppermute x42, starting transfers between devices, flip(): return lax.ppermute(values, axis, [(i, i ^ 1 << bit) for i in range(size)])  56.8 us
    unnamed x109, local copies, waits for them, and re-layouts  15.6 us
  transfers between devices with their start and end apart: 47, of which 20 were waited for; matrix products, arithmetic and copies ran while one was open for 4% of the time, Pallas kernels for 38%

profile of v5, /device:TPU:0, one launch (start us, length us, event | category | flops | bytes accessed | tf_op | source)
XLA Modules:
  0.0 529.4 jit_solution(1314215846901562080)
XLA Ops:
  9.1 4.1 collective-permute-start
  15.9 3.8 all-to-all-start
  22.0 12.8 %collective-permute-done.refs_1_ = bf16[1,32,5248]{2,1,0:T(8,128)(2,1)S(1)} collective-permute-done((bf16[1,32,5248]{2,1,0:T(8,128)(2,1)S(1)}, bf16[1,32,5248]{2,1,0:T(8,128)(2,1)S(1)}, u32[]{:S(2)}, u32[]{:S(2)}) %collective-permute-start) | collective-permute-done | bytes 335904 | tf_op jit(solution)/shard_map/ppermute | solution.py:805
  46.6 2.2 collective-permute-start.2
  49.2 4.5 collective-permute-done.2.refs_3_
  54.4 2.6 land.11
  57.0 2.6 collective-permute-start.5
  61.2 7.8 %collective-permute-done.6.refs_4_ = bf16[4,32,2048]{2,1,0:T(8,128)(2,1)S(1)} collective-permute-done((bf16[4,32,2048]{2,1,0:T(8,128)(2,1)}, bf16[4,32,2048]{2,1,0:T(8,128)(2,1)S(1)}, u32[]{:S(2)}, u32[]{:S(2)}) %collective-permute-start.6) | collective-permute-done | bytes 524320 | tf_op jit(solution)/shard_map/ppermute | solution.py:805
  70.8 3.7 land.12
  78.2 5.2 modulation.1
  83.4 6.8 %all-to-all-start.1 = ((f32[32,8,192]{2,1,0:T(8,128)}), f32[32,8,192]{2,1,0:T(8,128)S(1)}, u32[]{:S(2)}, u32[]{:S(2)}) async-start(f32[32,8,192]{2,1,0:T(8,128)} %bitcast.189), calls=%async_computation.1 | async-start | bytes 524288 | tf_op jit(solution)/shard_map/all_to_all | solution.py:1076
  94.0 14.1 %collective-permute-done.10.refs_3_ = bf16[8,32,2048]{2,1,0:T(8,128)(2,1)S(1)} collective-permute-done((bf16[8,32,2048]{2,1,0:T(8,128)(2,1)}, bf16[8,32,2048]{2,1,0:T(8,128)(2,1)S(1)}, u32[]{:S(2)}, u32[]{:S(2)}) %collective-permute-start.10) | collective-permute-done | bytes 1048608 | tf_op jit(solution)/shard_map/ppermute | solution.py:805
  110.4 4.8 land.13
  117.3 5.2 collective-permute-done.11
  123.9 26.4 %qkv_forward.1 = (f32[8,128]{1,0:T(8,128)}, bf16[1024,1024]{1,0:T(8,128)(2,1)}, bf16[1024,1024]{1,0:T(8,128)(2,1)}, bf16[1024,1024]{1,0:T(8,128)(2,1)}, bf16[102...) custom-call(s32[2,32]{1,0:T(2,128)} %pad_add_fusion.1.refs_0_, ...), custom_call_target="tpu_custom_call" | custom-call | flops 6442450944 | bytes 27262976 | tf_op jit(solution)/shard_map/qkv_forward/pallas_call | solution.py:79
  150.3 28.7 %attention_forward.1 = (f32[8,128]{1,0:T(8,128)}, bf16[1024,1024]{1,0:T(8,128)(2,1)}, bf16[1024,1024]{1,0:T(8,128)(2,1)}, f32[4,8,1024]{2,1,0:T(8,128)}) custom-call(s32[2,4]{1,0:T(2,128)} %pad_add_fusion.refs_0_, bf16[1024,1024]{1,0:T(8,128)(2,1)} %get-tuple-element.167.refs_1_, bf16[1024,1024]{1,0:T(8,128)(2,1)} %get-tuple-element.168.refs_2_, ...), custom_call_target="tpu_custom_call" | custom-call | flops 17179869184 | bytes 8388608 | tf_op jit(solution)/shard_map/attention_forward/pallas_call | solution.py:79
  179.0 10.0 %projection.1 = (f32[8,128]{1,0:T(8,128)}, f32[1024,1024]{1,0:T(8,128)}, bf16[1024,1024]{1,0:T(8,128)(2,1)}, bf16[1024,1024]{1,0:T(8,128)(2,1)}, bf16[1024,1024]{1,0:T(8,128)(2,1)}) custom-call(bf16[1024,1024]{1,0:T(8,128)(2,1)} %refs_4_.1, bf16[1024,1024]{1,0:T(8,128)(2,1)} %get-tuple-element.170.refs_1_.refs_5_, bf16[1024,1024]{1,0:T(8,128)(2,1)} %refs_3_.1, ...), custom_call_target="tpu_custom_call" | custom-call | flops 2147483648 | bytes 16777216 | tf_op jit(solution)/shard_map/projection/pallas_call | solution.py:79
  189.0 7.9 %all-gather.3.cloned.1.call-done.refs_3_.refs_4_ = bf16[1024,8192]{1,0:T(8,128)(2,1)} async-done(((bf16[32,8192]{1,0:T(8,128)(2,1)}), bf16[1024,8192]{1,0:T(8,128)(2,1)}) %all-gather.3.cloned.1.call-update) | async-done | bytes 16777232 | tf_op jit(solution)/shard_map/all_gather | solution.py:1074
  196.9 63.9 %feed_forward.1 = (f32[8,128]{1,0:T(8,128)}, f32[1024,1024]{1,0:T(8,128)}, f32[1024,1024]{1,0:T(8,128)}, bf16[512,4096]{1,0:T(8,128)(2,1)}, bf16[512,4096]{1,0:T...) custom-call(s32[6]{0:T(128)} %stack.32.refs_0_, bf16[1024,1024]{1,0:T(8,128)(2,1)} %get-tuple-element.172.refs_1_, ...), custom_call_target="tpu_custom_call" | custom-call | flops 51539607552 | bytes 20971520 | tf_op jit(solution)/shard_map/feed_forward/pallas_call | solution.py:79
  262.0 17.5 %middle.1 = (f32[8,128]{1,0:T(8,128)}, bf16[1024,1024]{1,0:T(8,128)(2,1)}, f32[1024,1024]{1,0:T(8,128)}, bf16[1024,1024]{1,0:T(8,128)(2,1)}, bf16[1024,1024]{1,0...) custom-call(f32[1024,1024]{1,0:T(8,128)} %get-tuple-element.175.refs_0_, ...), custom_call_target="tpu_custom_call" | custom-call | flops 4294967296 | bytes 31457280 | tf_op jit(solution)/shard_map/middle/pallas_call | solution.py:79
  279.5 11.5 %halving_sum.6 = (f32[8,128]{1,0:T(8,128)}, bf16[8,32,4096]{2,1,0:T(8,128)(2,1)}, bf16[8,32,4096]{2,1,0:T(8,128)(2,1)}, bf16[4,64,4096]{2,1,0:T(8,128)(2,1)}, bf16[4,64,4096]{2,1,0:T(8,128)(2,1)}) custom-call(s32[6]{0:T(128)} %stack.32.refs_0_, bf16[8,2,32,4096]{3,2,1,0:T(8,128)(2,1)} %bitcast.119, bf16[8,2,32,4096]{3,2,1,0:T(8,128)(2,1)} %bitcast.26.refs_2_.refs_4_, ...), custom_call_target="tpu_custom_call" | custom-call | flops 4194304 | bytes 25165824 | tf_op jit(solution)/shard_map/halving_sum/pallas_call | solution.py:79
  293.2 43.2 %attention_backward.1 = (f32[8,128]{1,0:T(8,128)}, bf16[1024,1024]{1,0:T(8,128)(2,1)}, bf16[1024,1024]{1,0:T(8,128)(2,1)}, bf16[1024,1024]{1,0:T(8,128)(2,1)}, f32[8,1024]{1,0:T(8,128)}) custom-call(s32[2,4]{1,0:T(2,128)} %pad_add_fusion.refs_0_, bf16[1024,1024]{1,0:T(8,128)(2,1)} %get-tuple-element.167.refs_1_, ...), custom_call_target="tpu_custom_call" | custom-call | flops 42949672960 | bytes 18874368 | tf_op jit(solution)/shard_map/attention_backward/pallas_call | solution.py:79
  336.4 2.7 collective-permute-done.15
  340.4 6.5 %halving_sum.7 = (f32[8,128]{1,0:T(8,128)}, bf16[4,32,4096]{2,1,0:T(8,128)(2,1)}, bf16[4,32,4096]{2,1,0:T(8,128)(2,1)}, bf16[2,64,4096]{2,1,0:T(8,128)(2,1)}, bf16[2,64,4096]{2,1,0:T(8,128)(2,1)}) custom-call(s32[6]{0:T(128)} %stack.32.refs_0_, bf16[4,2,32,4096]{3,2,1,0:T(8,128)(2,1)} %bitcast.123, bf16[4,2,32,4096]{3,2,1,0:T(8,128)(2,1)} %bitcast.127, ...), custom_call_target="tpu_custom_call" | custom-call | flops 2097152 | bytes 12582912 | tf_op jit(solution)/shard_map/halving_sum/pallas_call | solution.py:79
  346.9 13.3 %weight_grad.2 = (f32[8,128]{1,0:T(8,128)}, bf16[512,3072]{1,0:T(8,128)(2,1)}, bf16[512,3072]{1,0:T(8,128)(2,1)}) custom-call(s32[6]{0:T(128)} %stack.32.refs_0_, bf16[1024,1024]{1,0:T(8,128)(2,1)} %get-tuple-element.196.refs_1_, bf16[1024,1024]{1,0:T(8,128)(2,1)} %get-tuple-element.192.refs_2_.refs_0_, ...), custom_call_target="tpu_custom_call" | custom-call | flops 6442450944 | bytes 12582912 | tf_op jit(solution)/shard_map/weight_grad/pallas_call | solution.py:79
  360.2 3.3 collective-permute-start.17
  365.1 6.8 %weight_grad.3 = (f32[8,128]{1,0:T(8,128)}, bf16[512,1024]{1,0:T(8,128)(2,1)}, bf16[512,1024]{1,0:T(8,128)(2,1)}) custom-call(s32[6]{0:T(128)} %stack.32.refs_0_, bf16[1024,1024]{1,0:T(8,128)(2,1)} %get-tuple-element.170.refs_1_.refs_5_, bf16[1024,1024]{1,0:T(8,128)(2,1)} %get-tuple-element.205.refs_2_, f32[8,128]{1,0:T(8,128)} %get-tuple-element.206.refs_3_), custom_call_target="tpu_custom_call" | custom-call | flops 2147483648 | bytes 4194304 | tf_op jit(solution)/shard_map/weight_grad/pallas_call | solution.py:79
  371.9 4.5 collective-permute-start.23
  379.0 6.7 %halving_sum.8 = (f32[8,128]{1,0:T(8,128)}, bf16[8,32,1536]{2,1,0:T(8,128)(2,1)}, bf16[8,32,1536]{2,1,0:T(8,128)(2,1)}, bf16[4,64,1536]{2,1,0:T(8,128)(2,1)}, bf...) custom-call(s32[6]{0:T(128)} %stack.32.refs_0_, ...), custom_call_target="tpu_custom_call" | custom-call | flops 2097152 | bytes 12582912 | tf_op jit(solution)/shard_map/halving_sum/pallas_call | solution.py:79
  385.7 6.8 %collective-permute-start.20 = (bf16[256,1536]{1,0:T(8,128)(2,1)}, bf16[256,1536]{1,0:T(8,128)(2,1)S(1)}, u32[]{:S(2)}, u32[]{:S(2)}) collective-permute-start(bf16[256,1536]{1,0:T(8,128)(2,1)} %bitcast.210), channel_id=1, source_target_pairs={{0,2},{2,0},{4,6},{6,4},{8,10},{10,8},{12,14},{14,12},{16,18},{18,... | collective-permute-start | bytes 2359304 | tf_op jit(solution)/shard_map/ppermute | solution.py:805
  394.0 16.0 %first_norm_backward.1 = (f32[8,128]{1,0:T(8,128)}, bf16[1024,1024]{1,0:T(8,128)(2,1)}, f32[16,2048]{1,0:T(8,128)}) custom-call(bf16[1024,1024]{1,0:T(8,128)(2,1)} %get-tuple-element.192.refs_2_.refs_0_, bf16[1024,1024]{1,0:T(8,128)(2,1)} %get-tuple-element.193.refs_3_.refs_1_, bf16[1024,1024]{1,0:T(8,128)(2,1)} %get-tuple-element.194.refs_4_.refs_2_, ...), custom_call_target="tpu_custom_call" | custom-call | flops 6442450944 | bytes 18874368 | tf_op jit(solution)/shard_map/first_norm_backward/pallas_call | solution.py:79
  411.1 9.5 %collective-permute-done.22 = bf16[256,1024]{1,0:T(8,128)(2,1)S(1)} collective-permute-done((bf16[256,1024]{1,0:T(8,128)(2,1)}, bf16[256,1024]{1,0:T(8,128)(2,1)S(1)}, u32[]{:S(2)}, u32[]{:S(2)}) %collective-permute-start.22) | collective-permute-done | bytes 524320 | tf_op jit(solution)/shard_map/ppermute | solution.py:805
  423.3 6.4 %halving_sum.9 = (f32[8,128]{1,0:T(8,128)}, bf16[4,32,1536]{2,1,0:T(8,128)(2,1)}, bf16[4,32,1536]{2,1,0:T(8,128)(2,1)}, bf16[2,64,1536]{2,1,0:T(8,128)(2,1)}, bf...) custom-call(s32[6]{0:T(128)} %stack.32.refs_0_, ...), custom_call_target="tpu_custom_call" | custom-call | flops 2097152 | bytes 12582912 | tf_op jit(solution)/shard_map/halving_sum/pallas_call | solution.py:79
  431.8 4.5 collective-permute-done.25.refs_1_
  440.3 4.6 collective-permute-start.32
  445.5 2.0 collective-permute-start.29
  449.2 11.3 %collective-permute-done.30 = bf16[128,1024]{1,0:T(8,128)(2,1)S(1)} collective-permute-done((bf16[128,1024]{1,0:T(8,128)(2,1)}, bf16[128,1024]{1,0:T(8,128)(2,1)S(1)}, u32[]{:S(2)}, u32[]{:S(2)}) %collective-permute-start.30) | collective-permute-done | bytes 262176 | tf_op jit(solution)/shard_map/ppermute | solution.py:805
  460.6 2.0 collective-permute-start.27
  463.8 4.3 halving_sum.10
  470.7 2.0 collective-permute-start.34
  474.4 2.9 collective-permute-start.41
  478.9 7.8 %adaptive_norm_backward.1 = (f32[8,128]{1,0:T(8,128)}, f32[32,6144]{1,0:T(8,128)}, f32[32,40,32]{2,1,0:T(8,128)}) custom-call(s32[6]{0:T(128)} %stack.32.refs_0_, bf16[256,4096]{1,0:T(8,128)(2,1)} %all-gather.5.cloned.1.call-done.refs_1_, bf16[128,2048]{1,0:T(8,128)(2,1)} %bitcast.183, bf16[128,2048]{1,0:T(8,128)(2,1)} %bitcast.184, ...), custom_call_target="tpu_custom_call" | custom-call | flops 1000000000 | bytes 10000000 | tf_op jit(solution)/shard_map/adaptive_norm_backward/pallas_call | solution.py:79
  487.5 2.8 halving_sum.11
  490.4 2.8 collective-permute-start.38
  494.7 4.5 all-to-all-start.2
  501.2 7.4 %collective-permute-done.41.refs_3_ = bf16[32,4096]{1,0:T(8,128)(2,1)S(1)} collective-permute-done((bf16[32,4096]{1,0:T(8,128)(2,1)}, bf16[32,4096]{1,0:T(8,128)(2,1)S(1)}, u32[]{:S(2)}, u32[]{:S(2)}) %collective-permute-start.41) | collective-permute-done | bytes 262176 | tf_op jit(solution)/shard_map/ppermute | solution.py:805
  509.3 2.7 last_sum.2
  512.0 2.1 collective-permute-done.39.refs_5_
  (242 shorter events, 78.7 us)
Async XLA Ops:
  9.1 25.7 %collective-permute-start = (bf16[1,32,5248]{2,1,0:T(8,128)(2,1)S(1)}, bf16[1,32,5248]{2,1,0:T(8,128)(2,1)S(1)}, u32[]{:S(2)}, u32[]{:S(2)}) collective-permute-start(bf16[1,32,5248]{2,1,0:T(8,128)(2,1)S(1)} %maximum_bitcast_fusion.refs_0_), channel_id=1, source_target_pairs={{0,16},{2,18},{4,20},{6,22},{8,24},{10,26},{12,28},{14,30},{16,0},... | collective-permute-start | bytes 1007624 | tf_op jit(solution)/shard_map/ppermute | solution.py:805
  15.9 33.3 %all-to-all-start = ((bf16[32,32,192]{2,0,1:T(8,128)(2,1)}), bf16[32,32,192]{2,0,1:T(8,128)(2,1)S(1)}, u32[]{:S(2)}, u32[]{:S(2)}) async-start(bf16[32,32,192]{2,0,1:T(8,128)(2,1)} %copy.82), calls=%async_computation | async-start | bytes 1048576 | tf_op jit(solution)/shard_map/all_to_all | solution.py:1030
  19.7 177.1 %all-gather.3.cloned.1.call-start = ((), (), s32[]{:S(2)}) async-start(), calls=%async_computation.3 | async-start | bytes 17301504 | tf_op jit(solution)/shard_map/all_gather | solution.py:1074
  20.8 28.0 %copy-start.32 = (bf16[128,1024]{1,0:T(8,128)(2,1)S(1)}, bf16[128,1024]{1,0:T(8,128)(2,1)}, u32[]{:S(2)}) copy-start(bf16[128,1024]{1,0:T(8,128)(2,1)} %param.23) | copy-start | bytes 786436
  38.4 5.8 %collective-permute-start.1 = (bf16[2,32,1152]{2,1,0:T(8,128)(2,1)S(1)}, bf16[2,32,1152]{2,1,0:T(8,128)(2,1)S(1)}, u32[]{:S(2)}, u32[]{:S(2)}) collective-permute-start(bf16[2,32,1152]{2,1,0:T(8,128)(2,1)S(1)} %slice.95.refs_0_), channel_id=1, source_target_pairs={{0,8},{2,10},{4,12},{6,14},{8,0},{10,2},{12,4},{14,6},{16,24},{18,... | collective-permute-start | bytes 442376 | tf_op jit(solution)/shard_map/ppermute | solution.py:805
  39.6 9.3 %collective-permute-start.3 = (bf16[2,32,2048]{2,1,0:T(8,128)(2,1)S(1)}, bf16[2,32,2048]{2,1,0:T(8,128)(2,1)S(1)}, u32[]{:S(2)}, u32[]{:S(2)}) collective-permute-start(bf16[2,32,2048]{2,1,0:T(8,128)(2,1)S(1)} %get-tuple-element.278.refs_1_), channel_id=1, source_target_pairs={{0,2},{2,0},{4,6},{6,4},{8,10},{10,8},{12,14},{14,12},{16,18},{18,... | collective-permute-start | bytes 786440 | tf_op jit(solution)/shard_map/ppermute | solution.py:805
  41.5 7.8 %collective-permute-start.4 = (bf16[2,32,2048]{2,1,0:T(8,128)(2,1)S(1)}, bf16[2,32,2048]{2,1,0:T(8,128)(2,1)S(1)}, u32[]{:S(2)}, u32[]{:S(2)}) collective-permute-start(bf16[2,32,2048]{2,1,0:T(8,128)(2,1)S(1)} %get-tuple-element.277.refs_2_), channel_id=1, source_target_pairs={{0,8},{2,10},{4,12},{6,14},{8,0},{10,2},{12,4},{14,6},{16,24},{18,... | collective-permute-start | bytes 786440 | tf_op jit(solution)/shard_map/ppermute | solution.py:805
  46.6 7.2 %collective-permute-start.2 = (bf16[4,32,1152]{2,1,0:T(8,128)(2,1)}, bf16[4,32,1152]{2,1,0:T(8,128)(2,1)S(1)}, u32[]{:S(2)}, u32[]{:S(2)}) collective-permute-start(bf16[4,32,1152]{2,1,0:T(8,128)(2,1)} %get-tuple-element.155.refs_0_), channel_id=1, source_target_pairs={{0,4},{2,6},{4,0},{6,2},{8,12},{10,14},{12,8},{14,10},{16,20},{18,... | collective-permute-start | bytes 884744 | tf_op jit(solution)/shard_map/ppermute | solution.py:805
  57.0 12.1 %collective-permute-start.5 = (bf16[8,32,1152]{2,1,0:T(8,128)(2,1)}, bf16[8,32,1152]{2,1,0:T(8,128)(2,1)S(1)}, u32[]{:S(2)}, u32[]{:S(2)}) collective-permute-start(bf16[8,32,1152]{2,1,0:T(8,128)(2,1)} %get-tuple-element.156.refs_0_), channel_id=1, source_target_pairs={{0,2},{2,0},{4,6},{6,4},{8,10},{10,8},{12,14},{14,12},{16,18},{18,... | collective-permute-start | bytes 1769480 | tf_op jit(solution)/shard_map/ppermute | solution.py:805
  59.6 9.4 %collective-permute-start.6 = (bf16[4,32,2048]{2,1,0:T(8,128)(2,1)}, bf16[4,32,2048]{2,1,0:T(8,128)(2,1)S(1)}, u32[]{:S(2)}, u32[]{:S(2)}) collective-permute-start(bf16[4,32,2048]{2,1,0:T(8,128)(2,1)} %get-tuple-element.157.refs_1_), channel_id=1, source_target_pairs={{0,8},{2,10},{4,12},{6,14},{8,0},{10,2},{12,4},{14,6},{16,24},{18,... | collective-permute-start | bytes 1572872 | tf_op jit(solution)/shard_map/ppermute | solution.py:805
  59.6 9.5 %collective-permute-start.7 = (bf16[4,32,2048]{2,1,0:T(8,128)(2,1)}, bf16[4,32,2048]{2,1,0:T(8,128)(2,1)S(1)}, u32[]{:S(2)}, u32[]{:S(2)}) collective-permute-start(bf16[4,32,2048]{2,1,0:T(8,128)(2,1)} %get-tuple-element.158.refs_2_), channel_id=1, source_target_pairs={{0,4},{2,6},{4,0},{6,2},{8,12},{10,14},{12,8},{14,10},{16,20},{18,... | collective-permute-start | bytes 1572872 | tf_op jit(solution)/shard_map/ppermute | solution.py:805
  74.9 3.2 collective-permute-start.8
  76.1 32.0 %collective-permute-start.10 = (bf16[8,32,2048]{2,1,0:T(8,128)(2,1)}, bf16[8,32,2048]{2,1,0:T(8,128)(2,1)S(1)}, u32[]{:S(2)}, u32[]{:S(2)}) collective-permute-start(bf16[8,32,2048]{2,1,0:T(8,128)(2,1)} %get-tuple-element.163.refs_1_), channel_id=1, source_target_pairs={{0,2},{2,0},{4,6},{6,4},{8,10},{10,8},{12,14},{14,12},{16,18},{18,... | collective-permute-start | bytes 3145736 | tf_op jit(solution)/shard_map/ppermute | solution.py:805
  77.6 31.9 %collective-permute-start.9 = (bf16[8,32,2048]{2,1,0:T(8,128)(2,1)}, bf16[8,32,2048]{2,1,0:T(8,128)(2,1)S(1)}, u32[]{:S(2)}, u32[]{:S(2)}) collective-permute-start(bf16[8,32,2048]{2,1,0:T(8,128)(2,1)} %get-tuple-element.162.refs_0_), channel_id=1, source_target_pairs={{0,4},{2,6},{4,0},{6,2},{8,12},{10,14},{12,8},{14,10},{16,20},{18,... | collective-permute-start | bytes 3145736 | tf_op jit(solution)/shard_map/ppermute | solution.py:805
  83.4 32.9 %all-to-all-start.1 = ((f32[32,8,192]{2,1,0:T(8,128)}), f32[32,8,192]{2,1,0:T(8,128)S(1)}, u32[]{:S(2)}, u32[]{:S(2)}) async-start(f32[32,8,192]{2,1,0:T(8,128)} %bitcast.189), calls=%async_computation.1 | async-start | bytes 524288 | tf_op jit(solution)/shard_map/all_to_all | solution.py:1076
  90.2 388.7 %all-gather.5.cloned.1.call-start = ((), (), s32[]{:S(2)}) async-start(), calls=%async_computation.4 | async-start | bytes 2162688 | tf_op jit(solution)/shard_map/all_gather | solution.py:1112
  115.2 7.3 %collective-permute-start.11 = (bf16[16,32,2048]{2,1,0:T(8,128)(2,1)}, bf16[16,32,2048]{2,1,0:T(8,128)(2,1)S(1)}, u32[]{:S(2)}, u32[]{:S(2)}) collective-permute-start(bf16[16,32,2048]{2,1,0:T(8,128)(2,1)} %get-tuple-element.165), channel_id=1, source_target_pairs={{0,1},{1,0},{2,3},{3,2},{4,5},{5,4},{6,7},{7,6},{8,9},{9,8},{10,11... | collective-permute-start | bytes 6291464 | tf_op jit(solution)/shard_map/ppermute | solution.py:805
  115.2 7.5 %collective-permute-start.12 = (bf16[16,32,2048]{2,1,0:T(8,128)(2,1)}, bf16[16,32,2048]{2,1,0:T(8,128)(2,1)}, u32[]{:S(2)}, u32[]{:S(2)}) collective-permute-start(bf16[16,32,2048]{2,1,0:T(8,128)(2,1)} %get-tuple-element.166), channel_id=1, source_target_pairs={{0,1},{1,0},{2,3},{3,2},{4,5},{5,4},{6,7},{7,6},{8,9},{9,8},{10,11... | collective-permute-start | bytes 6291464 | tf_op jit(solution)/shard_map/ppermute | solution.py:805
  260.8 18.7 %collective-permute-start.13 = (bf16[512,4096]{1,0:T(8,128)(2,1)}, bf16[512,4096]{1,0:T(8,128)(2,1)}, u32[]{:S(2)}, u32[]{:S(2)}) collective-permute-start(bf16[512,4096]{1,0:T(8,128)(2,1)} %get-tuple-element.187), channel_id=1, source_target_pairs={{0,1},{1,0},{2,3},{3,2},{4,5},{5,4},{6,7},{7,6},{8,9},{9,8},{10,11... | collective-permute-start | bytes 12582920 | tf_op jit(solution)/shard_map/ppermute | solution.py:805
  261.1 18.4 %collective-permute-start.14 = (bf16[512,4096]{1,0:T(8,128)(2,1)}, bf16[512,4096]{1,0:T(8,128)(2,1)}, u32[]{:S(2)}, u32[]{:S(2)}) collective-permute-start(bf16[512,4096]{1,0:T(8,128)(2,1)} %get-tuple-element.189), channel_id=1, source_target_pairs={{0,1},{1,0},{2,3},{3,2},{4,5},{5,4},{6,7},{7,6},{8,9},{9,8},{10,11... | collective-permute-start | bytes 12582920 | tf_op jit(solution)/shard_map/ppermute | solution.py:805
  291.0 48.1 %collective-permute-start.15 = (bf16[256,4096]{1,0:T(8,128)(2,1)}, bf16[256,4096]{1,0:T(8,128)(2,1)S(1)}, u32[]{:S(2)}, u32[]{:S(2)}) collective-permute-start(bf16[256,4096]{1,0:T(8,128)(2,1)} %bitcast.205), channel_id=1, source_target_pairs={{0,2},{2,0},{4,6},{6,4},{8,10},{10,8},{12,14},{14,12},{16,18},{18,... | collective-permute-start | bytes 6291464 | tf_op jit(solution)/shard_map/ppermute | solution.py:805
  292.6 47.8 %collective-permute-start.16 = (bf16[256,4096]{1,0:T(8,128)(2,1)}, bf16[256,4096]{1,0:T(8,128)(2,1)}, u32[]{:S(2)}, u32[]{:S(2)}) collective-permute-start(bf16[256,4096]{1,0:T(8,128)(2,1)} %bitcast.204), channel_id=1, source_target_pairs={{0,4},{2,6},{4,0},{6,2},{8,12},{10,14},{12,8},{14,10},{16,20},{18,... | collective-permute-start | bytes 6291464 | tf_op jit(solution)/shard_map/ppermute | solution.py:805
  360.2 16.3 %collective-permute-start.17 = (bf16[512,3072]{1,0:T(8,128)(2,1)}, bf16[512,3072]{1,0:T(8,128)(2,1)S(1)}, u32[]{:S(2)}, u32[]{:S(2)}) collective-permute-start(bf16[512,3072]{1,0:T(8,128)(2,1)} %get-tuple-element.204), channel_id=1, source_target_pairs={{0,1},{1,0},{2,3},{3,2},{4,5},{5,4},{6,7},{7,6},{8,9},{9,8},{10,11... | collective-permute-start | bytes 9437192 | tf_op jit(solution)/shard_map/ppermute | solution.py:805
  371.9 4.6 collective-permute-start.18
  371.9 39.1 %collective-permute-start.23 = (bf16[128,4096]{1,0:T(8,128)(2,1)}, bf16[128,4096]{1,0:T(8,128)(2,1)}, u32[]{:S(2)}, u32[]{:S(2)}) collective-permute-start(bf16[128,4096]{1,0:T(8,128)(2,1)} %bitcast.208), channel_id=1, source_target_pairs={{0,4},{2,6},{4,0},{6,2},{8,12},{10,14},{12,8},{14,10},{16,20},{18,... | collective-permute-start | bytes 3145736 | tf_op jit(solution)/shard_map/ppermute | solution.py:805
  376.4 34.7 %collective-permute-start.24 = (bf16[128,4096]{1,0:T(8,128)(2,1)}, bf16[128,4096]{1,0:T(8,128)(2,1)}, u32[]{:S(2)}, u32[]{:S(2)}) collective-permute-start(bf16[128,4096]{1,0:T(8,128)(2,1)} %bitcast.207), channel_id=1, source_target_pairs={{0,8},{2,10},{4,12},{6,14},{8,0},{10,2},{12,4},{14,6},{16,24},{18,... | collective-permute-start | bytes 3145736 | tf_op jit(solution)/shard_map/ppermute | solution.py:805
  385.7 34.9 %collective-permute-start.20 = (bf16[256,1536]{1,0:T(8,128)(2,1)}, bf16[256,1536]{1,0:T(8,128)(2,1)S(1)}, u32[]{:S(2)}, u32[]{:S(2)}) collective-permute-start(bf16[256,1536]{1,0:T(8,128)(2,1)} %bitcast.210), channel_id=1, source_target_pairs={{0,2},{2,0},{4,6},{6,4},{8,10},{10,8},{12,14},{14,12},{16,18},{18,... | collective-permute-start | bytes 2359304 | tf_op jit(solution)/shard_map/ppermute | solution.py:805
  392.5 29.9 %collective-permute-start.21 = (bf16[256,1536]{1,0:T(8,128)(2,1)}, bf16[256,1536]{1,0:T(8,128)(2,1)S(1)}, u32[]{:S(2)}, u32[]{:S(2)}) collective-permute-start(bf16[256,1536]{1,0:T(8,128)(2,1)} %bitcast.209), channel_id=1, source_target_pairs={{0,4},{2,6},{4,0},{6,2},{8,12},{10,14},{12,8},{14,10},{16,20},{18,... | collective-permute-start | bytes 2359304 | tf_op jit(solution)/shard_map/ppermute | solution.py:805
  392.5 28.1 %collective-permute-start.22 = (bf16[256,1024]{1,0:T(8,128)(2,1)}, bf16[256,1024]{1,0:T(8,128)(2,1)S(1)}, u32[]{:S(2)}, u32[]{:S(2)}) collective-permute-start(bf16[256,1024]{1,0:T(8,128)(2,1)} %bitcast.213), channel_id=1, source_target_pairs={{0,8},{2,10},{4,12},{6,14},{8,0},{10,2},{12,4},{14,6},{16,24},{18,... | collective-permute-start | bytes 1572872 | tf_op jit(solution)/shard_map/ppermute | solution.py:805
  411.0 18.7 %collective-permute-start.19 = (bf16[1,8,2048]{2,1,0:T(8,128)(2,1)S(1)}, bf16[1,8,2048]{2,1,0:T(8,128)(2,1)S(1)}, u32[]{:S(2)}, u32[]{:S(2)}) collective-permute-start(bf16[1,8,2048]{2,1,0:T(8,128)(2,1)S(1)} %fusion.14.refs_0_), channel_id=1, source_target_pairs={{0,16},{2,18},{4,20},{6,22},{8,24},{10,26},{12,28},{14,30},{16,0},... | collective-permute-start | bytes 98312 | tf_op jit(solution)/shard_map/ppermute | solution.py:805
  431.8 4.5 collective-permute-start.25
  438.4 7.1 %collective-permute-start.26 = (bf16[4,8,2048]{2,1,0:T(8,128)(2,1)}, bf16[4,8,2048]{2,1,0:T(8,128)(2,1)S(1)}, u32[]{:S(2)}, u32[]{:S(2)}) collective-permute-start(bf16[4,8,2048]{2,1,0:T(8,128)(2,1)} %get-tuple-element.228.refs_0_), channel_id=1, source_target_pairs={{0,4},{2,6},{4,0},{6,2},{8,12},{10,14},{12,8},{14,10},{16,20},{18,... | collective-permute-start | bytes 393224 | tf_op jit(solution)/shard_map/ppermute | solution.py:805
  440.2 22.4 %collective-permute-start.31 = (bf16[64,4096]{1,0:T(8,128)(2,1)}, bf16[64,4096]{1,0:T(8,128)(2,1)S(1)}, u32[]{:S(2)}, u32[]{:S(2)}) collective-permute-start(bf16[64,4096]{1,0:T(8,128)(2,1)} %bitcast.212), channel_id=1, source_target_pairs={{0,8},{2,10},{4,12},{6,14},{8,0},{10,2},{12,4},{14,6},{16,24},{18,... | collective-permute-start | bytes 1572872 | tf_op jit(solution)/shard_map/ppermute | solution.py:805
  440.3 22.4 %collective-permute-start.32 = (bf16[64,4096]{1,0:T(8,128)(2,1)}, bf16[64,4096]{1,0:T(8,128)(2,1)S(1)}, u32[]{:S(2)}, u32[]{:S(2)}) collective-permute-start(bf16[64,4096]{1,0:T(8,128)(2,1)} %bitcast.211), channel_id=1, source_target_pairs={{0,2},{2,0},{4,6},{6,4},{8,10},{10,8},{12,14},{14,12},{16,18},{18,... | collective-permute-start | bytes 1572872 | tf_op jit(solution)/shard_map/ppermute | solution.py:805
  444.9 15.7 %collective-permute-start.30 = (bf16[128,1024]{1,0:T(8,128)(2,1)}, bf16[128,1024]{1,0:T(8,128)(2,1)S(1)}, u32[]{:S(2)}, u32[]{:S(2)}) collective-permute-start(bf16[128,1024]{1,0:T(8,128)(2,1)} %bitcast.218), channel_id=1, source_target_pairs={{0,2},{2,0},{4,6},{6,4},{8,10},{10,8},{12,14},{14,12},{16,18},{18,... | collective-permute-start | bytes 786440 | tf_op jit(solution)/shard_map/ppermute | solution.py:805
  444.9 17.7 %collective-permute-start.28 = (bf16[128,1536]{1,0:T(8,128)(2,1)}, bf16[128,1536]{1,0:T(8,128)(2,1)S(1)}, u32[]{:S(2)}, u32[]{:S(2)}) collective-permute-start(bf16[128,1536]{1,0:T(8,128)(2,1)} %bitcast.215), channel_id=1, source_target_pairs={{0,4},{2,6},{4,0},{6,2},{8,12},{10,14},{12,8},{14,10},{16,20},{18,... | collective-permute-start | bytes 1179656 | tf_op jit(solution)/shard_map/ppermute | solution.py:805
  445.5 17.1 %collective-permute-start.29 = (bf16[128,1536]{1,0:T(8,128)(2,1)}, bf16[128,1536]{1,0:T(8,128)(2,1)S(1)}, u32[]{:S(2)}, u32[]{:S(2)}) collective-permute-start(bf16[128,1536]{1,0:T(8,128)(2,1)} %bitcast.214), channel_id=1, source_target_pairs={{0,8},{2,10},{4,12},{6,14},{8,0},{10,2},{12,4},{14,6},{16,24},{18,... | collective-permute-start | bytes 1179656 | tf_op jit(solution)/shard_map/ppermute | solution.py:805
  460.6 7.6 %collective-permute-start.27 = (bf16[8,8,2048]{2,1,0:T(8,128)(2,1)}, bf16[8,8,2048]{2,1,0:T(8,128)(2,1)S(1)}, u32[]{:S(2)}, u32[]{:S(2)}) collective-permute-start(bf16[8,8,2048]{2,1,0:T(8,128)(2,1)} %get-tuple-element.230.refs_0_), channel_id=1, source_target_pairs={{0,2},{2,0},{4,6},{6,4},{8,10},{10,8},{12,14},{14,12},{16,18},{18,... | collective-permute-start | bytes 786440 | tf_op jit(solution)/shard_map/ppermute | solution.py:805
  470.7 3.6 collective-permute-start.33
  470.7 16.0 %collective-permute-start.34 = (bf16[64,1536]{1,0:T(8,128)(2,1)}, bf16[64,1536]{1,0:T(8,128)(2,1)S(1)}, u32[]{:S(2)}, u32[]{:S(2)}) collective-permute-start(bf16[64,1536]{1,0:T(8,128)(2,1)} %bitcast.220), channel_id=1, source_target_pairs={{0,8},{2,10},{4,12},{6,14},{8,0},{10,2},{12,4},{14,6},{16,24},{18,... | collective-permute-start | bytes 589832 | tf_op jit(solution)/shard_map/ppermute | solution.py:805
  472.7 14.0 %collective-permute-start.35 = (bf16[64,1536]{1,0:T(8,128)(2,1)}, bf16[64,1536]{1,0:T(8,128)(2,1)S(1)}, u32[]{:S(2)}, u32[]{:S(2)}) collective-permute-start(bf16[64,1536]{1,0:T(8,128)(2,1)} %bitcast.219), channel_id=1, source_target_pairs={{0,2},{2,0},{4,6},{6,4},{8,10},{10,8},{12,14},{14,12},{16,18},{18,... | collective-permute-start | bytes 589832 | tf_op jit(solution)/shard_map/ppermute | solution.py:805
  473.8 13.0 %collective-permute-start.36 = (bf16[64,1024]{1,0:T(8,128)(2,1)}, bf16[64,1024]{1,0:T(8,128)(2,1)S(1)}, u32[]{:S(2)}, u32[]{:S(2)}) collective-permute-start(bf16[64,1024]{1,0:T(8,128)(2,1)} %bitcast.221), channel_id=1, source_target_pairs={{0,4},{2,6},{4,0},{6,2},{8,12},{10,14},{12,8},{14,10},{16,20},{18,... | collective-permute-start | bytes 393224 | tf_op jit(solution)/shard_map/ppermute | solution.py:805
  474.3 26.8 %collective-permute-start.40 = (bf16[32,4096]{1,0:T(8,128)(2,1)}, bf16[32,4096]{1,0:T(8,128)(2,1)S(1)}, u32[]{:S(2)}, u32[]{:S(2)}) collective-permute-start(bf16[32,4096]{1,0:T(8,128)(2,1)} %bitcast.217), channel_id=1, source_target_pairs={{0,16},{2,18},{4,20},{6,22},{8,24},{10,26},{12,28},{14,30},{16,0},... | collective-permute-start | bytes 786440 | tf_op jit(solution)/shard_map/ppermute | solution.py:805
  474.4 34.2 %collective-permute-start.41 = (bf16[32,4096]{1,0:T(8,128)(2,1)}, bf16[32,4096]{1,0:T(8,128)(2,1)S(1)}, u32[]{:S(2)}, u32[]{:S(2)}) collective-permute-start(bf16[32,4096]{1,0:T(8,128)(2,1)} %bitcast.216), channel_id=1, source_target_pairs={{0,16},{2,18},{4,20},{6,22},{8,24},{10,26},{12,28},{14,30},{16,0},... | collective-permute-start | bytes 786440 | tf_op jit(solution)/shard_map/ppermute | solution.py:805
  490.3 23.8 %collective-permute-start.37 = (bf16[32,1536]{1,0:T(8,128)(2,1)}, bf16[32,1536]{1,0:T(8,128)(2,1)S(1)}, u32[]{:S(2)}, u32[]{:S(2)}) collective-permute-start(bf16[32,1536]{1,0:T(8,128)(2,1)} %bitcast.224), channel_id=1, source_target_pairs={{0,16},{2,18},{4,20},{6,22},{8,24},{10,26},{12,28},{14,30},{16,0},... | collective-permute-start | bytes 294920 | tf_op jit(solution)/shard_map/ppermute | solution.py:805
  490.4 23.7 %collective-permute-start.38 = (bf16[32,1536]{1,0:T(8,128)(2,1)}, bf16[32,1536]{1,0:T(8,128)(2,1)S(1)}, u32[]{:S(2)}, u32[]{:S(2)}) collective-permute-start(bf16[32,1536]{1,0:T(8,128)(2,1)} %bitcast.223), channel_id=1, source_target_pairs={{0,16},{2,18},{4,20},{6,22},{8,24},{10,26},{12,28},{14,30},{16,0},... | collective-permute-start | bytes 294920 | tf_op jit(solution)/shard_map/ppermute | solution.py:805
  493.2 20.8 %collective-permute-start.39 = (bf16[32,1024]{1,0:T(8,128)(2,1)}, bf16[32,1024]{1,0:T(8,128)(2,1)S(1)}, u32[]{:S(2)}, u32[]{:S(2)}) collective-permute-start(bf16[32,1024]{1,0:T(8,128)(2,1)} %bitcast.225), channel_id=1, source_target_pairs={{0,16},{2,18},{4,20},{6,22},{8,24},{10,26},{12,28},{14,30},{16,0},... | collective-permute-start | bytes 196616 | tf_op jit(solution)/shard_map/ppermute | solution.py:805
  494.7 23.8 %all-to-all-start.2 = ((f32[32,1,1280]{2,1,0:T(1,128)}), f32[32,1,1280]{2,1,0:T(1,128)S(1)}, u32[]{:S(2)}, u32[]{:S(2)}) async-start(f32[32,1,1280]{2,1,0:T(1,128)} %reshape.669), calls=%async_computation.2 | async-start | bytes 327680 | tf_op jit(solution)/shard_map/all_to_all | solution.py:1204
  (50 other events, 231.3 us)
Sparse Core Ops, SparseCore 0:
  74.6 122.2 all-gather.2
  365.2 64.6 all-gather.4
